TPU v7x, 512 devices: a whole 4x8x8 slice. The times are simulated.
512 devices in a mesh: outer: 32 (over x, y), inner: 16 (over z, core).
Axes of the slice: x: 4, y: 8, z: 8, core: 2. Of those that a mesh axis runs over, the one named last changes fastest.
Arguments:
- offsets: float32 [3, 262144], P(None, ('outer', 'inner')), may hold values from -0.45 to 0.45
- charges: float32 [64, 262144], P(None, ('outer', 'inner')), may hold values from -1.2 to 1.2
- counts: int32 [8192], P(('outer', 'inner')), may hold values from 1 to 32, as said below
- near: int32 [8192, 12], P(('outer', 'inner')), may hold values from 0 to 8191, as said below
- far: int32 [8192, 12], P(('outer', 'inner')), may hold values from 0 to 8191, as said below
- upward: float32 [165, 165], replicated
- downward: float32 [165, 165], replicated
Outputs:
- potential: float32 [64, 262144], P(None, ('outer', 'inner'))
Inputs may be any that keep to these rules, and one draw needn't show every extreme that they name: `counts`: some leaf of every device's range has exactly 32 occupied slots. near[g] holds 12 different leaves, g itself among them; far[g] holds 12 different leaves, none of them in near[g]. All of them belong to the device that owns g or to a device whose inner index differs by one, in the same outer group. `far`: as for near.
All inputs are finite; a program needn't handle non-finite values.
Results may differ from a plain program's by a relative error of at most 0.0003.
Values sent between devices are 32-bit elements; how exact they have to be, the bound alone decides.
No kernel may reach another device: no remote copies, remote signals or barrier semaphores. Data moves between devices by JAX's collectives and lax.ppermute only.
A program may use at most 64 MiB of HBM per device.

v0:
```python
import jax
import jax.numpy as jnp
from jax import lax
from jax.sharding import PartitionSpec as P

SOFTEN = 0.25
GOLDEN = 2.399963229728653
UPPER_LEVEL = lax.Precision.HIGHEST


def with_halo(cells, sides, width):
    for axis, dim in sides:
        count = lax.axis_size(axis)
        ends = count - 1
        head = lax.slice_in_dim(cells, 0, width, axis=dim)
        tail = lax.slice_in_dim(cells, cells.shape[dim] - width, cells.shape[dim], axis=dim)
        cells = jnp.concatenate(
            [
                lax.ppermute(tail, axis, [(i, (i + 1) % count) for i in range(ends)]),
                cells,
                lax.ppermute(head, axis, [((i + 1) % count, i) for i in range(ends)]),
            ],
            axis=dim,
        )
    return cells


def sphere(count):
    steps_t = jnp.arange(count, dtype=jnp.float32)
    height = 1.0 - (2.0 * steps_t + 1.0) / count
    radial = jnp.sqrt(jnp.maximum(1.0 - height * height, 0.0))
    return jnp.stack(
        [radial * jnp.cos(steps_t * GOLDEN), radial * jnp.sin(steps_t * GOLDEN), height]
    )


def morton(leaf_ids):
    coords = []
    for axis_id in range(3):
        bitsum = jnp.zeros_like(leaf_ids)
        for bit_level in range(10):
            bitsum = bitsum | (leaf_ids >> 3 * bit_level + axis_id & 1) << bit_level
        coords.append(bitsum)
    return jnp.stack(coords).astype(jnp.float32) + 0.5


def green(target, source):
    first = target[0] - source[0]
    second = target[1] - source[1]
    third = target[2] - source[2]
    return lax.rsqrt(first * first + second * second + third * third + SOFTEN)


def leaf_expand(centres, points, charges, upward, dirs):
    checks = centres[:, :, None] + 1.8 * dirs[:, None, :]
    kern = green(checks[:, :, :, None], points[:, :, None, :])
    check_pot = jnp.einsum("ltp,rlp->lrt", kern, charges, precision=UPPER_LEVEL)
    return (
        18.0 / upward.shape[0] * jnp.einsum("lrt,ti->lri", check_pot, upward, precision=UPPER_LEVEL)
    )


def device_expand(centres, equiv, dev_centre, upward, dirs):
    checks = dev_centre[:, None] + 6.0 * dirs
    sources = centres[:, :, None] + 0.9 * dirs[:, None, :]
    kern = green(checks[:, None, :, None], sources[:, :, None, :])
    check_pot = jnp.einsum("lti,lri->rt", kern, equiv, precision=UPPER_LEVEL)
    return 60.0 / upward.shape[0] * jnp.dot(check_pot, upward, precision=UPPER_LEVEL)


def shards(offsets, charges, counts, near, far, upward, downward):
    inner_n = lax.axis_size("inner")
    outer_n = lax.axis_size("outer")
    inner_id = lax.axis_index("inner")
    outer_id = lax.axis_index("outer")
    terms = upward.shape[0]
    rhs_n = charges.shape[0]
    leaf_n = counts.shape[0]
    slots = offsets.shape[1] // leaf_n
    device = outer_id * inner_n + inner_id
    dirs = sphere(terms)
    own_ids = device * leaf_n + jnp.arange(leaf_n, dtype=jnp.int32)
    centres = morton(own_ids)
    filled = (jnp.arange(slots, dtype=jnp.int32)[None, :] < counts[:, None]).astype(jnp.float32)
    masked = charges.reshape(rhs_n, leaf_n, slots) * filled[None]
    points = centres[:, :, None] + offsets.reshape(3, leaf_n, slots)
    all_ids = jnp.arange(outer_n * inner_n * leaf_n, dtype=jnp.int32)
    group_table = morton(all_ids).reshape(3, outer_n, inner_n * leaf_n).mean(axis=2)
    peer_ids = outer_id * (inner_n * leaf_n) + jnp.arange(inner_n * leaf_n, dtype=jnp.int32)
    device_table = morton(peer_ids).reshape(3, inner_n, leaf_n).mean(axis=2)
    dev_centre = lax.dynamic_index_in_dim(device_table, inner_id, 1, keepdims=False)
    cluster_centre = lax.dynamic_index_in_dim(group_table, outer_id, 1, keepdims=False)
    own_equiv = leaf_expand(centres, points, masked, upward, dirs)
    dev_equiv = device_expand(centres, own_equiv, dev_centre, upward, dirs)
    kern_up = green(
        cluster_centre[:, None, None] + 20.0 * dirs[:, :, None],
        dev_centre[:, None, None] + 3.0 * dirs[:, None, :],
    )
    partial_value = jnp.einsum("ti,ri->rt", kern_up, dev_equiv, precision=UPPER_LEVEL)
    group_targets = cluster_centre[:, None] + 10.0 * dirs
    cluster_check_surface = lax.psum(partial_value, "inner")
    group_equiv = 200.0 / terms * jnp.dot(cluster_check_surface, upward, precision=UPPER_LEVEL)
    piece = lax.all_gather(group_equiv[None], "outer", axis=0, tiled=True)

    def one_group(turn, accum):
        source_centre = lax.dynamic_index_in_dim(group_table, turn, 1, keepdims=False)
        kern = green(
            group_targets[:, :, None], source_centre[:, None, None] + 20.0 * dirs[:, None, :]
        )
        weight = (jnp.abs(turn - outer_id) >= 2).astype(jnp.float32)
        expansion = lax.dynamic_index_in_dim(piece, turn, 0, keepdims=False)
        return accum + weight * jnp.einsum("ti,ri->rt", kern, expansion, precision=UPPER_LEVEL)

    group_down = lax.fori_loop(0, piece.shape[0], one_group, jnp.zeros((rhs_n, terms), jnp.float32))
    group_local = 200.0 / terms * jnp.dot(group_down, downward, precision=UPPER_LEVEL)
    dev_targets = dev_centre[:, None] + 3.0 * dirs
    device_piece = lax.all_gather(dev_equiv[None], "inner", axis=0, tiled=True)

    def one_device(turn, accum):
        source_centre = lax.dynamic_index_in_dim(device_table, turn, 1, keepdims=False)
        kern = green(dev_targets[:, :, None], source_centre[:, None, None] + 3.0 * dirs[:, None, :])
        weight = (jnp.abs(turn - inner_id) >= 2).astype(jnp.float32)
        expansion = lax.dynamic_index_in_dim(device_piece, turn, 0, keepdims=False)
        return accum + weight * jnp.einsum("ti,ri->rt", kern, expansion, precision=UPPER_LEVEL)

    device_down = lax.fori_loop(
        0, device_piece.shape[0], one_device, jnp.zeros((rhs_n, terms), jnp.float32)
    )
    kern_group = green(
        dev_targets[:, :, None], cluster_centre[:, None, None] + 20.0 * dirs[:, None, :]
    )
    device_down = device_down + jnp.einsum(
        "ti,ri->rt", kern_group, group_local, precision=UPPER_LEVEL
    )
    device_local = 60.0 / terms * jnp.dot(device_down, downward, precision=UPPER_LEVEL)
    stacked = jnp.concatenate([offsets, masked.reshape(rhs_n, leaf_n * slots)], axis=0)
    beside_all = with_halo(stacked, (("inner", 1),), leaf_n * slots)
    base = (device - 1) * leaf_n
    window_centres = morton(base + jnp.arange(3 * leaf_n, dtype=jnp.int32))
    window_points = window_centres[:, :, None] + beside_all[:3].reshape(3, 3 * leaf_n, slots)
    window_charges = beside_all[3:].reshape(rhs_n, 3 * leaf_n, slots)
    window_equiv = with_halo(own_equiv, (("inner", 0),), leaf_n)
    leaf_target_points = centres[:, :, None] + 0.9 * dirs[:, None, :]
    far_local = far - base

    def far_add(turn, total):
        column = lax.dynamic_index_in_dim(far_local, turn, 1, keepdims=False)
        source_equiv = jnp.take(window_equiv, column, axis=0)
        source_centre = jnp.take(window_centres, column, axis=1)
        kern = green(
            leaf_target_points[:, :, :, None],
            source_centre[:, :, None, None] + 1.8 * dirs[:, None, None, :],
        )
        return total + jnp.einsum("lti,lri->lrt", kern, source_equiv, precision=UPPER_LEVEL)

    leaf_down = lax.fori_loop(
        0, far.shape[1], far_add, jnp.zeros((leaf_n, rhs_n, terms), jnp.float32)
    )
    kern_dev = green(
        leaf_target_points[:, :, :, None],
        dev_centre[:, None, None, None] + 6.0 * dirs[:, None, None, :],
    )
    leaf_down = leaf_down + jnp.einsum("lti,ri->lrt", kern_dev, device_local, precision=UPPER_LEVEL)
    leaf_local = (
        18.0 / terms * jnp.einsum("lrt,ti->lri", leaf_down, downward, precision=UPPER_LEVEL)
    )
    kern_eval = green(
        points[:, :, :, None], centres[:, :, None, None] + 1.8 * dirs[:, None, None, :]
    )
    far_part = jnp.einsum("lpi,lri->rlp", kern_eval, leaf_local, precision=UPPER_LEVEL)
    near_local = near - base
    near_points = jnp.take(window_points, near_local, axis=1)
    near_charges = jnp.take(window_charges, near_local, axis=1)
    kern_near = green(points[:, :, None, :, None], near_points[:, :, :, None, :])
    near_part = jnp.einsum("lkps,rlks->rlp", kern_near, near_charges, precision=UPPER_LEVEL)
    return (far_part + near_part).reshape(rhs_n, leaf_n * slots)


def solution(mesh):
    in_specs = (
        P(None, ("outer", "inner")),
        P(None, ("outer", "inner")),
        P(("outer", "inner")),
        P(("outer", "inner"), None),
        P(("outer", "inner"), None),
        P(),
        P(),
    )
    out_specs = P(None, ("outer", "inner"))
    return jax.shard_map(shards, mesh=mesh, in_specs=in_specs, out_specs=out_specs, check_vma=False)
```

profile of v0, /device:TPU:1, one launch (start us, length us, event | category | flops | bytes accessed | tf_op | source)
XLA Modules:
  0.0 291.7 jit_solution(17521019367233028346)
XLA Ops:
  10.3 1.4 fusion.151
  12.7 5.4 %collective-permute-start = (f32[16,64,165]{2,1,0:T(8,128)S(1)}, f32[16,64,165]{2,1,0:T(8,128)}, u32[]{:S(2)}, u32[]{:S(2)}) collective-permute-start(f32[16,64,165]{2,1,0:T(8,128)S(1)} %convolution_multiply_fusion.3), channel_id=1, source_target_pairs={{0,1},{1,2},{2,3},{3,4},{4,5},{5,6},{6,7},{7,8},{8,9},{9,10},{10,1... | collective-permute-start | bytes 2027528 | tf_op jit(solution)/shard_map/ppermute | solution.py:19
  18.1 5.6 %collective-permute-start.1 = (f32[16,64,165]{2,1,0:T(8,128)S(1)}, f32[16,64,165]{2,1,0:T(8,128)}, u32[]{:S(2)}, u32[]{:S(2)}) collective-permute-start(f32[16,64,165]{2,1,0:T(8,128)S(1)} %convolution_multiply_fusion.3), channel_id=1, source_target_pairs={{1,0},{2,1},{3,2},{4,3},{5,4},{6,5},{7,6},{8,7},{9,8},{10,9},{11,1... | collective-permute-start | bytes 2027528 | tf_op jit(solution)/shard_map/ppermute | solution.py:21
  24.1 1.9 collective-permute-start.2
  26.1 2.4 collective-permute-start.3
  28.8 3.4 %fusion.136 = f32[64,165]{1,0:T(8,128)S(1)} fusion(f32[16,64,165]{2,1,0:T(8,128)S(1)} %convolution_multiply_fusion.3, f32[16,165]{1,0:T(8,128)S(1)} %get-tuple-element.595, f32[165]{0:T(256)S(1)} %bitcast.235, f32[16,165]{1,0:T(8,128)S(1)} %get-tuple-element.596, f32[165]{0:T(256)S(1)} %bitcast.236, f32[16,165]{1,0:T(8,128)S(1)} %get-tuple-element.594, ...), kind=kOutput, calls=%fused_computation.154 | convolution fusion | flops 338461184 | bytes 751740 | tf_op jit(solution)/shard_map/lti,lri->rt/dot_general | solution.py:67
  33.0 46.8 %psum.7 = f32[64,165]{1,0:T(8,128)S(1)} all-reduce(f32[64,165]{1,0:T(8,128)S(1)} %fusion.190), channel_id=1, replica_groups=mesh['outer'=32,'inner'=16] {'inner'}, use_global_device_ids=true, to_apply=%region_6.7 | all-reduce | flops 10560 | bytes 84480 | tf_op jit(solution)/shard_map/psum | solution.py:101
  80.7 21.2 %all-gather = f32[1024,165]{1,0:T(8,128)S(1)} all-gather(f32[64,165]{1,0:T(8,128)S(1)} %convolution_multiply_fusion.7), channel_id=2, replica_groups=mesh['outer'=32,'inner'=16] {'inner'}, dimensions={0}, use_global_device_ids=true | all-gather | bytes 718080 | tf_op jit(solution)/shard_map/all_gather | solution.py:117
  102.8 8.8 %while.43 = (s32[]{:T(128)}, f32[64,165]{1,0:T(8,128)S(1)}, s32[]{:T(128)}, f32[16,64,165]{2,1,0:T(8,128)S(1)}, f32[3,165]{1,0:T(4,128)S(1)}, /*index=5*/f32[3,1...) while((s32[]{:T(128)}, f32[64,165]{1,0:T(8,128)S(1)}, s32[]{:T(128)}, ...), condition=%wide.region_4.5_spmd.clone, body=%wide.region_3.4_spmd.clone.sunk | while | flops 21186500 | bytes 191529 | solution.py:126
  116.2 2.6 gather_fusion.2
  118.9 7.1 %fusion.131 = f32[16,64,32]{1,2,0:T(8,128)S(1)} fusion(f32[16,12,32]{2,1,0:T(8,128)S(1)} %get-tuple-element.589, f32[16,32]{1,0:T(8,128)S(1)} %get-tuple-element.601, f32[16,12,32]{2,1,0:T(8,128)S(1)} %get-tuple-element.590, f32[16,32]{1,0:T(8,128)S(1)} %get-tuple-element.602, f32[16,12,32]{2,1,0:T(8,128)S(1)} %get-tuple-element.588, ...), kind=kOutput, calls=%fused_computation.153 | convolution fusion | flops 153157632 | bytes 1784000 | tf_op jit(solution)/shard_map/lkps,rlks->rlp/dot_general | solution.py:175
  126.1 3.6 %pad_maximum_fusion = f32[48,64,165]{2,1,0:T(8,128)} fusion(f32[16,64,165]{2,1,0:T(8,128)} %collective-permute-done.1, f32[16,64,165]{2,1,0:T(8,128)S(1)} %convolution_multiply_fusion.3, f32[16,64,165]{2,1,0:T(8,128)} %collective-permute-done), kind=kLoop, calls=%fused_computation.90 | loop fusion | flops 1013760 | bytes 4055040 | tf_op jit(solution)/shard_map/concatenate | solution.py:17
  129.6 103.0 %while.42 = (s32[]{:T(128)}, f32[16,64,165]{2,1,0:T(8,128)S(1)}, s32[16,12]{0,1:T(8,128)}, f32[48,64,165]{2,1,0:T(8,128)}, f32[3,16,165]{2,1,0:T(8,128)S(1)}, /*...) while((s32[]{:T(128)}, f32[16,64,165]{2,1,0:T(8,128)S(1)}, ...), condition=%wide.region_1.0_spmd.clone, body=%wide.region_0.0_spmd.clone.sunk | while | flops 338977664 | bytes 3612815 | solution.py:156
  131.1 2.5 gather_fusion.1
  133.7 4.5 %fusion.288 = f32[16,64,165]{2,1,0:T(8,128)S(1)} fusion(f32[16,165]{1,0:T(8,128)S(1)} %get-tuple-element.783, f32[16,165]{1,0:T(8,128)S(1)} %get-tuple-element.784, f32[16,165]{1,0:T(8,128)S(1)} %get-tuple-element.785, f32[16,165]{1,0:T(8,128)S(1)} %get-tuple-element.786, f32[16,165]{1,0:T(8,128)S(1)} %get-tuple-element.787, ...), kind=kOutput, calls=%fused_computation.22.clone.1 | convolution fusion | flops 338968064 | bytes 2090897 | tf_op jit(solution)/shard_map/while/body/eval_jaxpr/lti,lri->lrt/dot_general | solution.py:154
  139.7 2.5 gather_fusion.1
  142.2 4.5 %fusion.288 = f32[16,64,165]{2,1,0:T(8,128)S(1)} fusion(f32[16,165]{1,0:T(8,128)S(1)} %get-tuple-element.783, f32[16,165]{1,0:T(8,128)S(1)} %get-tuple-element.784, f32[16,165]{1,0:T(8,128)S(1)} %get-tuple-element.785, f32[16,165]{1,0:T(8,128)S(1)} %get-tuple-element.786, f32[16,165]{1,0:T(8,128)S(1)} %get-tuple-element.787, ...), kind=kOutput, calls=%fused_computation.22.clone.1 | convolution fusion | flops 338968064 | bytes 2090897 | tf_op jit(solution)/shard_map/while/body/eval_jaxpr/lti,lri->lrt/dot_general | solution.py:154
  148.3 2.5 gather_fusion.1
  150.8 4.5 %fusion.288 = f32[16,64,165]{2,1,0:T(8,128)S(1)} fusion(f32[16,165]{1,0:T(8,128)S(1)} %get-tuple-element.783, f32[16,165]{1,0:T(8,128)S(1)} %get-tuple-element.784, f32[16,165]{1,0:T(8,128)S(1)} %get-tuple-element.785, f32[16,165]{1,0:T(8,128)S(1)} %get-tuple-element.786, f32[16,165]{1,0:T(8,128)S(1)} %get-tuple-element.787, ...), kind=kOutput, calls=%fused_computation.22.clone.1 | convolution fusion | flops 338968064 | bytes 2090897 | tf_op jit(solution)/shard_map/while/body/eval_jaxpr/lti,lri->lrt/dot_general | solution.py:154
  156.9 2.5 gather_fusion.1
  159.4 4.5 %fusion.288 = f32[16,64,165]{2,1,0:T(8,128)S(1)} fusion(f32[16,165]{1,0:T(8,128)S(1)} %get-tuple-element.783, f32[16,165]{1,0:T(8,128)S(1)} %get-tuple-element.784, f32[16,165]{1,0:T(8,128)S(1)} %get-tuple-element.785, f32[16,165]{1,0:T(8,128)S(1)} %get-tuple-element.786, f32[16,165]{1,0:T(8,128)S(1)} %get-tuple-element.787, ...), kind=kOutput, calls=%fused_computation.22.clone.1 | convolution fusion | flops 338968064 | bytes 2090897 | tf_op jit(solution)/shard_map/while/body/eval_jaxpr/lti,lri->lrt/dot_general | solution.py:154
  165.5 2.5 gather_fusion.1
  168.0 4.5 %fusion.288 = f32[16,64,165]{2,1,0:T(8,128)S(1)} fusion(f32[16,165]{1,0:T(8,128)S(1)} %get-tuple-element.783, f32[16,165]{1,0:T(8,128)S(1)} %get-tuple-element.784, f32[16,165]{1,0:T(8,128)S(1)} %get-tuple-element.785, f32[16,165]{1,0:T(8,128)S(1)} %get-tuple-element.786, f32[16,165]{1,0:T(8,128)S(1)} %get-tuple-element.787, ...), kind=kOutput, calls=%fused_computation.22.clone.1 | convolution fusion | flops 338968064 | bytes 2090897 | tf_op jit(solution)/shard_map/while/body/eval_jaxpr/lti,lri->lrt/dot_general | solution.py:154
  174.1 2.5 gather_fusion.1
  176.6 4.5 %fusion.288 = f32[16,64,165]{2,1,0:T(8,128)S(1)} fusion(f32[16,165]{1,0:T(8,128)S(1)} %get-tuple-element.783, f32[16,165]{1,0:T(8,128)S(1)} %get-tuple-element.784, f32[16,165]{1,0:T(8,128)S(1)} %get-tuple-element.785, f32[16,165]{1,0:T(8,128)S(1)} %get-tuple-element.786, f32[16,165]{1,0:T(8,128)S(1)} %get-tuple-element.787, ...), kind=kOutput, calls=%fused_computation.22.clone.1 | convolution fusion | flops 338968064 | bytes 2090897 | tf_op jit(solution)/shard_map/while/body/eval_jaxpr/lti,lri->lrt/dot_general | solution.py:154
  182.6 2.5 gather_fusion.1
  185.2 4.5 %fusion.288 = f32[16,64,165]{2,1,0:T(8,128)S(1)} fusion(f32[16,165]{1,0:T(8,128)S(1)} %get-tuple-element.783, f32[16,165]{1,0:T(8,128)S(1)} %get-tuple-element.784, f32[16,165]{1,0:T(8,128)S(1)} %get-tuple-element.785, f32[16,165]{1,0:T(8,128)S(1)} %get-tuple-element.786, f32[16,165]{1,0:T(8,128)S(1)} %get-tuple-element.787, ...), kind=kOutput, calls=%fused_computation.22.clone.1 | convolution fusion | flops 338968064 | bytes 2090897 | tf_op jit(solution)/shard_map/while/body/eval_jaxpr/lti,lri->lrt/dot_general | solution.py:154
  191.2 2.5 gather_fusion.1
  193.7 4.5 %fusion.288 = f32[16,64,165]{2,1,0:T(8,128)S(1)} fusion(f32[16,165]{1,0:T(8,128)S(1)} %get-tuple-element.783, f32[16,165]{1,0:T(8,128)S(1)} %get-tuple-element.784, f32[16,165]{1,0:T(8,128)S(1)} %get-tuple-element.785, f32[16,165]{1,0:T(8,128)S(1)} %get-tuple-element.786, f32[16,165]{1,0:T(8,128)S(1)} %get-tuple-element.787, ...), kind=kOutput, calls=%fused_computation.22.clone.1 | convolution fusion | flops 338968064 | bytes 2090897 | tf_op jit(solution)/shard_map/while/body/eval_jaxpr/lti,lri->lrt/dot_general | solution.py:154
  199.8 2.5 gather_fusion.1
  202.3 4.5 %fusion.288 = f32[16,64,165]{2,1,0:T(8,128)S(1)} fusion(f32[16,165]{1,0:T(8,128)S(1)} %get-tuple-element.783, f32[16,165]{1,0:T(8,128)S(1)} %get-tuple-element.784, f32[16,165]{1,0:T(8,128)S(1)} %get-tuple-element.785, f32[16,165]{1,0:T(8,128)S(1)} %get-tuple-element.786, f32[16,165]{1,0:T(8,128)S(1)} %get-tuple-element.787, ...), kind=kOutput, calls=%fused_computation.22.clone.1 | convolution fusion | flops 338968064 | bytes 2090897 | tf_op jit(solution)/shard_map/while/body/eval_jaxpr/lti,lri->lrt/dot_general | solution.py:154
  208.4 2.5 gather_fusion.1
  210.9 4.5 %fusion.288 = f32[16,64,165]{2,1,0:T(8,128)S(1)} fusion(f32[16,165]{1,0:T(8,128)S(1)} %get-tuple-element.783, f32[16,165]{1,0:T(8,128)S(1)} %get-tuple-element.784, f32[16,165]{1,0:T(8,128)S(1)} %get-tuple-element.785, f32[16,165]{1,0:T(8,128)S(1)} %get-tuple-element.786, f32[16,165]{1,0:T(8,128)S(1)} %get-tuple-element.787, ...), kind=kOutput, calls=%fused_computation.22.clone.1 | convolution fusion | flops 338968064 | bytes 2090897 | tf_op jit(solution)/shard_map/while/body/eval_jaxpr/lti,lri->lrt/dot_general | solution.py:154
  217.0 2.5 gather_fusion.1
  219.5 4.5 %fusion.288 = f32[16,64,165]{2,1,0:T(8,128)S(1)} fusion(f32[16,165]{1,0:T(8,128)S(1)} %get-tuple-element.783, f32[16,165]{1,0:T(8,128)S(1)} %get-tuple-element.784, f32[16,165]{1,0:T(8,128)S(1)} %get-tuple-element.785, f32[16,165]{1,0:T(8,128)S(1)} %get-tuple-element.786, f32[16,165]{1,0:T(8,128)S(1)} %get-tuple-element.787, ...), kind=kOutput, calls=%fused_computation.22.clone.1 | convolution fusion | flops 338968064 | bytes 2090897 | tf_op jit(solution)/shard_map/while/body/eval_jaxpr/lti,lri->lrt/dot_general | solution.py:154
  225.5 2.5 gather_fusion.1
  228.1 4.5 %fusion.288 = f32[16,64,165]{2,1,0:T(8,128)S(1)} fusion(f32[16,165]{1,0:T(8,128)S(1)} %get-tuple-element.783, f32[16,165]{1,0:T(8,128)S(1)} %get-tuple-element.784, f32[16,165]{1,0:T(8,128)S(1)} %get-tuple-element.785, f32[16,165]{1,0:T(8,128)S(1)} %get-tuple-element.786, f32[16,165]{1,0:T(8,128)S(1)} %get-tuple-element.787, ...), kind=kOutput, calls=%fused_computation.22.clone.1 | convolution fusion | flops 338968064 | bytes 2090897 | tf_op jit(solution)/shard_map/while/body/eval_jaxpr/lti,lri->lrt/dot_general | solution.py:154
  232.7 44.5 %while.44 = (s32[]{:T(128)}, f32[64,165]{1,0:T(8,128)S(1)}, s32[]{:T(128)}, f32[32,64,165]{2,1,0:T(8,128)}, f32[3,165]{1,0:T(4,128)S(1)}, /*index=5*/f32[3,32]{0...) while((s32[]{:T(128)}, f32[64,165]{1,0:T(8,128)S(1)}, s32[]{:T(128)}, ...), condition=%wide.region_8.9_spmd.clone, body=%wide.region_7.8_spmd.clone.sunk | while | flops 21186500 | bytes 166557 | solution.py:114
  241.2 1.3 fusion.298
  242.6 1.3 fusion.298
  244.0 1.3 fusion.298
  245.4 1.3 fusion.298
  246.7 1.3 fusion.298
  248.1 1.3 fusion.298
  249.5 1.3 fusion.298
  250.9 1.3 fusion.298
  252.3 1.3 fusion.298
  253.7 1.3 fusion.298
  255.1 1.3 fusion.298
  256.5 1.3 fusion.298
  257.9 1.3 fusion.298
  259.3 1.3 fusion.298
  260.6 1.3 fusion.298
  262.0 1.3 fusion.298
  263.4 1.3 fusion.298
  264.8 1.3 fusion.298
  266.2 1.3 fusion.298
  267.6 1.3 fusion.298
  269.0 1.3 fusion.298
  270.4 1.3 fusion.298
  271.8 1.3 fusion.298
  273.1 1.3 fusion.298
  274.5 1.3 fusion.298
  278.2 3.7 %fusion.128 = f32[16,64,165]{2,1,0:T(8,128)S(1)} fusion(f32[64,165,1]{1,0,2:T(8,128)S(1)} %fusion.139, f32[165]{0:T(256)S(1)} %bitcast.226, f32[16,165]{1,0:T(8,128)S(1)} %get-tuple-element.595, f32[165]{0:T(256)S(1)} %bitcast.227, f32[16,165]{1,0:T(8,128)S(1)} %get-tuple-element.596, f32[165]{0:T(256)S(1)} %bitcast.225, f32[16,165]{1,0:T(8,128)S(1)} %get-tuple-element.594), kind=kOutput, calls=%fused_computation.151 | convolution fusion | flops 338461184 | bytes 751740 | tf_op jit(solution)/shard_map/lti,ri->lrt/dot_general | solution.py:163
  (454 shorter events, 54.5 us)
Async XLA Ops:
  6.5 5.2 %copy-start = (f32[165,165]{1,0:T(8,128)S(1)}, f32[165,165]{1,0:T(8,128)}, u32[]{:S(2)}) copy-start(f32[165,165]{1,0:T(8,128)} %param.18) | copy-start | bytes 326704
  6.5 17.6 %copy-start.4 = (f32[3,512]{1,0:T(4,128)S(1)}, f32[3,512]{1,0:T(4,128)}, u32[]{:S(2)}) copy-start(f32[3,512]{1,0:T(4,128)} %param.13) | copy-start | bytes 18436
  6.5 17.5 %copy-start.3 = (f32[64,512]{1,0:T(8,128)S(1)}, f32[64,512]{1,0:T(8,128)}, u32[]{:S(2)}) copy-start(f32[64,512]{1,0:T(8,128)} %param.14) | copy-start | bytes 393220
  6.5 17.3 %copy-start.9 = (s32[16]{0:T(128)S(1)}, s32[16]{0:T(128)}, u32[]{:S(2)}) copy-start(s32[16]{0:T(128)} %param.15) | copy-start | bytes 196
  6.5 226.2 %all-gather.4.cloned.1.call-start = ((), (), s32[]{:S(2)}) async-start(), calls=%async_computation | async-start | bytes 2162688 | tf_op jit(solution)/shard_map/all_gather | solution.py:103
  12.7 113.3 %collective-permute-start = (f32[16,64,165]{2,1,0:T(8,128)S(1)}, f32[16,64,165]{2,1,0:T(8,128)}, u32[]{:S(2)}, u32[]{:S(2)}) collective-permute-start(f32[16,64,165]{2,1,0:T(8,128)S(1)} %convolution_multiply_fusion.3), channel_id=1, source_target_pairs={{0,1},{1,2},{2,3},{3,4},{4,5},{5,6},{6,7},{7,8},{8,9},{9,10},{10,1... | collective-permute-start | bytes 2027528 | tf_op jit(solution)/shard_map/ppermute | solution.py:19
  18.1 107.9 %collective-permute-start.1 = (f32[16,64,165]{2,1,0:T(8,128)S(1)}, f32[16,64,165]{2,1,0:T(8,128)}, u32[]{:S(2)}, u32[]{:S(2)}) collective-permute-start(f32[16,64,165]{2,1,0:T(8,128)S(1)} %convolution_multiply_fusion.3), channel_id=1, source_target_pairs={{1,0},{2,1},{3,2},{4,3},{5,4},{6,5},{7,6},{8,7},{9,8},{10,9},{11,1... | collective-permute-start | bytes 2027528 | tf_op jit(solution)/shard_map/ppermute | solution.py:21
  24.1 90.5 %collective-permute-start.2 = (f32[67,512]{1,0:T(8,128)S(1)}, f32[67,512]{1,0:T(8,128)S(1)}, u32[]{:S(2)}, u32[]{:S(2)}) collective-permute-start(f32[67,512]{1,0:T(8,128)S(1)} %pad_maximum_fusion.2), channel_id=1, source_target_pairs={{0,1},{1,2},{2,3},{3,4},{4,5},{5,6},{6,7},{7,8},{8,9},{9,10},{10,1... | collective-permute-start | bytes 411656 | tf_op jit(solution)/shard_map/ppermute | solution.py:19
  26.1 88.6 %collective-permute-start.3 = (f32[67,512]{1,0:T(8,128)S(1)}, f32[67,512]{1,0:T(8,128)S(1)}, u32[]{:S(2)}, u32[]{:S(2)}) collective-permute-start(f32[67,512]{1,0:T(8,128)S(1)} %pad_maximum_fusion.2), channel_id=1, source_target_pairs={{1,0},{2,1},{3,2},{4,3},{5,4},{6,5},{7,6},{8,7},{9,8},{10,9},{11,1... | collective-permute-start | bytes 411656 | tf_op jit(solution)/shard_map/ppermute | solution.py:21
  32.5 80.3 %copy-start.7 = (s32[16,12]{1,0:T(8,128)S(1)}, s32[16,12]{1,0:T(8,128)}, u32[]{:S(2)}) copy-start(s32[16,12]{1,0:T(8,128)} %param.17) | copy-start | bytes 2308
  32.6 80.9 %copy-start.8 = (s32[16,12]{1,0:T(8,128)S(1)}, s32[16,12]{1,0:T(8,128)}, u32[]{:S(2)}) copy-start(s32[16,12]{1,0:T(8,128)} %param.16) | copy-start | bytes 2308
  126.0 3.6 %copy-start.2 = (f32[16,64,165]{2,1,0:T(8,128)S(1)}, f32[16,64,165]{2,1,0:T(8,128)}, u32[]{:S(2)}) copy-start(f32[16,64,165]{2,1,0:T(8,128)} %custom-call) | copy-start | bytes 2027524
  232.6 44.6 %copy-start.1 = (f32[165,165]{1,0:T(8,128)S(1)}, f32[165,165]{1,0:T(8,128)}, u32[]{:S(2)}) copy-start(f32[165,165]{1,0:T(8,128)} %param.19) | copy-start | bytes 326704
  232.6 44.8 %copy-start.10 = (f32[1,165]{1,0:T(1,128)S(1)}, f32[1,165]{1,0:T(1,128)}, u32[]{:S(2)}) copy-start(f32[1,165]{1,0:T(1,128)} %get-tuple-element.603) | copy-start | bytes 1984
  232.6 44.8 %copy-start.11 = (f32[1,165]{1,0:T(1,128)S(1)}, f32[1,165]{1,0:T(1,128)}, u32[]{:S(2)}) copy-start(f32[1,165]{1,0:T(1,128)} %get-tuple-element.604) | copy-start | bytes 1984
  232.6 44.8 %copy-start.12 = (f32[1,165]{1,0:T(1,128)S(1)}, f32[1,165]{1,0:T(1,128)}, u32[]{:S(2)}) copy-start(f32[1,165]{1,0:T(1,128)} %get-tuple-element.605) | copy-start | bytes 1984
  232.7 44.8 %copy-start.13 = (f32[1,1,165]{2,1,0:T(1,128)S(1)}, f32[1,1,165]{2,1,0:T(1,128)}, u32[]{:S(2)}) copy-start(f32[1,1,165]{2,1,0:T(1,128)} %get-tuple-element.614) | copy-start | bytes 1984
  232.7 44.8 %copy-start.14 = (f32[1,1,165]{2,1,0:T(1,128)S(1)}, f32[1,1,165]{2,1,0:T(1,128)}, u32[]{:S(2)}) copy-start(f32[1,1,165]{2,1,0:T(1,128)} %get-tuple-element.615) | copy-start | bytes 1984
  232.7 44.8 %copy-start.15 = (f32[1,1,165]{2,1,0:T(1,128)S(1)}, f32[1,1,165]{2,1,0:T(1,128)}, u32[]{:S(2)}) copy-start(f32[1,1,165]{2,1,0:T(1,128)} %get-tuple-element.616) | copy-start | bytes 1984
  232.7 45.5 %copy-start.16 = (f32[1,1,1,165]{3,2,1,0:T(1,128)S(1)}, f32[1,1,1,165]{3,2,1,0:T(1,128)}, u32[]{:S(2)}) copy-start(f32[1,1,1,165]{3,2,1,0:T(1,128)} %get-tuple-element.611) | copy-start | bytes 1984
  232.7 45.5 %copy-start.17 = (f32[1,1,1,165]{3,2,1,0:T(1,128)S(1)}, f32[1,1,1,165]{3,2,1,0:T(1,128)}, u32[]{:S(2)}) copy-start(f32[1,1,1,165]{3,2,1,0:T(1,128)} %get-tuple-element.612) | copy-start | bytes 1984
  232.7 45.5 %copy-start.18 = (f32[1,1,1,165]{3,2,1,0:T(1,128)S(1)}, f32[1,1,1,165]{3,2,1,0:T(1,128)}, u32[]{:S(2)}) copy-start(f32[1,1,1,165]{3,2,1,0:T(1,128)} %get-tuple-element.613) | copy-start | bytes 1984
  281.8 1.0 copy-start.5
  281.8 1.0 copy-start.6
Sparse Core Ops, SparseCore 0:
  80.8 82.0 all-gather.3
where the time goes:
time: 294 us; the launch traced here: 292 us
  matrix products  123 us (42%)
  blocking collectives  68 us (23%)
  local copies, waits for them, and re-layouts  49.2 us (17%)
  other arithmetic  20.3 us (7%)
  starting transfers between devices  15.4 us (5%)
  between operations  14 us (5%)
    dot_general x12, matrix products, far_add(): jnp.einsum('lti,lri->lrt', kern, source_equiv, precision=UPPER_LEVEL)  54.3 us
    psum x1, blocking collectives, shards(): cluster_check_surface = lax.psum(partial_value, 'inner')  46.8 us
    dot_general x32, matrix products, one_group(): jnp.einsum('ti,ri->rt', kern, expansion, precision=UPPER_LEVEL)  40.5 us
    gather x12, local copies, waits for them, and re-layouts, far_add(): source_equiv = jnp.take(window_equiv, column, axis=0)  30.1 us
    all_gather x1, blocking collectives, shards(): device_piece = lax.all_gather(dev_equiv[None], 'inner', axis=0, tiled=True)  21.2 us
    reduce_and x12, other arithmetic, far_add(): source_equiv = jnp.take(window_equiv, column, axis=0)  8.2 us
    ppermute x2, starting transfers between devices, with_halo(): lax.ppermute(head, axis, [((i + 1) % count, i) for i in range(ends)])  8.06 us
    ppermute x2, starting transfers between devices, with_halo(): lax.ppermute(tail, axis, [(i, (i + 1) % count) for i in range(ends)])  7.31 us
  transfers between devices with their start and end apart: 5, of which 0 were waited for; matrix products, arithmetic and copies ran while one was open for 46% of the time, Pallas kernels for 0%

commit v1 on v0

v1 whole, which is shorter than its diff:
```python
import functools

import jax
import jax.numpy as jnp
import numpy as np
from jax import lax
from jax.experimental import pallas as pl
from jax.experimental.pallas import tpu as pltpu
from jax.sharding import PartitionSpec as P

SOFTEN = 0.25
GOLDEN = 2.399963229728653
RHS = 64
TERMS = 165
SUB = 176
LANE = 256
LEAVES = 16
SLOTS = 32
POINTS = LEAVES * SLOTS
ROWS = 72
INNER = 16
OUTER = 32
PART = RHS // INNER
BF = jnp.bfloat16
F32 = jnp.float32


def sphere_tables():
    steps = np.arange(TERMS, dtype=np.float32)
    height = (np.float32(1.0) - (np.float32(2.0) * steps + np.float32(1.0)) / np.float32(TERMS)).astype(np.float32)
    radial = np.sqrt(np.maximum(np.float32(1.0) - height * height, np.float32(0.0))).astype(np.float32)
    angle = (steps * np.float32(GOLDEN)).astype(np.float32)
    dirs = np.stack([radial * np.cos(angle), radial * np.sin(angle), height]).astype(np.float32)
    col = np.zeros((SUB, 128), np.float32)
    col[:TERMS, :3] = dirs.T
    row = np.zeros((8, LANE), np.float32)
    row[:3, :TERMS] = dirs
    return col, row


def split(x):
    high = x.astype(BF)
    return high, (x - high.astype(F32)).astype(BF)


def dot(a, b):
    return jnp.dot(a, b, preferred_element_type=F32)


def dot_nt(a, b):
    return lax.dot_general(a, b, (((1,), (1,)), ((), ())), preferred_element_type=F32)


def mm3(a, b, f=dot):
    return f(a[0], b[0]) + f(a[1], b[0]) + f(a[0], b[1])


def columns(col_ref):
    return [jnp.broadcast_to(col_ref[:, c : c + 1], (SUB, 128)) for c in range(3)]


def two(x):
    return jnp.concatenate([x, x], axis=1)


def surface_products(col_ref, row_ref):
    cols = [two(c) for c in columns(col_ref)]
    return (
        cols[0] * row_ref[0:1, :] + cols[1] * row_ref[1:2, :] + cols[2] * row_ref[2:3, :]
    )


def pair_kernel(base, col_ref, row_ref, shift, radius_t, radius_i):
    dx, dy, dz = shift
    cols = columns(col_ref)
    side = (-2.0 * radius_i * dx) * cols[0] + (-2.0 * radius_i * dy) * cols[1] + (-2.0 * radius_i * dz) * cols[2]
    along = (
        (2.0 * radius_t * dx) * row_ref[0:1, :]
        + (2.0 * radius_t * dy) * row_ref[1:2, :]
        + (2.0 * radius_t * dz) * row_ref[2:3, :]
        + (dx * dx + dy * dy + dz * dz)
    )
    return lax.rsqrt(base + two(side) + along)


def base_of(products, radius_t, radius_i):
    return products * (-2.0 * radius_t * radius_i) + (radius_t * radius_t + radius_i * radius_i + SOFTEN)


def bits(ids, low, axis, top=14):
    total = 0
    for level in range(5):
        place = 3 * level + axis
        if low <= place < top:
            total = total + (((ids >> place) & 1) << level)
    return total


def corner(leaf_id, low):
    return [bits(leaf_id, low, axis) for axis in range(3)]


def local_leaf(index):
    return ((index & 1) + ((index >> 3) & 1) * 2, (index >> 1) & 1, (index >> 2) & 1)


def peer_box(inner):
    return (((inner >> 2) & 1) * 4, (inner & 1) * 2 + ((inner >> 3) & 1) * 4, ((inner >> 1) & 1) * 2)


def leaf_kernel(offs, col_ref):
    total = SOFTEN
    for c in range(3):
        col = jnp.broadcast_to(col_ref[:, c : c + 1], (SUB, 128)) * 1.8
        diff = jnp.concatenate([col] * (POINTS // 128), axis=1) - offs[c : c + 1, :]
        total = total + diff * diff
    return lax.rsqrt(total)


def padded(map_ref, pad_ref, scale):
    pad_ref[...] = jnp.zeros_like(pad_ref)
    pad_ref[0:TERMS, 0:TERMS] = map_ref[...] * scale
    return split(pad_ref[...])


def leaf_equivalents(charges, kern, up):
    block = lax.broadcasted_iota(jnp.int32, (RHS, 256), 1) // SLOTS
    out = []
    for half in range(2):
        lanes = slice(half * 256, half * 256 + 256)
        own = charges[:, lanes]
        spread = split(jnp.concatenate([jnp.where(block == g, own, 0.0) for g in range(8)], axis=0))
        check = mm3(spread, (kern[0][:, lanes], kern[1][:, lanes]), dot_nt)
        out.append(mm3(split(check), up))
    return out


def pack(rows):
    low, high = rows[:, :128], rows[:, 128:]
    n = rows.shape[0]
    top = lax.broadcasted_iota(jnp.int32, (n, 128), 0) % 8 < 4
    first = jnp.where(top, low, pltpu.roll(high, 4, 0))
    second = jnp.where(top, pltpu.roll(low, n - 4, 0), high)
    tiles = []
    for m in range(n // 8):
        tiles += [first[8 * m : 8 * m + 8], second[8 * m : 8 * m + 8]]
    return jnp.concatenate(tiles, axis=0)


def unpack(tiles):
    n = tiles.shape[0] // 2
    first = jnp.concatenate([tiles[16 * m : 16 * m + 8] for m in range(n // 8)], axis=0)
    second = jnp.concatenate([tiles[16 * m + 8 : 16 * m + 16] for m in range(n // 8)], axis=0)
    top = lax.broadcasted_iota(jnp.int32, (n, 128), 0) % 8 < 4
    low = jnp.where(top, first, pltpu.roll(second, 4, 0))
    high = jnp.where(top, pltpu.roll(first, n - 4, 0), second)
    return jnp.concatenate([low, high], axis=1)


def tile_dot(tile, high, low, acc):
    a_high, a_low = split(tile)
    both = jnp.concatenate([a_high, a_low], axis=0)
    rest = SUB - 128
    front = dot(both, high[:128]) + dot(both, low[:128])
    back = dot(both[:, :rest], high[128:]) + dot(both[:, :rest], low[128:])
    return acc[0] + front, acc[1] + back


def tile_sum(acc):
    front = acc[0][:8] + acc[0][8:]
    back = acc[1][:8] + acc[1][8:]
    return front + pltpu.roll(back, 4, 0)


def head_kernel(
    off_hbm, q_hbm, counts_hbm, up_hbm, down_hbm, col_hbm, row_hbm,
    out_ref, halo_ref, up_ref, down_ref, col_ref, row_ref,
    off_ref, q_ref, counts_ref, pad_ref, sems,
):
    moves = [
        pltpu.make_async_copy(src, dst, sems.at[n])
        for n, (src, dst) in enumerate(
            (
                (q_hbm, q_ref),
                (off_hbm, off_ref),
                (counts_hbm, counts_ref),
                (up_hbm, up_ref),
                (col_hbm, col_ref),
                (row_hbm, row_ref),
                (down_hbm, down_ref),
            )
        )
    ]
    for move in moves:
        move.start()
    for move in moves[:-1]:
        move.wait()
    lane = lax.broadcasted_iota(jnp.int32, (8, POINTS), 1)
    limit = jnp.zeros((8, POINTS), jnp.int32)
    for g in range(LEAVES):
        limit = jnp.where(lane // SLOTS == g, counts_ref[g], limit)
    filled = (lane % SLOTS < limit)[0:1]
    charges = jnp.where(filled, q_ref[...], 0.0)
    halo_ref[0:RHS, :] = charges
    halo_ref[RHS:ROWS, :] = jnp.zeros((ROWS - RHS, POINTS), F32)
    halo_ref[RHS : RHS + 3, :] = off_ref[...]
    kern = split(leaf_kernel(off_ref[...], col_ref))
    up = padded(up_ref, pad_ref, 18.0 / TERMS)
    up = (up[0][:, :], up[1][:, :])
    halves = leaf_equivalents(charges, kern, up)
    base = base_of(surface_products(col_ref, row_ref), 6.0, 0.9)
    acc = jnp.zeros((RHS, LANE), F32)
    for half in range(2):
        equiv = split(halves[half])
        for g in range(8):
            x, y, z = local_leaf(half * 8 + g)
            k_high, k_low = split(pair_kernel(base, col_ref, row_ref, (1.5 - x, 0.5 - y, 0.5 - z), 6.0, 0.9))
            rows = slice(g * RHS, g * RHS + RHS)
            acc = acc + dot(equiv[0][rows, :SUB], k_high) + dot(equiv[1][rows, :SUB], k_high) + dot(
                equiv[0][rows, :SUB], k_low
            )
    up60 = padded(up_ref, pad_ref, 60.0 / TERMS)
    out_ref[...] = pack(mm3(split(acc[:, :SUB]), up60))
    moves[-1].wait()


def group_up_kernel(x_ref, up_ref, col_ref, row_ref, out_ref, pad_ref):
    base = base_of(surface_products(col_ref, row_ref), 20.0, 3.0)
    acc = (jnp.zeros((16, LANE), F32), jnp.zeros((16, LANE), F32))
    for e in range(INNER):
        x, y, z = peer_box(e)
        kern = split(pair_kernel(base, col_ref, row_ref, (4.0 - x - 2.0, 4.0 - y - 1.0, 2.0 - z - 1.0), 20.0, 3.0))
        acc = tile_dot(x_ref[8 * e : 8 * e + 8, :], kern[0], kern[1], acc)
    check = tile_sum(acc)
    both = jnp.concatenate([check, check], axis=0)
    equiv = mm3(split(both[:, :SUB]), padded(up_ref, pad_ref, 200.0 / TERMS))[:8]
    top = lax.broadcasted_iota(jnp.int32, (8, 128), 0) < 4
    tile = jnp.where(top, equiv[:, :128], pltpu.roll(equiv[:, 128:], 4, 0))
    for p in range(OUTER):
        out_ref[8 * p : 8 * p + 8, :] = tile


def peers_kernel(x_ref, col_ref, row_ref, out_ref):
    equiv = unpack(x_ref[...])
    both = jnp.concatenate(split(equiv), axis=1)
    base = base_of(surface_products(col_ref, row_ref), 3.0, 3.0)
    row = lax.broadcasted_iota(jnp.int32, (RHS, RHS), 0)
    lane = lax.broadcasted_iota(jnp.int32, (RHS, RHS), 1)
    dest = row // PART
    px = (dest >> 2) & 1
    py = (dest & 1) + ((dest >> 3) & 1) * 2
    pz = (dest >> 1) & 1

    def one(dx, dy, dz, acc):
        sx, sy, sz = px - dx, py - dy, pz - dz
        inside = (sx >= 0) & (sx < 2) & (sy >= 0) & (sy < 4) & (sz >= 0) & (sz < 2)
        source = (sy & 1) + (sz & 1) * 2 + (sx & 1) * 4 + ((sy >> 1) & 1) * 8
        apart = jnp.abs(source - dest) >= 2
        pick = (inside & apart & (lane == source * PART + row % PART)).astype(F32).astype(BF)
        moved = dot(pick, both).astype(BF)
        shift = (dx.astype(F32) * 4.0, dy * 2.0, dz.astype(F32) * 2.0)
        kern = split(pair_kernel(base, col_ref, row_ref, shift, 3.0, 3.0))
        a = (moved[:, :SUB], moved[:, LANE : LANE + SUB])
        return acc + mm3(a, kern)

    def step(turn, acc):
        for dy in range(-3, 4):
            acc = one(turn // 3 - 1, dy, turn % 3 - 1, acc)
        return acc

    out_ref[...] = lax.fori_loop(0, 9, step, jnp.zeros((RHS, LANE), F32))


def group_maps_kernel(flow_ref, col_ref, row_ref, out_ref, down_ref):
    outer = lax.axis_index("outer")
    own = corner(outer * 256, 8)
    cols = [two(c) * 20.0 for c in columns(col_ref)]

    def step(turn, carry):
        for n in range(4):
            p = turn * 4 + n
            other = corner(p * 256, 8)
            total = SOFTEN
            for c in range(3):
                shift = (own[c] - other[c]).astype(F32)
                diff = (shift + 10.0 * row_ref[c : c + 1, :]) - cols[c]
                total = total + diff * diff
            high, low = split(lax.rsqrt(total))
            out_ref[p, 0, :, :] = high
            out_ref[p, 1, :, :] = low
        return carry

    lax.fori_loop(0, OUTER // 4, step, 0)
    base = base_of(surface_products(col_ref, row_ref), 3.0, 20.0)
    for d in range(INNER):
        x, y, z = peer_box(d)
        high, low = split(pair_kernel(base, col_ref, row_ref, (x + 2.0 - 4.0, y + 1.0 - 4.0, z + 1.0 - 2.0), 3.0, 20.0))
        down_ref[d, 0, :, :] = high
        down_ref[d, 1, :, :] = low


def local_kernel(x_ref, peers_ref, maps_ref, to_dev_ref, down_ref, out_ref, pad_ref):
    outer = lax.axis_index("outer")
    acc = (jnp.zeros((16, LANE), F32), jnp.zeros((16, LANE), F32))
    for p in range(OUTER):
        weight = (jnp.abs(p - outer) >= 2).astype(F32)
        acc = tile_dot(x_ref[8 * p : 8 * p + 8, :] * weight, maps_ref[p, 0], maps_ref[p, 1], acc)
    check = tile_sum(acc)
    both = jnp.concatenate([check, check], axis=0)
    group = mm3(split(both[:, :SUB]), padded(down_ref, pad_ref, 200.0 / TERMS))[:8]
    pieces = jnp.concatenate(split(group[:, :SUB]), axis=0)
    top = lax.broadcasted_iota(jnp.int32, (8, LANE), 0) < 4
    found = []
    for d in range(INNER):
        part = dot(pieces, to_dev_ref[d, 0]) + dot(pieces, to_dev_ref[d, 1])
        found.append(part[:8] + part[8:])
    merged = [jnp.where(top, found[2 * m], pltpu.roll(found[2 * m + 1], 4, 0)) for m in range(INNER // 2)]
    total = jnp.concatenate(merged, axis=0) + peers_ref[...]
    out_ref[...] = pack(mm3(split(total[:, :SUB]), padded(down_ref, pad_ref, 60.0 / TERMS)))


def operator_kernel(own_ref, down_ref, col_ref, row_ref, w_ref, m_ref, halo_ref, pad_ref):
    halo_ref[...] = own_ref[...]
    off = own_ref[RHS : RHS + 3, :]
    down = padded(down_ref, pad_ref, 18.0 / TERMS)
    down = (down[0][:, :SUB], down[1][:, :SUB])
    weights = split(mm3(down, split(leaf_kernel(off, col_ref))))
    w_ref[0, :, :] = weights[0]
    w_ref[1, :, :] = weights[1]
    base = base_of(surface_products(col_ref, row_ref), 0.9, 6.0)
    block = lax.broadcasted_iota(jnp.int32, (SUB, 256), 1) // SLOTS
    for half in range(2):
        lanes = slice(half * 256, half * 256 + 256)
        own = (weights[0][:, lanes], weights[1][:, lanes])
        acc = jnp.zeros((SUB, 256), F32)
        for g in range(8):
            x, y, z = local_leaf(half * 8 + g)
            kern = pair_kernel(base, col_ref, row_ref, (x - 1.5, y - 0.5, z - 0.5), 0.9, 6.0)
            acc = jnp.where(block == g, mm3(split(kern[:, :SUB]), own), acc)
        m_high, m_low = split(acc)
        m_ref[0, :, lanes] = m_high
        m_ref[1, :, lanes] = m_low


def near_kernel(near_ref, left_ref, own_ref, right_ref, out_ref, mask_ref, high_ref, low_ref):
    offs = jnp.concatenate([own_ref[RHS:ROWS, :], jnp.zeros((120, POINTS), F32)], axis=0).T
    inner = lax.axis_index("inner")
    device = lax.axis_index("outer") * INNER + inner
    base = (device - 1) * LEAVES
    total = 3 * POINTS
    lane = lax.broadcasted_iota(jnp.int32, (LEAVES, total), 1) // SLOTS
    found = jnp.zeros((LEAVES, total), F32)
    near = near_ref[...] - base
    for k in range(12):
        found = jnp.where(lane == near[:, k : k + 1], 1.0, found)
    mask_ref[...] = found
    leaf = lax.broadcasted_iota(jnp.int32, (1, POINTS), 1) // SLOTS
    within = local_leaf(leaf)
    own_box = corner(device * LEAVES, 4)
    sources = []
    for c in range(3):
        lanes = []
        for side, ref in ((-1, left_ref), (0, own_ref), (1, right_ref)):
            box = corner((device + side) * LEAVES, 4)[c] - own_box[c]
            lanes.append(ref[RHS + c : RHS + c + 1, :] + (box + within[c]).astype(F32))
        sources.append(jnp.concatenate(lanes, axis=1))
    for g in range(LEAVES):
        rows = slice(g * SLOTS, g * SLOTS + SLOTS)
        place = local_leaf(g)
        dist = SOFTEN
        for c in range(3):
            diff = (offs[rows, c : c + 1] + float(place[c])) - sources[c]
            dist = dist + diff * diff
        k_high, k_low = split(lax.rsqrt(dist) * mask_ref[g : g + 1, :])
        high_ref[rows, :] = k_high
        low_ref[rows, :] = k_low
    charges = jnp.concatenate([r[0:RHS, :] for r in (left_ref, own_ref, right_ref)], axis=1)
    q_high, q_low = split(charges)
    both = jnp.concatenate([q_high, q_low], axis=0)
    res = dot_nt(high_ref[...], both)
    res = res + jnp.concatenate([dot_nt(low_ref[...], q_high), jnp.zeros((POINTS, RHS), F32)], axis=1)
    flipped = res.T
    out_ref[...] = flipped[:RHS] + flipped[RHS:]


def far_kernel(far_ref, left_ref, own_ref, right_ref, w_ref, up_ref, near_ref, col_ref, row_ref, out_ref, pad_ref, base_ref, e_ref, dl_ref, side_ref):
    inner = lax.axis_index("inner")
    device = lax.axis_index("outer") * INNER + inner
    up = padded(up_ref, pad_ref, 18.0 / TERMS)
    for side, ref in enumerate((left_ref, own_ref, right_ref)):
        kern = split(leaf_kernel(ref[RHS : RHS + 3, :], col_ref))
        halves = leaf_equivalents(ref[0:RHS, :], kern, up)
        for half in range(2):
            e_high, e_low = split(halves[half])
            for g in range(8):
                start = ((side * 2 + half) * 8 + g) * 2 * RHS
                e_ref[start : start + RHS, :] = e_high[g * RHS : g * RHS + RHS]
                e_ref[start + RHS : start + 2 * RHS, :] = e_low[g * RHS : g * RHS + RHS]
    products = base_of(surface_products(col_ref, row_ref), 0.9, 1.8)
    first = (device - 1) * LEAVES
    boxes = [corner((device + side) * LEAVES, 4) for side in (-1, 0, 1)]
    boxes = [[(box[c] - boxes[1][c]).astype(F32) for c in range(3)] for box in boxes]
    cols = [c * 3.6 for c in columns(col_ref)]
    for window in range(3 * LEAVES):
        place = local_leaf(window % LEAVES)
        at = [boxes[window // LEAVES][c] + float(place[c]) for c in range(3)]
        side_ref[window * SUB : (window + 1) * SUB, :] = at[0] * cols[0] + at[1] * cols[1] + at[2] * cols[2]

    def one_leaf(g, carry):
        own = [p.astype(F32) for p in local_leaf(g)]
        own_side = side_ref[pl.ds(pl.multiple_of((g + LEAVES) * SUB, SUB), SUB), :]
        base_ref[...] = products - two(own_side)
        acc = jnp.zeros((RHS, LANE), F32)
        for k in range(12):
            window = far_ref[g, k] - first
            side = window >> 4
            place = local_leaf(window & 15)
            shift = []
            for c in range(3):
                box = jnp.where(side == 0, boxes[0][c], jnp.where(side == 1, 0.0, boxes[2][c]))
                shift.append(own[c] - box - place[c].astype(F32))
            along = (
                (1.8 * shift[0]) * row_ref[0:1, :]
                + (1.8 * shift[1]) * row_ref[1:2, :]
                + (1.8 * shift[2]) * row_ref[2:3, :]
                + (shift[0] * shift[0] + shift[1] * shift[1] + shift[2] * shift[2])
            )
            source_side = side_ref[pl.ds(pl.multiple_of(window * SUB, SUB), SUB), :]
            k_high, k_low = split(lax.rsqrt(base_ref[...] + two(source_side) + along))
            start = pl.multiple_of(window * (2 * RHS), 2 * RHS)
            equiv = e_ref[pl.ds(start, 2 * RHS), :][:, :SUB]
            wide = dot(equiv, k_high)
            acc = acc + wide[:RHS] + wide[RHS:] + dot(equiv[:RHS], k_low)
        high, low = split(acc)
        start = pl.multiple_of(g * RHS, RHS)
        dl_ref[0, pl.ds(start, RHS), :] = high
        dl_ref[1, pl.ds(start, RHS), :] = low
        return carry

    lax.fori_loop(0, LEAVES, one_leaf, 0)
    block = lax.broadcasted_iota(jnp.int32, (RHS, 256), 1) // SLOTS
    for half in range(2):
        lanes = slice(half * 256, half * 256 + 256)
        rows = slice(half * 8 * RHS, (half + 1) * 8 * RHS)
        local = (dl_ref[0, rows, :][:, :SUB], dl_ref[1, rows, :][:, :SUB])
        res = mm3(local, (w_ref[0, :, lanes], w_ref[1, :, lanes]))
        acc = near_ref[:, lanes]
        for g in range(8):
            acc = acc + jnp.where(block == g, res[g * RHS : (g + 1) * RHS], 0.0)
        out_ref[:, lanes] = acc


def tail_kernel(x_ref, base_ref, m_ref, out_ref):
    local = split(unpack(x_ref[...])[:, :SUB])
    out_ref[...] = base_ref[...] + mm3(local, (m_ref[0], m_ref[1]))


VM = pl.BlockSpec(memory_space=pltpu.VMEM)
SM = pl.BlockSpec(memory_space=pltpu.SMEM)


def call(kernel, name, outs, specs, scratch, cost, *args, vmem=32):
    return pl.pallas_call(
        kernel,
        name=name,
        out_shape=outs,
        in_specs=specs,
        out_specs=jax.tree.map(lambda _: VM, outs),
        scratch_shapes=scratch,
        compiler_params=pltpu.CompilerParams(vmem_limit_bytes=vmem * 1024 * 1024),
        cost_estimate=pl.CostEstimate(flops=cost, bytes_accessed=500000, transcendentals=0),
    )(*args)


def tie(value, *others):
    return lax.optimization_barrier((value,) + others)[0]


def shards(offsets, charges, counts, near, far, upward, downward):
    col_np, row_np = sphere_tables()
    col, row = jnp.asarray(col_np), jnp.asarray(row_np)
    pad = pltpu.VMEM((SUB, LANE), F32)
    sds = jax.ShapeDtypeStruct
    flow = sds((2 * RHS, 128), F32)
    us = 400_000_000

    hbm = pl.BlockSpec(memory_space=pltpu.HBM)
    square = sds((TERMS, TERMS), F32)
    dev_equiv, own, upward, downward, col, row = call(
        head_kernel, "leaf_and_device_equiv",
        (flow, sds((ROWS, POINTS), F32), square, square, sds((SUB, 128), F32), sds((8, LANE), F32)), [hbm] * 7,
        [
            pltpu.VMEM((3, POINTS), F32),
            pltpu.VMEM((RHS, POINTS), F32),
            pltpu.SMEM((LEAVES,), jnp.int32),
            pad,
            pltpu.SemaphoreType.DMA((7,)),
        ],
        3 * us, *(pltpu.with_memory_space_constraint(a, pltpu.HBM) for a in (offsets, charges, counts, upward, downward, col, row)),
    )
    peers_equiv = lax.all_to_all(dev_equiv, "inner", 0, 0, tiled=True)
    weights, evaluate, halo = call(
        operator_kernel, "evaluation_maps",
        (sds((2, SUB, POINTS), BF), sds((2, SUB, POINTS), BF), sds((ROWS, POINTS), F32)), [VM, VM, VM, VM], [pad], 5 * us,
        own, downward, col, row,
    )
    ends = INNER - 1
    left = lax.ppermute(halo, "inner", [(i, i + 1) for i in range(ends)])
    right = lax.ppermute(halo, "inner", [(i + 1, i) for i in range(ends)])
    group_maps, to_devices = call(
        group_maps_kernel, "group_maps",
        (sds((OUTER, 2, SUB, LANE), BF), sds((INNER, 2, SUB, LANE), BF)), [VM, VM, VM], [], 5 * us,
        dev_equiv, col, row,
    )
    peers_equiv = tie(peers_equiv, weights, evaluate, group_maps, to_devices)
    group_equiv = call(
        group_up_kernel, "group_equiv", sds((8 * OUTER, 128), F32), [VM, VM, VM, VM], [pad], 2 * us,
        peers_equiv, upward, col, row,
    )
    groups = lax.all_to_all(group_equiv, "outer", 0, 0, tiled=True)
    peers_part = call(
        peers_kernel, "device_to_device", sds((RHS, LANE), F32), [VM, VM, VM], [], 8 * us, peers_equiv, col, row,
    )
    near_part = call(
        near_kernel, "near_field", sds((RHS, POINTS), F32), [VM, VM, VM, VM],
        [pltpu.VMEM((LEAVES, 3 * POINTS), F32), pltpu.VMEM((POINTS, 3 * POINTS), BF), pltpu.VMEM((POINTS, 3 * POINTS), BF)], 4 * us,
        near, left, own, right,
    )
    groups = tie(groups, near_part, peers_part)
    local = call(
        local_kernel, "group_and_device_local", flow, [VM, VM, VM, VM, VM], [pad], 3 * us,
        groups, peers_part, group_maps, to_devices, downward,
    )
    dev_local = lax.all_to_all(local, "inner", 0, 0, tiled=True)
    base = call(
        far_kernel, "far_field", sds((RHS, POINTS), F32), [SM, VM, VM, VM, VM, VM, VM, VM, VM],
        [
            pad,
            pad,
            pltpu.VMEM((3 * LEAVES * 2 * RHS, LANE), BF),
            pltpu.VMEM((2, LEAVES * RHS, LANE), BF),
            pltpu.VMEM((3 * LEAVES * SUB, 128), F32),
        ],
        12 * us, far, left, own, right, weights, upward, near_part, col, row,
    )
    return call(tail_kernel, "potential", sds((RHS, POINTS), F32), [VM, VM, VM], [], us, dev_local, base, evaluate)


def solution(mesh):
    both = ("outer", "inner")
    in_specs = (P(None, both), P(None, both), P(both), P(both, None), P(both, None), P(), P())
    return jax.shard_map(shards, mesh=mesh, in_specs=in_specs, out_specs=P(None, both), check_vma=False)
```

time: 294 us -> 96.8 us (0.33)
  matrix products: 123 us -> 0 us
  blocking collectives: 68 us -> 0 us
  Pallas kernels: 0 us -> 48.5 us
  local copies, waits for them, and re-layouts: 49.2 us -> 13.3 us
  other arithmetic: 20.3 us -> 0 us
  starting transfers between devices: 15.4 us -> 34.2 us
  between operations: 14 us -> 0.2 us
    dot_general x73 -> x0, matrix products: 123 us -> none  [the longest x12 54.3 us: far_add(): jnp.einsum('lti,lri->lrt', kern, source_equiv, precision=UPPER_LEVEL)]
    pallas_call x0 -> x9, Pallas kernels: none -> 48.5 us  [call(): pl.pallas_call(kernel, name=name, out_shape=outs, in_specs=specs, out_spe...]
    psum x1 -> x0, blocking collectives: 46.8 us -> none  [shards(): cluster_check_surface = lax.psum(partial_value, 'inner')]
    gather x26 -> x0, local copies, waits for them, and re-layouts: 40.3 us -> none  [the longest x12 30.1 us: far_add(): source_equiv = jnp.take(window_equiv, column, axis=0)]
    all_to_all x0 -> x3, starting transfers between devices: none -> 23.5 us  [the longest x1 9.86 us: shards(): groups = lax.all_to_all(group_equiv, 'outer', 0, 0, tiled=True)]
    all_gather x1 -> x0, blocking collectives: 21.2 us -> none  [shards(): device_piece = lax.all_gather(dev_equiv[None], 'inner', axis=0, tiled=True)]
    unnamed x44 -> x38, local copies, waits for them, and re-layouts: 1.53 us -> 13.3 us
    reduce_and x12 -> x0, other arithmetic: 8.2 us -> none  [far_add(): source_equiv = jnp.take(window_equiv, column, axis=0)]
  transfers between devices with their start and end apart: 5 -> 5, of which waited for: 0 -> 0; matrix products, arithmetic and copies ran while one was open for 46% -> 0% of each run, Pallas kernels for 0% -> 39%
where the time goes in v1:
time: 96.8 us; the launch traced here: 96.1 us
  Pallas kernels  48.5 us (50%)
  starting transfers between devices  34.2 us (35%)
  local copies, waits for them, and re-layouts  13.3 us (14%)
    pallas_call x9, Pallas kernels, call(): pl.pallas_call(kernel, name=name, out_shape=outs, in_specs=specs, out_spe...  48.5 us
    unnamed x38, local copies, waits for them, and re-layouts  13.3 us
    all_to_all x1, starting transfers between devices, shards(): groups = lax.all_to_all(group_equiv, 'outer', 0, 0, tiled=True)  9.86 us
    ppermute x1, starting transfers between devices, shards(): right = lax.ppermute(halo, 'inner', [(i + 1, i) for i in range(ends)])  8.77 us
    all_to_all x1, starting transfers between devices, shards(): dev_local = lax.all_to_all(local, 'inner', 0, 0, tiled=True)  7.49 us
    all_to_all x1, starting transfers between devices, shards(): peers_equiv = lax.all_to_all(dev_equiv, 'inner', 0, 0, tiled=True)  6.16 us
  transfers between devices with their start and end apart: 5, of which 0 were waited for; matrix products, arithmetic and copies ran while one was open for 0% of the time, Pallas kernels for 39%

profile of v1, /device:TPU:1, one launch (start us, length us, event | category | flops | bytes accessed | tf_op | source)
XLA Modules:
  0.0 96.1 jit_solution(13899373445872556453)
XLA Ops:
  0.0 4.4 %leaf_and_device_equiv.1 = (f32[128,128]{1,0:T(8,128)}, f32[72,512]{1,0:T(8,128)S(1)}, f32[165,165]{1,0:T(8,128)S(1)}, f32[165,165]{1,0:T(8,128)S(1)}, f32[176,128]{1,0:T(8,128)S(1)}, /*index=5*/f32[8,256]{1,0:T(8,128)S(1)}) custom-call(f32[3,512]{1,0:T(4,128)} %off_hbm.1, f32[64,512]{1,0:T(8,128)} %q_hbm.1, s32[16]{0:T(128)} %counts_hbm.1, ...), custom_call_target="tpu_custom_call" | custom-call | flops 1200000000 | bytes 500000 | tf_op jit(solution)/shard_map/leaf_and_device_equiv/pallas_call | solution.py:463
  4.4 0.0 copy-start.6
  4.4 0.7 copy-done.6
  5.1 0.0 copy-start.9
  5.1 0.0 copy-start.16
  5.1 2.7 %evaluation_maps.1 = (bf16[2,176,512]{2,1,0:T(8,128)(2,1)S(1)}, bf16[2,176,512]{2,1,0:T(8,128)(2,1)S(1)}, f32[72,512]{1,0:T(8,128)}) custom-call(f32[72,512]{1,0:T(8,128)S(1)} %get-tuple-element.19.own_ref, f32[165,165]{1,0:T(8,128)S(1)} %get-tuple-element.20.down_ref, f32[176,128]{1,0:T(8,128)S(1)} %get-tuple-element.21.col_ref, ...), custom_call_target="tpu_custom_call" | custom-call | flops 2000000000 | bytes 500000 | tf_op jit(solution)/shard_map/evaluation_maps/pallas_call | solution.py:463
  7.7 0.0 copy-done.9
  7.7 0.0 copy-start.4
  7.7 0.7 copy-done.4
  8.5 0.0 copy-start.12
  8.5 0.8 copy-done.12
  9.2 8.8 %collective-permute-start.1 = (f32[72,512]{1,0:T(8,128)}, f32[72,512]{1,0:T(8,128)S(1)}, u32[]{:S(2)}, u32[]{:S(2)}) collective-permute-start(f32[72,512]{1,0:T(8,128)} %get-tuple-element.29), channel_id=1, source_target_pairs={{1,0},{2,1},{3,2},{4,3},{5,4},{6,5},{7,6},{8,7},{9,8},{10,9},{11,1... | collective-permute-start | bytes 442376 | tf_op jit(solution)/shard_map/ppermute | solution.py:509
  18.0 1.9 %collective-permute-start = (f32[72,512]{1,0:T(8,128)}, f32[72,512]{1,0:T(8,128)}, u32[]{:S(2)}, u32[]{:S(2)}) collective-permute-start(f32[72,512]{1,0:T(8,128)} %get-tuple-element.29), channel_id=1, source_target_pairs={{0,1},{1,2},{2,3},{3,4},{4,5},{5,6},{6,7},{7,8},{8,9},{9,10},{10,1... | collective-permute-start | bytes 442376 | tf_op jit(solution)/shard_map/ppermute | solution.py:508
  19.9 6.2 %all-to-all-start = ((f32[16,8,128]{2,1,0:T(8,128)}), f32[16,8,128]{2,1,0:T(8,128)S(1)}, u32[]{:S(2)}, u32[]{:S(2)}) async-start(f32[16,8,128]{2,1,0:T(8,128)} %bitcast), calls=%async_computation | async-start | bytes 131072 | tf_op jit(solution)/shard_map/all_to_all | solution.py:501
  26.1 5.8 %group_maps.1 = (bf16[32,2,176,256]{3,2,1,0:T(8,128)(2,1)S(1)}, bf16[16,2,176,256]{3,2,1,0:T(8,128)(2,1)S(1)}) custom-call(f32[128,128]{1,0:T(8,128)} %get-tuple-element.18.flow_ref, f32[176,128]{1,0:T(8,128)S(1)} %get-tuple-element.21.col_ref, f32[8,256]{1,0:T(8,128)S(1)} %get-tuple-element.22.row_ref), custom_call_target="tpu_custom_call" | custom-call | flops 2000000000 | bytes 500000 | tf_op jit(solution)/shard_map/group_maps/pallas_call | solution.py:463
  31.9 0.0 copy-start
  31.9 2.5 %copy-done = bf16[32,2,176,256]{3,2,1,0:T(8,128)(2,1)} copy-done((bf16[32,2,176,256]{3,2,1,0:T(8,128)(2,1)}, bf16[32,2,176,256]{3,2,1,0:T(8,128)(2,1)S(1)}, u32[]{:S(2)}) %copy-start) | copy-done | bytes 5767192
  34.4 0.0 all-to-all-done
  34.4 0.0 copy-done.16
  34.4 0.0 copy-start.7
  34.4 0.9 copy-done.7
  35.4 1.8 %group_equiv.1 = f32[256,128]{1,0:T(8,128)} custom-call(f32[128,128]{1,0:T(8,128)S(1)} %bitcast.7, f32[165,165]{1,0:T(8,128)S(1)} %copy-done.7, f32[176,128]{1,0:T(8,128)S(1)} %get-tuple-element.21.col_ref, f32[8,256]{1,0:T(8,128)S(1)} %get-tuple-element.22.row_ref), custom_call_target="tpu_custom_call" | custom-call | flops 800000000 | bytes 500000 | tf_op jit(solution)/shard_map/group_equiv/pallas_call | solution.py:463
  37.2 9.9 %all-to-all-start.1 = ((f32[32,8,128]{2,1,0:T(8,128)}), f32[32,8,128]{2,1,0:T(8,128)S(1)}, u32[]{:S(2)}, u32[]{:S(2)}) async-start(f32[32,8,128]{2,1,0:T(8,128)} %bitcast.2), calls=%async_computation.1 | async-start | bytes 262144 | tf_op jit(solution)/shard_map/all_to_all | solution.py:520
  47.0 0.0 copy-start.17
  47.1 0.7 copy-done.17
  47.7 0.0 copy-start.2
  47.8 0.0 copy-start.10
  47.8 9.8 %device_to_device.1.peers_ref = f32[64,256]{1,0:T(8,128)S(1)} custom-call(f32[128,128]{1,0:T(8,128)S(1)} %bitcast.8, f32[176,128]{1,0:T(8,128)S(1)} %get-tuple-element.21.col_ref, f32[8,256]{1,0:T(8,128)S(1)} %copy-done.17), custom_call_target="tpu_custom_call" | custom-call | flops 3200000000 | bytes 500000 | tf_op jit(solution)/shard_map/device_to_device/pallas_call | solution.py:463
  57.6 0.0 collective-permute-done.1.right_ref
  57.6 0.0 collective-permute-done.left_ref
  57.6 0.0 copy-done.2
  57.6 0.0 copy-done.10
  57.6 0.0 copy-start.3
  57.7 0.0 copy-start.18
  57.7 3.0 %near_field.1.near_ref = f32[64,512]{1,0:T(8,128)S(1)} custom-call(s32[16,12]{1,0:T(8,128)S(1)} %copy-done.2, f32[72,512]{1,0:T(8,128)} %collective-permute-done.left_ref, f32[72,512]{1,0:T(8,128)S(1)} %copy-done.10, f32[72,512]{1,0:T(8,128)S(1)} %collective-permute-done.1.right_ref), custom_call_target="tpu_custom_call" | custom-call | flops 1600000000 | bytes 500000 | tf_op jit(solution)/shard_map/near_field/pallas_call | solution.py:463
  60.6 0.0 copy-start.14
  60.6 0.6 copy-done.14
  61.3 0.0 all-to-all-done.1
  61.3 0.0 copy-start.1
  61.3 2.6 %copy-done.1 = bf16[32,2,176,256]{3,2,1,0:T(8,128)(2,1)S(1)} copy-done((bf16[32,2,176,256]{3,2,1,0:T(8,128)(2,1)S(1)}, bf16[32,2,176,256]{3,2,1,0:T(8,128)(2,1)}, u32[]{:S(2)}) %copy-start.1) | copy-done | bytes 5767192
  63.9 3.0 %group_and_device_local.1 = f32[128,128]{1,0:T(8,128)} custom-call(f32[256,128]{1,0:T(8,128)S(1)} %bitcast.6, f32[64,256]{1,0:T(8,128)S(1)} %device_to_device.1.peers_ref, bf16[32,2,176,256]{3,2,1,0:T(8,128)(2,1)S(1)} %copy-done.1, bf16[16,2,176,256]{3,2,1,0:T(8,128)(2,1)S(1)} %get-tuple-element.26.to_dev_ref, f32[165,165]{1,0:T(8,128)S(1)} %get-tuple-element.20.down_ref), custom_call_target="tpu_custom_call" | custom-call | flops 1200000000 | bytes 500000 | tf_op jit(solution)/shard_map/group_and_device_local/pallas_call | solution.py:463
  66.9 7.5 %all-to-all-start.2 = ((f32[16,8,128]{2,1,0:T(8,128)}), f32[16,8,128]{2,1,0:T(8,128)S(1)}, u32[]{:S(2)}, u32[]{:S(2)}) async-start(f32[16,8,128]{2,1,0:T(8,128)} %bitcast.4), calls=%async_computation.2 | async-start | bytes 131072 | tf_op jit(solution)/shard_map/all_to_all | solution.py:534
  74.4 0.0 copy-done.3
  74.4 0.0 copy-done.18
  74.4 0.0 copy-start.8
  74.4 0.9 copy-done.8
  75.3 0.0 copy-start.11
  75.3 0.9 copy-done.11
  76.2 0.0 copy-start.13
  76.2 1.0 %copy-done.13 = bf16[2,176,512]{2,1,0:T(8,128)(2,1)S(1)} copy-done((bf16[2,176,512]{2,1,0:T(8,128)(2,1)S(1)}, bf16[2,176,512]{2,1,0:T(8,128)(2,1)}, u32[]{:S(2)}) %copy-start.13) | copy-done | bytes 360472
  77.2 0.0 copy-start.15
  77.2 0.9 copy-done.15
  78.1 0.0 copy-start.5
  78.1 17.1 %far_field.1.base_ref = f32[64,512]{1,0:T(8,128)S(1)} custom-call(s32[16,12]{1,0:T(8,128)S(1)} %copy-done.3, f32[72,512]{1,0:T(8,128)} %collective-permute-done.left_ref, f32[72,512]{1,0:T(8,128)S(1)} %copy-done.11, f32[72,512]{1,0:T(8,128)S(1)} %collective-permute-done.1.right_ref, bf16[2,176,512]{2,1,0:T(8,128)(2,1)S(1)} %copy-done.13, ...), custom_call_target="tpu_custom_call" | custom-call | flops 4800000000 | bytes 500000 | tf_op jit(solution)/shard_map/far_field/pallas_call | solution.py:463
  95.2 0.0 all-to-all-done.2
  95.3 0.0 copy-done.5
  95.3 0.9 potential.1
Async XLA Ops:
  4.4 0.7 copy-start.6
  5.1 2.7 %copy-start.9 = (f32[72,512]{1,0:T(8,128)}, f32[72,512]{1,0:T(8,128)S(1)}, u32[]{:S(2)}) copy-start(f32[72,512]{1,0:T(8,128)S(1)} %get-tuple-element.19.own_ref) | copy-start | bytes 442372
  5.1 29.4 %copy-start.16 = (f32[8,256]{1,0:T(8,128)}, f32[8,256]{1,0:T(8,128)S(1)}, u32[]{:S(2)}) copy-start(f32[8,256]{1,0:T(8,128)S(1)} %get-tuple-element.22.row_ref) | copy-start | bytes 24580
  7.7 0.8 copy-start.4
  8.5 0.8 copy-start.12
  9.2 48.4 %collective-permute-start.1 = (f32[72,512]{1,0:T(8,128)}, f32[72,512]{1,0:T(8,128)S(1)}, u32[]{:S(2)}, u32[]{:S(2)}) collective-permute-start(f32[72,512]{1,0:T(8,128)} %get-tuple-element.29), channel_id=1, source_target_pairs={{1,0},{2,1},{3,2},{4,3},{5,4},{6,5},{7,6},{8,7},{9,8},{10,9},{11,1... | collective-permute-start | bytes 442376 | tf_op jit(solution)/shard_map/ppermute | solution.py:509
  18.0 39.6 %collective-permute-start = (f32[72,512]{1,0:T(8,128)}, f32[72,512]{1,0:T(8,128)}, u32[]{:S(2)}, u32[]{:S(2)}) collective-permute-start(f32[72,512]{1,0:T(8,128)} %get-tuple-element.29), channel_id=1, source_target_pairs={{0,1},{1,2},{2,3},{3,4},{4,5},{5,6},{6,7},{7,8},{8,9},{9,10},{10,1... | collective-permute-start | bytes 442376 | tf_op jit(solution)/shard_map/ppermute | solution.py:508
  19.9 14.5 %all-to-all-start = ((f32[16,8,128]{2,1,0:T(8,128)}), f32[16,8,128]{2,1,0:T(8,128)S(1)}, u32[]{:S(2)}, u32[]{:S(2)}) async-start(f32[16,8,128]{2,1,0:T(8,128)} %bitcast), calls=%async_computation | async-start | bytes 131072 | tf_op jit(solution)/shard_map/all_to_all | solution.py:501
  31.9 2.5 %copy-start = (bf16[32,2,176,256]{3,2,1,0:T(8,128)(2,1)}, bf16[32,2,176,256]{3,2,1,0:T(8,128)(2,1)S(1)}, u32[]{:S(2)}) copy-start(bf16[32,2,176,256]{3,2,1,0:T(8,128)(2,1)S(1)} %get-tuple-element.25.maps_ref) | copy-start | bytes 17301508
  34.4 0.9 copy-start.7
  37.2 24.1 %all-to-all-start.1 = ((f32[32,8,128]{2,1,0:T(8,128)}), f32[32,8,128]{2,1,0:T(8,128)S(1)}, u32[]{:S(2)}, u32[]{:S(2)}) async-start(f32[32,8,128]{2,1,0:T(8,128)} %bitcast.2), calls=%async_computation.1 | async-start | bytes 262144 | tf_op jit(solution)/shard_map/all_to_all | solution.py:520
  47.0 0.7 copy-start.17
  47.7 9.9 %copy-start.2 = (s32[16,12]{1,0:T(8,128)S(1)}, s32[16,12]{1,0:T(8,128)}, u32[]{:S(2)}) copy-start(s32[16,12]{1,0:T(8,128)} %near_ref.1) | copy-start | bytes 2308
  47.8 9.9 %copy-start.10 = (f32[72,512]{1,0:T(8,128)S(1)}, f32[72,512]{1,0:T(8,128)}, u32[]{:S(2)}) copy-start(f32[72,512]{1,0:T(8,128)} %copy-done.9) | copy-start | bytes 442372
  57.6 16.7 %copy-start.3 = (s32[16,12]{1,0:T(8,128)S(1)}, s32[16,12]{1,0:T(8,128)}, u32[]{:S(2)}) copy-start(s32[16,12]{1,0:T(8,128)} %far_ref.1) | copy-start | bytes 2308
  57.7 16.7 %copy-start.18 = (f32[8,256]{1,0:T(8,128)S(1)}, f32[8,256]{1,0:T(8,128)}, u32[]{:S(2)}) copy-start(f32[8,256]{1,0:T(8,128)} %copy-done.16) | copy-start | bytes 24580
  60.6 0.6 copy-start.14
  61.3 2.6 %copy-start.1 = (bf16[32,2,176,256]{3,2,1,0:T(8,128)(2,1)S(1)}, bf16[32,2,176,256]{3,2,1,0:T(8,128)(2,1)}, u32[]{:S(2)}) copy-start(bf16[32,2,176,256]{3,2,1,0:T(8,128)(2,1)} %copy-done) | copy-start | bytes 17301508
  66.9 28.3 %all-to-all-start.2 = ((f32[16,8,128]{2,1,0:T(8,128)}), f32[16,8,128]{2,1,0:T(8,128)S(1)}, u32[]{:S(2)}, u32[]{:S(2)}) async-start(f32[16,8,128]{2,1,0:T(8,128)} %bitcast.4), calls=%async_computation.2 | async-start | bytes 131072 | tf_op jit(solution)/shard_map/all_to_all | solution.py:534
  74.4 0.9 copy-start.8
  75.3 0.9 copy-start.11
  76.2 1.0 %copy-start.13 = (bf16[2,176,512]{2,1,0:T(8,128)(2,1)S(1)}, bf16[2,176,512]{2,1,0:T(8,128)(2,1)}, u32[]{:S(2)}) copy-start(bf16[2,176,512]{2,1,0:T(8,128)(2,1)} %copy-done.12) | copy-start | bytes 1081348
  77.2 0.9 copy-start.15
  78.1 17.1 %copy-start.5 = (bf16[2,176,512]{2,1,0:T(8,128)(2,1)S(1)}, bf16[2,176,512]{2,1,0:T(8,128)(2,1)}, u32[]{:S(2)}) copy-start(bf16[2,176,512]{2,1,0:T(8,128)(2,1)} %copy-done.4) | copy-start | bytes 1081348

commit v2 on v1

v2 whole, which is shorter than its diff:
```python
import functools

import jax
import jax.numpy as jnp
import numpy as np
from jax import lax
from jax.experimental import pallas as pl
from jax.experimental.pallas import tpu as pltpu
from jax.sharding import PartitionSpec as P

SOFTEN = 0.25
GOLDEN = 2.399963229728653
RHS = 64
TERMS = 165
SUB = 176
LANE = 256
LEAVES = 16
SLOTS = 32
POINTS = LEAVES * SLOTS
ROWS = 72
INNER = 16
OUTER = 32
PART = RHS // INNER
BF = jnp.bfloat16
F32 = jnp.float32


def sphere_tables():
    steps = np.arange(TERMS, dtype=np.float32)
    height = (np.float32(1.0) - (np.float32(2.0) * steps + np.float32(1.0)) / np.float32(TERMS)).astype(np.float32)
    radial = np.sqrt(np.maximum(np.float32(1.0) - height * height, np.float32(0.0))).astype(np.float32)
    angle = (steps * np.float32(GOLDEN)).astype(np.float32)
    dirs = np.stack([radial * np.cos(angle), radial * np.sin(angle), height]).astype(np.float32)
    col = np.zeros((SUB, 128), np.float32)
    col[:TERMS, :3] = dirs.T
    row = np.zeros((8, LANE), np.float32)
    row[:3, :TERMS] = dirs
    return col, row


def split(x):
    high = x.astype(BF)
    return high, (x - high.astype(F32)).astype(BF)


def dot(a, b):
    return jnp.dot(a, b, preferred_element_type=F32)


def dot_nt(a, b):
    return lax.dot_general(a, b, (((1,), (1,)), ((), ())), preferred_element_type=F32)


def mm3(a, b, f=dot):
    return f(a[0], b[0]) + f(a[1], b[0]) + f(a[0], b[1])


def columns(col_ref):
    return [jnp.broadcast_to(col_ref[:, c : c + 1], (SUB, 128)) for c in range(3)]


def two(x):
    return jnp.concatenate([x, x], axis=1)


def square_of(axis, shift, radius_t, radius_i, cols, row_ref):
    diff = (radius_t * row_ref[axis : axis + 1, :] + shift) - two(radius_i * cols[axis])
    return diff * diff


def box_kernels(xs, ys, zs, radius_t, radius_i, col_ref, row_ref, tab_ref):
    cols = columns(col_ref)
    for n, shift in enumerate(xs):
        tab_ref[n] = square_of(0, shift, radius_t, radius_i, cols, row_ref)
    zsq = len(xs)
    for n, shift in enumerate(zs):
        tab_ref[zsq + n] = square_of(2, shift, radius_t, radius_i, cols, row_ref) + SOFTEN
    start = zsq + len(zs)
    for b, shift in enumerate(ys):
        ysq = square_of(1, shift, radius_t, radius_i, cols, row_ref)
        for c in range(len(zs)):
            tab_ref[start + b * len(zs) + c] = ysq + tab_ref[zsq + c]
    for b in range(len(ys)):
        for c in range(len(zs)):
            for a in range(len(xs)):
                yield (a, b, c), lax.rsqrt(tab_ref[a] + tab_ref[start + b * len(zs) + c])


def bits(ids, low, axis, top=14):
    total = 0
    for level in range(5):
        place = 3 * level + axis
        if low <= place < top:
            total = total + (((ids >> place) & 1) << level)
    return total


def corner(leaf_id, low):
    return [bits(leaf_id, low, axis) for axis in range(3)]


def local_leaf(index):
    return ((index & 1) + ((index >> 3) & 1) * 2, (index >> 1) & 1, (index >> 2) & 1)


def peer_box(inner):
    return (((inner >> 2) & 1) * 4, (inner & 1) * 2 + ((inner >> 3) & 1) * 4, ((inner >> 1) & 1) * 2)


def leaf_kernel(offs, col_ref):
    total = SOFTEN
    for c in range(3):
        col = jnp.broadcast_to(col_ref[:, c : c + 1], (SUB, 128)) * 1.8
        diff = jnp.concatenate([col] * (POINTS // 128), axis=1) - offs[c : c + 1, :]
        total = total + diff * diff
    return lax.rsqrt(total)


def padded(map_ref, pad_ref, scale):
    pad_ref[...] = jnp.zeros_like(pad_ref)
    pad_ref[0:TERMS, 0:TERMS] = map_ref[...] * scale
    return split(pad_ref[...])


def leaf_equivalents(charges, kern, up):
    block = lax.broadcasted_iota(jnp.int32, (RHS, 256), 1) // SLOTS
    out = []
    for half in range(2):
        lanes = slice(half * 256, half * 256 + 256)
        own = charges[:, lanes]
        spread = split(jnp.concatenate([jnp.where(block == g, own, 0.0) for g in range(8)], axis=0))
        check = mm3(spread, (kern[0][:, lanes], kern[1][:, lanes]), dot_nt)
        out.append(mm3(split(check), up))
    return out


def pack(rows):
    low, high = rows[:, :128], rows[:, 128:]
    n = rows.shape[0]
    top = lax.broadcasted_iota(jnp.int32, (n, 128), 0) % 8 < 4
    first = jnp.where(top, low, pltpu.roll(high, 4, 0))
    second = jnp.where(top, pltpu.roll(low, n - 4, 0), high)
    tiles = []
    for m in range(n // 8):
        tiles += [first[8 * m : 8 * m + 8], second[8 * m : 8 * m + 8]]
    return jnp.concatenate(tiles, axis=0)


def unpack(tiles):
    n = tiles.shape[0] // 2
    first = jnp.concatenate([tiles[16 * m : 16 * m + 8] for m in range(n // 8)], axis=0)
    second = jnp.concatenate([tiles[16 * m + 8 : 16 * m + 16] for m in range(n // 8)], axis=0)
    top = lax.broadcasted_iota(jnp.int32, (n, 128), 0) % 8 < 4
    low = jnp.where(top, first, pltpu.roll(second, 4, 0))
    high = jnp.where(top, pltpu.roll(first, n - 4, 0), second)
    return jnp.concatenate([low, high], axis=1)


def tile_dot(tile, high, low, acc):
    a_high, a_low = split(tile)
    both = jnp.concatenate([a_high, a_low], axis=0)
    rest = SUB - 128
    front = dot(both, high[:128]) + dot(both, low[:128])
    back = dot(both[:, :rest], high[128:]) + dot(both[:, :rest], low[128:])
    return acc[0] + front, acc[1] + back


def tile_sum(acc):
    front = acc[0][:8] + acc[0][8:]
    back = acc[1][:8] + acc[1][8:]
    return front + pltpu.roll(back, 4, 0)


def head_kernel(
    off_hbm, q_hbm, counts_hbm, up_hbm, down_hbm, col_hbm, row_hbm,
    out_ref, halo_ref, up_ref, down_ref, col_ref, row_ref,
    off_ref, q_ref, counts_ref, pad_ref, tab_ref, sems,
):
    moves = [
        pltpu.make_async_copy(src, dst, sems.at[n])
        for n, (src, dst) in enumerate(
            (
                (q_hbm, q_ref),
                (off_hbm, off_ref),
                (counts_hbm, counts_ref),
                (up_hbm, up_ref),
                (col_hbm, col_ref),
                (row_hbm, row_ref),
                (down_hbm, down_ref),
            )
        )
    ]
    for move in moves:
        move.start()
    for move in moves[:-1]:
        move.wait()
    lane = lax.broadcasted_iota(jnp.int32, (8, POINTS), 1)
    limit = jnp.zeros((8, POINTS), jnp.int32)
    for g in range(LEAVES):
        limit = jnp.where(lane // SLOTS == g, counts_ref[g], limit)
    filled = (lane % SLOTS < limit)[0:1]
    charges = jnp.where(filled, q_ref[...], 0.0)
    halo_ref[0:RHS, :] = charges
    halo_ref[RHS:ROWS, :] = jnp.zeros((ROWS - RHS, POINTS), F32)
    halo_ref[RHS : RHS + 3, :] = off_ref[...]
    kern = split(leaf_kernel(off_ref[...], col_ref))
    up = padded(up_ref, pad_ref, 18.0 / TERMS)
    up = (up[0][:, :], up[1][:, :])
    halves = leaf_equivalents(charges, kern, up)
    equiv = [split(h) for h in halves]
    acc = jnp.zeros((RHS, LANE), F32)
    for (x, y, z), kern in box_kernels(
        (1.5, 0.5, -0.5, -1.5), (0.5, -0.5), (0.5, -0.5), 6.0, 0.9, col_ref, row_ref, tab_ref
    ):
        half, g = (x >> 1), (x & 1) + 2 * y + 4 * z
        rows = slice(g * RHS, g * RHS + RHS)
        acc = acc + mm3((equiv[half][0][rows, :SUB], equiv[half][1][rows, :SUB]), split(kern))
    up60 = padded(up_ref, pad_ref, 60.0 / TERMS)
    out_ref[...] = pack(mm3(split(acc[:, :SUB]), up60))
    moves[-1].wait()


def group_up_kernel(x_ref, maps_ref, up_ref, out_ref, pad_ref):
    acc = (jnp.zeros((16, LANE), F32), jnp.zeros((16, LANE), F32))
    for e in range(INNER):
        acc = tile_dot(x_ref[8 * e : 8 * e + 8, :], maps_ref[e, 0], maps_ref[e, 1], acc)
    check = tile_sum(acc)
    both = jnp.concatenate([check, check], axis=0)
    equiv = mm3(split(both[:, :SUB]), padded(up_ref, pad_ref, 200.0 / TERMS))[:8]
    top = lax.broadcasted_iota(jnp.int32, (8, 128), 0) < 4
    tile = jnp.where(top, equiv[:, :128], pltpu.roll(equiv[:, 128:], 4, 0))
    for p in range(OUTER):
        out_ref[8 * p : 8 * p + 8, :] = tile


def box_order(rows):
    return jnp.concatenate(
        [rows[8 * k : 8 * k + 8] for k in (y * 4 + x * 2 + z for x in (0, 1) for z in (0, 1) for y in (0, 1))], axis=0
    )


def index_order(rows):
    return jnp.concatenate(
        [rows[8 * k : 8 * k + 8] for k in (x * 4 + z * 2 + y for y in (0, 1) for x in (0, 1) for z in (0, 1))], axis=0
    )


def peers_kernel(x_ref, col_ref, row_ref, out_ref, tab_ref, shifted_ref):
    equiv = jnp.concatenate([box_order(unpack(x_ref[...])), jnp.zeros((16, LANE), F32)], axis=0)
    shifted_ref[...] = jnp.zeros_like(shifted_ref)
    for q in range(4):
        high, low = split(pltpu.roll(equiv, 4 * q, 0) if q else equiv)
        shifted_ref[q, 0, RHS : RHS + 80, :] = high
        shifted_ref[q, 1, RHS : RHS + 80, :] = low
    cols = columns(col_ref)
    for dy in range(-3, 4):
        tab_ref[dy + 3] = square_of(1, 2.0 * dy, 3.0, 3.0, cols, row_ref) + SOFTEN
    row = lax.broadcasted_iota(jnp.int32, (RHS, 128), 0)
    lane = lax.broadcasted_iota(jnp.int32, (RHS, 128), 1)
    px, pz, py = row >> 5, (row >> 4) & 1, (row >> 2) & 3
    dest = (py & 1) + pz * 2 + px * 4 + (py >> 1) * 8

    def step(turn, acc):
        dx = turn // 3 - 1
        dz = turn % 3 - 1
        sx, sy, sz = px - dx, py - (lane - 3), pz - dz
        inside = (sx >= 0) & (sx < 2) & (sy >= 0) & (sy < 4) & (sz >= 0) & (sz < 2)
        source = (sy & 1) + sz * 2 + sx * 4 + (sy >> 1) * 8
        mask = (inside & (jnp.abs(source - dest) >= 2)).astype(F32)
        plane = square_of(0, dx.astype(F32) * 4.0, 3.0, 3.0, cols, row_ref)
        plane = plane + square_of(2, dz.astype(F32) * 2.0, 3.0, 3.0, cols, row_ref)
        tab_ref[7] = plane
        for dy in range(-3, 4):
            q = dy % 4
            start = pl.multiple_of(RHS - (dx * 2 + dz) * 16 - 4 * (dy - q), 16)
            keep = two(jnp.broadcast_to(mask[:, dy + 3 : dy + 4], (RHS, 128))).astype(BF)
            high = shifted_ref[q, 0, pl.ds(start, RHS), :] * keep
            low = shifted_ref[q, 1, pl.ds(start, RHS), :] * keep
            kern = split(lax.rsqrt(tab_ref[7] + tab_ref[dy + 3]))
            acc = acc + mm3((high[:, :SUB], low[:, :SUB]), kern)
        return acc

    out_ref[...] = index_order(lax.fori_loop(0, 9, step, jnp.zeros((RHS, LANE), F32)))


def local_kernel(x_ref, peers_ref, down_ref, col_ref, row_ref, out_ref, pad_ref, tab_ref):
    outer = lax.axis_index("outer")
    own = [p.astype(F32) for p in corner(outer * 256, 8)]
    cols = columns(col_ref)
    for n in range(4):
        tab_ref[n] = square_of(2, own[2] - 4.0 * n, 10.0, 20.0, cols, row_ref) + SOFTEN
    for x in range(4):
        xsq = square_of(0, own[0] - 8.0 * x, 10.0, 20.0, cols, row_ref)
        for y in range(2):
            tab_ref[4 + x * 2 + y] = xsq + square_of(1, own[1] - 8.0 * y, 10.0, 20.0, cols, row_ref)
    acc = (jnp.zeros((16, LANE), F32), jnp.zeros((16, LANE), F32))
    for p in range(OUTER):
        z, x, y = (p & 1) + ((p >> 3) & 1) * 2, ((p >> 1) & 1) + ((p >> 4) & 1) * 2, (p >> 2) & 1
        weight = (jnp.abs(p - outer) >= 2).astype(F32)
        kern = split(lax.rsqrt(tab_ref[4 + x * 2 + y] + tab_ref[z]))
        acc = tile_dot(x_ref[8 * p : 8 * p + 8, :] * weight, kern[0], kern[1], acc)
    check = tile_sum(acc)
    both = jnp.concatenate([check, check], axis=0)
    group = mm3(split(both[:, :SUB]), padded(down_ref, pad_ref, 200.0 / TERMS))[:8]
    pieces = jnp.concatenate(split(group[:, :SUB]), axis=0)
    top = lax.broadcasted_iota(jnp.int32, (8, LANE), 0) < 4
    found = [None] * INNER
    for (x, y, z), kern in box_kernels(
        (-2.0, 2.0), (-3.0, -1.0, 1.0, 3.0), (-1.0, 1.0), 3.0, 20.0, col_ref, row_ref, tab_ref
    ):
        high, low = split(kern)
        part = dot(pieces, high) + dot(pieces, low)
        found[(y & 1) + z * 2 + x * 4 + (y >> 1) * 8] = part[:8] + part[8:]
    merged = [jnp.where(top, found[2 * m], pltpu.roll(found[2 * m + 1], 4, 0)) for m in range(INNER // 2)]
    total = jnp.concatenate(merged, axis=0) + peers_ref[...]
    out_ref[...] = pack(mm3(split(total[:, :SUB]), padded(down_ref, pad_ref, 60.0 / TERMS)))


def up_maps_kernel(flow_ref, col_ref, row_ref, out_ref, tab_ref):
    for (x, y, z), kern in box_kernels(
        (2.0, -2.0), (3.0, 1.0, -1.0, -3.0), (1.0, -1.0), 20.0, 3.0, col_ref, row_ref, tab_ref
    ):
        d = (y & 1) + z * 2 + x * 4 + (y >> 1) * 8
        high, low = split(kern)
        out_ref[d, 0, :, :] = high
        out_ref[d, 1, :, :] = low


def operator_kernel(own_ref, down_ref, col_ref, row_ref, w_ref, m_ref, pad_ref, tab_ref):
    off = own_ref[RHS : RHS + 3, :]
    down = padded(down_ref, pad_ref, 18.0 / TERMS)
    down = (down[0][:, :SUB], down[1][:, :SUB])
    weights = split(mm3(down, split(leaf_kernel(off, col_ref))))
    w_ref[0, :, :] = weights[0]
    w_ref[1, :, :] = weights[1]
    block = lax.broadcasted_iota(jnp.int32, (SUB, 256), 1) // SLOTS
    found = [jnp.zeros((SUB, 256), F32)] * 2
    for (x, y, z), kern in box_kernels(
        (-1.5, -0.5, 0.5, 1.5), (-0.5, 0.5), (-0.5, 0.5), 0.9, 6.0, col_ref, row_ref, tab_ref
    ):
        half, g = (x >> 1), (x & 1) + 2 * y + 4 * z
        lanes = slice(half * 256, half * 256 + 256)
        own = (weights[0][:, lanes], weights[1][:, lanes])
        found[half] = jnp.where(block == g, mm3(split(kern[:, :SUB]), own), found[half])
    for half in range(2):
        lanes = slice(half * 256, half * 256 + 256)
        m_high, m_low = split(found[half])
        m_ref[0, :, lanes] = m_high
        m_ref[1, :, lanes] = m_low


def near_kernel(near_ref, left_ref, own_ref, right_ref, out_ref, mask_ref, high_ref, low_ref):
    offs = jnp.concatenate([own_ref[RHS:ROWS, :], jnp.zeros((120, POINTS), F32)], axis=0).T
    inner = lax.axis_index("inner")
    device = lax.axis_index("outer") * INNER + inner
    base = (device - 1) * LEAVES
    total = 3 * POINTS
    lane = lax.broadcasted_iota(jnp.int32, (LEAVES, total), 1) // SLOTS
    found = jnp.zeros((LEAVES, total), F32)
    near = near_ref[...] - base
    for k in range(12):
        found = jnp.where(lane == near[:, k : k + 1], 1.0, found)
    mask_ref[...] = found
    leaf = lax.broadcasted_iota(jnp.int32, (1, POINTS), 1) // SLOTS
    within = local_leaf(leaf)
    own_box = corner(device * LEAVES, 4)
    sources = []
    for c in range(3):
        lanes = []
        for side, ref in ((-1, left_ref), (0, own_ref), (1, right_ref)):
            box = corner((device + side) * LEAVES, 4)[c] - own_box[c]
            lanes.append(ref[RHS + c : RHS + c + 1, :] + (box + within[c]).astype(F32))
        sources.append(jnp.concatenate(lanes, axis=1))
    for g in range(LEAVES):
        rows = slice(g * SLOTS, g * SLOTS + SLOTS)
        place = local_leaf(g)
        dist = SOFTEN
        for c in range(3):
            diff = (offs[rows, c : c + 1] + float(place[c])) - sources[c]
            dist = dist + diff * diff
        k_high, k_low = split(lax.rsqrt(dist) * mask_ref[g : g + 1, :])
        high_ref[rows, :] = k_high
        low_ref[rows, :] = k_low
    charges = jnp.concatenate([r[0:RHS, :] for r in (left_ref, own_ref, right_ref)], axis=1)
    q_high, q_low = split(charges)
    both = jnp.concatenate([q_high, q_low], axis=0)
    res = dot_nt(high_ref[...], both)
    res = res + jnp.concatenate([dot_nt(low_ref[...], q_high), jnp.zeros((POINTS, RHS), F32)], axis=1)
    flipped = res.T
    out_ref[...] = flipped[:RHS] + flipped[RHS:]


def far_kernel(far_ref, left_ref, own_ref, right_ref, w_ref, up_ref, near_ref, col_ref, row_ref, out_ref, pad_ref, e_ref, dl_ref, xtab_ref, tab_ref):
    inner = lax.axis_index("inner")
    device = lax.axis_index("outer") * INNER + inner
    up = padded(up_ref, pad_ref, 18.0 / TERMS)
    for side, ref in enumerate((left_ref, own_ref, right_ref)):
        kern = split(leaf_kernel(ref[RHS : RHS + 3, :], col_ref))
        halves = leaf_equivalents(ref[0:RHS, :], kern, up)
        for half in range(2):
            e_high, e_low = split(halves[half])
            for g in range(8):
                start = ((side * 2 + half) * 8 + g) * 2 * RHS
                e_ref[start : start + RHS, :] = e_high[g * RHS : g * RHS + RHS]
                e_ref[start + RHS : start + 2 * RHS, :] = e_low[g * RHS : g * RHS + RHS]
    first = (device - 1) * LEAVES
    boxes = [corner((device + side) * LEAVES, 4) for side in (-1, 0, 1)]
    boxes = [[(boxes[1][c] - box[c]).astype(F32) for c in range(3)] for box in boxes]
    cols = columns(col_ref)
    for side in range(3):
        for n in range(7):
            xtab_ref[side * 7 + n] = square_of(0, boxes[side][0] + (n - 3.0), 0.9, 1.8, cols, row_ref)
        for c in range(3):
            tab_ref[27 + c] = square_of(2, boxes[side][2] + (c - 1.0), 0.9, 1.8, cols, row_ref) + SOFTEN
        for b in range(3):
            ysq = square_of(1, boxes[side][1] + (b - 1.0), 0.9, 1.8, cols, row_ref)
            for c in range(3):
                tab_ref[side * 9 + b * 3 + c] = ysq + tab_ref[27 + c]

    def one_leaf(g, carry):
        own = local_leaf(g)
        acc = jnp.zeros((RHS, LANE), F32)
        for k in range(12):
            window = far_ref[g, k] - first
            side = window >> 4
            place = local_leaf(window & 15)
            x = side * 7 + 3 + own[0] - place[0]
            yz = side * 9 + 4 + (own[1] - place[1]) * 3 + own[2] - place[2]
            k_high, k_low = split(lax.rsqrt(xtab_ref[x] + tab_ref[yz]))
            start = pl.multiple_of(window * (2 * RHS), 2 * RHS)
            equiv = e_ref[pl.ds(start, 2 * RHS), :][:, :SUB]
            wide = dot(equiv, k_high)
            acc = acc + wide[:RHS] + wide[RHS:] + dot(equiv[:RHS], k_low)
        high, low = split(acc)
        start = pl.multiple_of(g * RHS, RHS)
        dl_ref[0, pl.ds(start, RHS), :] = high
        dl_ref[1, pl.ds(start, RHS), :] = low
        return carry

    lax.fori_loop(0, LEAVES, one_leaf, 0)
    block = lax.broadcasted_iota(jnp.int32, (RHS, 256), 1) // SLOTS
    for half in range(2):
        lanes = slice(half * 256, half * 256 + 256)
        rows = slice(half * 8 * RHS, (half + 1) * 8 * RHS)
        local = (dl_ref[0, rows, :][:, :SUB], dl_ref[1, rows, :][:, :SUB])
        res = mm3(local, (w_ref[0, :, lanes], w_ref[1, :, lanes]))
        acc = near_ref[:, lanes]
        for g in range(8):
            acc = acc + jnp.where(block == g, res[g * RHS : (g + 1) * RHS], 0.0)
        out_ref[:, lanes] = acc


def tail_kernel(x_ref, base_ref, m_ref, out_ref):
    local = split(unpack(x_ref[...])[:, :SUB])
    out_ref[...] = base_ref[...] + mm3(local, (m_ref[0], m_ref[1]))


VM = pl.BlockSpec(memory_space=pltpu.VMEM)
SM = pl.BlockSpec(memory_space=pltpu.SMEM)


def call(kernel, name, outs, specs, scratch, vmem, *args):
    return pl.pallas_call(
        kernel,
        name=name,
        out_shape=outs,
        in_specs=specs,
        out_specs=jax.tree.map(lambda _: VM, outs),
        scratch_shapes=scratch,
        compiler_params=pltpu.CompilerParams(vmem_limit_bytes=vmem * 1024 * 1024),
        cost_estimate=pl.CostEstimate(flops=1000, bytes_accessed=1000, transcendentals=0),
    )(*args)


def tie(value, *others):
    return lax.optimization_barrier((value,) + others)[0]


def shards(offsets, charges, counts, near, far, upward, downward):
    col_np, row_np = sphere_tables()
    sds = jax.ShapeDtypeStruct
    pad = pltpu.VMEM((SUB, LANE), F32)
    flow = sds((2 * RHS, 128), F32)
    square = sds((TERMS, TERMS), F32)

    def tables(n):
        return pltpu.VMEM((n, SUB, LANE), F32)

    def maps(n):
        return sds((n, 2, SUB, LANE), BF)

    inputs = (offsets, charges, counts, upward, downward, jnp.asarray(col_np), jnp.asarray(row_np))
    dev_equiv, own, upward, downward, col, row = call(
        head_kernel, "leaf_and_device_equiv",
        (flow, sds((ROWS, POINTS), F32), square, square, sds((SUB, 128), F32), sds((8, LANE), F32)),
        [pl.BlockSpec(memory_space=pltpu.HBM)] * 7,
        [
            pltpu.VMEM((3, POINTS), F32),
            pltpu.VMEM((RHS, POINTS), F32),
            pltpu.SMEM((LEAVES,), jnp.int32),
            pad,
            tables(10),
            pltpu.SemaphoreType.DMA((7,)),
        ],
        16, *(pltpu.with_memory_space_constraint(a, pltpu.HBM) for a in inputs),
    )
    peers_equiv = lax.all_to_all(dev_equiv, "inner", 0, 0, tiled=True)
    up_maps = call(up_maps_kernel, "up_maps", maps(INNER), [VM, VM, VM], [tables(14)], 12, dev_equiv, col, row)
    ends = INNER - 1
    left = lax.ppermute(own, "inner", [(i, i + 1) for i in range(ends)])
    right = lax.ppermute(own, "inner", [(i + 1, i) for i in range(ends)])
    group_equiv = call(
        group_up_kernel, "group_equiv", sds((8 * OUTER, 128), F32), [VM, VM, VM], [pad], 6,
        peers_equiv, up_maps, upward,
    )
    groups = lax.all_to_all(group_equiv, "outer", 0, 0, tiled=True)
    peers_part = call(
        peers_kernel, "device_to_device", sds((RHS, LANE), F32), [VM, VM, VM],
        [tables(8), pltpu.VMEM((4, 2, 3 * RHS, LANE), BF)], 6, peers_equiv, col, row,
    )
    groups = tie(groups, peers_part)
    local = call(
        local_kernel, "group_and_device_local", flow, [VM, VM, VM, VM, VM], [pad, tables(14)], 8,
        groups, peers_part, downward, col, row,
    )
    dev_local = lax.all_to_all(local, "inner", 0, 0, tiled=True)
    weights, evaluate = call(
        operator_kernel, "evaluation_maps", (sds((2, SUB, POINTS), BF), sds((2, SUB, POINTS), BF)),
        [VM, VM, VM, VM], [pad, tables(10)], 12, own, downward, col, row,
    )
    near_part = call(
        near_kernel, "near_field", sds((RHS, POINTS), F32), [VM, VM, VM, VM],
        [pltpu.VMEM((LEAVES, 3 * POINTS), F32), pltpu.VMEM((POINTS, 3 * POINTS), BF), pltpu.VMEM((POINTS, 3 * POINTS), BF)],
        14, near, left, own, right,
    )
    base = call(
        far_kernel, "far_field", sds((RHS, POINTS), F32), [SM, VM, VM, VM, VM, VM, VM, VM, VM],
        [
            pad,
            pltpu.VMEM((3 * LEAVES * 2 * RHS, LANE), BF),
            pltpu.VMEM((2, LEAVES * RHS, LANE), BF),
            tables(21),
            tables(30),
        ],
        24, far, left, own, right, weights, upward, near_part, col, row,
    )
    return call(tail_kernel, "potential", sds((RHS, POINTS), F32), [VM, VM, VM], [], 4, dev_local, base, evaluate)


def solution(mesh):
    both = ("outer", "inner")
    in_specs = (P(None, both), P(None, both), P(both), P(both, None), P(both, None), P(), P())
    return jax.shard_map(shards, mesh=mesh, in_specs=in_specs, out_specs=P(None, both), check_vma=False)
```

time: 96.8 us -> 75.6 us (0.78)
  local copies, waits for them, and re-layouts: 13.3 us -> 0.66 us
  Pallas kernels: 48.5 us -> 37.2 us
  waiting for transfers between devices: 0.01 us -> 6.13 us
  starting transfers between devices: 34.2 us -> 31.1 us
    unnamed x38 -> x6, local copies, waits for them, and re-layouts: 13.3 us -> 0.66 us
    pallas_call x9, Pallas kernels: 48.5 us -> 37.2 us  [call(): pl.pallas_call(kernel, name=name, out_shape=outs, in_specs=specs, out_spe...]
    ppermute x2, starting transfers between devices: 10.7 us -> 4.46 us  [the longest x1 2.54 us: shards(): left = lax.ppermute(own, 'inner', [(i, i + 1) for i in range(ends)])]
    all_to_all x1, waiting for transfers between devices: 0.01 us -> 6.12 us  [shards(): peers_equiv = lax.all_to_all(dev_equiv, 'inner', 0, 0, tiled=True)]
    all_to_all x1, starting transfers between devices: 6.16 us -> 11.8 us  [shards(): peers_equiv = lax.all_to_all(dev_equiv, 'inner', 0, 0, tiled=True)]
    all_to_all x1, starting transfers between devices: 7.49 us -> 5.13 us  [shards(): dev_local = lax.all_to_all(local, 'inner', 0, 0, tiled=True)]
  transfers between devices with their start and end apart: 5 -> 5, of which waited for: 0 -> 1; matrix products, arithmetic and copies ran while one was open for 0% -> 0% of each run, Pallas kernels for 39% -> 41%
where the time goes in v2:
time: 75.6 us; the launch traced here: 75.2 us
  Pallas kernels  37.2 us (49%)
  starting transfers between devices  31.1 us (41%)
  waiting for transfers between devices  6.13 us (8%)
    pallas_call x9, Pallas kernels, call(): pl.pallas_call(kernel, name=name, out_shape=outs, in_specs=specs, out_spe...  37.2 us
    all_to_all x1, starting transfers between devices, shards(): peers_equiv = lax.all_to_all(dev_equiv, 'inner', 0, 0, tiled=True)  11.8 us
    all_to_all x1, starting transfers between devices, shards(): groups = lax.all_to_all(group_equiv, 'outer', 0, 0, tiled=True)  9.67 us
    all_to_all x1, waiting for transfers between devices, shards(): peers_equiv = lax.all_to_all(dev_equiv, 'inner', 0, 0, tiled=True)  6.12 us
    all_to_all x1, starting transfers between devices, shards(): dev_local = lax.all_to_all(local, 'inner', 0, 0, tiled=True)  5.13 us
    ppermute x1, starting transfers between devices, shards(): left = lax.ppermute(own, 'inner', [(i, i + 1) for i in range(ends)])  2.54 us
    ppermute x1, starting transfers between devices, shards(): right = lax.ppermute(own, 'inner', [(i + 1, i) for i in range(ends)])  1.92 us
  transfers between devices with their start and end apart: 5, of which 1 were waited for; matrix products, arithmetic and copies ran while one was open for 0% of the time, Pallas kernels for 41%

profile of v2, /device:TPU:1, one launch (start us, length us, event | category | flops | bytes accessed | tf_op | source)
XLA Modules:
  0.0 75.2 jit_solution(11385630296391185381)
XLA Ops:
  0.0 4.7 %leaf_and_device_equiv.1 = (f32[128,128]{1,0:T(8,128)}, f32[72,512]{1,0:T(8,128)S(1)}, f32[165,165]{1,0:T(8,128)S(1)}, f32[165,165]{1,0:T(8,128)S(1)}, f32[176,128]{1,0:T(8,128)S(1)}, /*index=5*/f32[8,256]{1,0:T(8,128)S(1)}) custom-call(f32[3,512]{1,0:T(4,128)} %off_hbm.1, f32[64,512]{1,0:T(8,128)} %q_hbm.1, s32[16]{0:T(128)} %counts_hbm.1, ...), custom_call_target="tpu_custom_call" | custom-call | flops 1000 | bytes 1000 | tf_op jit(solution)/shard_map/leaf_and_device_equiv/pallas_call | solution.py:463
  4.7 11.8 %all-to-all-start = ((f32[16,8,128]{2,1,0:T(8,128)}), f32[16,8,128]{2,1,0:T(8,128)S(1)}, u32[]{:S(2)}, u32[]{:S(2)}) async-start(f32[16,8,128]{2,1,0:T(8,128)} %bitcast), calls=%async_computation | async-start | bytes 131072 | tf_op jit(solution)/shard_map/all_to_all | solution.py:507
  16.5 1.7 %up_maps.1.maps_ref = bf16[16,2,176,256]{3,2,1,0:T(8,128)(2,1)S(1)} custom-call(f32[128,128]{1,0:T(8,128)} %get-tuple-element.14.flow_ref, f32[176,128]{1,0:T(8,128)S(1)} %get-tuple-element.15.col_ref, f32[8,256]{1,0:T(8,128)S(1)} %get-tuple-element.16.row_ref), custom_call_target="tpu_custom_call" | custom-call | flops 1000 | bytes 1000 | tf_op jit(solution)/shard_map/up_maps/pallas_call | solution.py:463
  18.2 0.0 copy-start.1
  18.2 0.0 copy-start.2
  18.2 6.1 %all-to-all-done = f32[16,8,128]{2,1,0:T(8,128)S(1)} async-done(((f32[16,8,128]{2,1,0:T(8,128)}), f32[16,8,128]{2,1,0:T(8,128)S(1)}, u32[]{:S(2)}, u32[]{:S(2)}) %all-to-all-start) | async-done | bytes 65568 | tf_op jit(solution)/shard_map/all_to_all | solution.py:507
  24.3 0.7 group_equiv.1
  25.1 0.0 copy-start
  25.1 0.6 copy-done
  25.7 9.7 %all-to-all-start.1 = ((f32[32,8,128]{2,1,0:T(8,128)}), f32[32,8,128]{2,1,0:T(8,128)S(1)}, u32[]{:S(2)}, u32[]{:S(2)}) async-start(f32[32,8,128]{2,1,0:T(8,128)} %bitcast.8), calls=%async_computation.1 | async-start | bytes 262144 | tf_op jit(solution)/shard_map/all_to_all | solution.py:516
  35.4 2.5 %collective-permute-start = (f32[72,512]{1,0:T(8,128)S(1)}, f32[72,512]{1,0:T(8,128)S(1)}, u32[]{:S(2)}, u32[]{:S(2)}) collective-permute-start(f32[72,512]{1,0:T(8,128)S(1)} %get-tuple-element.20.own_ref), channel_id=1, source_target_pairs={{0,1},{1,2},{2,3},{3,4},{4,5},{5,6},{6,7},{7,8},{8,9},{9,10},{10,1... | collective-permute-start | bytes 442376 | tf_op jit(solution)/shard_map/ppermute | solution.py:510
  37.9 1.9 %collective-permute-start.1 = (f32[72,512]{1,0:T(8,128)S(1)}, f32[72,512]{1,0:T(8,128)S(1)}, u32[]{:S(2)}, u32[]{:S(2)}) collective-permute-start(f32[72,512]{1,0:T(8,128)S(1)} %get-tuple-element.20.own_ref), channel_id=1, source_target_pairs={{1,0},{2,1},{3,2},{4,3},{5,4},{6,5},{7,6},{8,7},{9,8},{10,9},{11,1... | collective-permute-start | bytes 442376 | tf_op jit(solution)/shard_map/ppermute | solution.py:511
  39.9 5.7 %device_to_device.1.peers_ref = f32[64,256]{1,0:T(8,128)S(1)} custom-call(f32[128,128]{1,0:T(8,128)S(1)} %bitcast.7, f32[176,128]{1,0:T(8,128)S(1)} %get-tuple-element.15.col_ref, f32[8,256]{1,0:T(8,128)S(1)} %get-tuple-element.16.row_ref), custom_call_target="tpu_custom_call" | custom-call | flops 1000 | bytes 1000 | tf_op jit(solution)/shard_map/device_to_device/pallas_call | solution.py:463
  45.6 0.0 all-to-all-done.1
  45.6 3.7 %group_and_device_local.1 = f32[128,128]{1,0:T(8,128)} custom-call(f32[256,128]{1,0:T(8,128)S(1)} %bitcast.9, f32[64,256]{1,0:T(8,128)S(1)} %device_to_device.1.peers_ref, f32[165,165]{1,0:T(8,128)S(1)} %get-tuple-element.19.down_ref, f32[176,128]{1,0:T(8,128)S(1)} %get-tuple-element.15.col_ref, f32[8,256]{1,0:T(8,128)S(1)} %get-tuple-element.16.row_ref), custom_call_target="tpu_custom_call" | custom-call | flops 1000 | bytes 1000 | tf_op jit(solution)/shard_map/group_and_device_local/pallas_call | solution.py:463
  49.3 5.1 %all-to-all-start.2 = ((f32[16,8,128]{2,1,0:T(8,128)}), f32[16,8,128]{2,1,0:T(8,128)S(1)}, u32[]{:S(2)}, u32[]{:S(2)}) async-start(f32[16,8,128]{2,1,0:T(8,128)} %bitcast.4), calls=%async_computation.2 | async-start | bytes 131072 | tf_op jit(solution)/shard_map/all_to_all | solution.py:526
  54.4 1.9 %evaluation_maps.1 = (bf16[2,176,512]{2,1,0:T(8,128)(2,1)S(1)}, bf16[2,176,512]{2,1,0:T(8,128)(2,1)S(1)}) custom-call(f32[72,512]{1,0:T(8,128)S(1)} %get-tuple-element.20.own_ref, f32[165,165]{1,0:T(8,128)S(1)} %get-tuple-element.19.down_ref, f32[176,128]{1,0:T(8,128)S(1)} %get-tuple-element.15.col_ref, f32[8,256]{1,0:T(8,128)S(1)} %get-tuple-element.16.row_ref), custom_call_target="tpu_custom_call" | custom-call | flops 1000 | bytes 1000 | tf_op jit(solution)/shard_map/evaluation_maps/pallas_call | solution.py:463
  56.3 0.0 collective-permute-done.left_ref
  56.4 0.0 collective-permute-done.1.right_ref
  56.4 0.0 copy-done.1
  56.4 2.0 %near_field.1.near_ref = f32[64,512]{1,0:T(8,128)S(1)} custom-call(s32[16,12]{1,0:T(8,128)S(1)} %copy-done.1, f32[72,512]{1,0:T(8,128)S(1)} %collective-permute-done.left_ref, f32[72,512]{1,0:T(8,128)S(1)} %get-tuple-element.20.own_ref, f32[72,512]{1,0:T(8,128)S(1)} %collective-permute-done.1.right_ref), custom_call_target="tpu_custom_call" | custom-call | flops 1000 | bytes 1000 | tf_op jit(solution)/shard_map/near_field/pallas_call | solution.py:463
  58.4 0.0 copy-done.2
  58.4 15.9 %far_field.1.base_ref = f32[64,512]{1,0:T(8,128)S(1)} custom-call(s32[16,12]{1,0:T(8,128)S(1)} %copy-done.2, f32[72,512]{1,0:T(8,128)S(1)} %collective-permute-done.left_ref, f32[72,512]{1,0:T(8,128)S(1)} %get-tuple-element.20.own_ref, f32[72,512]{1,0:T(8,128)S(1)} %collective-permute-done.1.right_ref, bf16[2,176,512]{2,1,0:T(8,128)(2,1)S(1)} %get-tuple-element.21.w_ref, ...), custom_call_target="tpu_custom_call" | custom-call | flops 1000 | bytes 1000 | tf_op jit(solution)/shard_map/far_field/pallas_call | solution.py:463
  74.3 0.0 all-to-all-done.2
  74.3 0.9 %potential.1 = f32[64,512]{1,0:T(8,128)} custom-call(f32[128,128]{1,0:T(8,128)S(1)} %bitcast.10, f32[64,512]{1,0:T(8,128)S(1)} %far_field.1.base_ref, bf16[2,176,512]{2,1,0:T(8,128)(2,1)S(1)} %get-tuple-element.22.m_ref), custom_call_target="tpu_custom_call" | custom-call | flops 1000 | bytes 1000 | tf_op jit(solution)/shard_map/potential/pallas_call | solution.py:463
Async XLA Ops:
  4.7 19.7 %all-to-all-start = ((f32[16,8,128]{2,1,0:T(8,128)}), f32[16,8,128]{2,1,0:T(8,128)S(1)}, u32[]{:S(2)}, u32[]{:S(2)}) async-start(f32[16,8,128]{2,1,0:T(8,128)} %bitcast), calls=%async_computation | async-start | bytes 131072 | tf_op jit(solution)/shard_map/all_to_all | solution.py:507
  18.2 38.2 %copy-start.1 = (s32[16,12]{1,0:T(8,128)S(1)}, s32[16,12]{1,0:T(8,128)}, u32[]{:S(2)}) copy-start(s32[16,12]{1,0:T(8,128)} %near_ref.1) | copy-start | bytes 2308
  18.2 40.2 %copy-start.2 = (s32[16,12]{1,0:T(8,128)S(1)}, s32[16,12]{1,0:T(8,128)}, u32[]{:S(2)}) copy-start(s32[16,12]{1,0:T(8,128)} %far_ref.1) | copy-start | bytes 2308
  25.1 0.7 copy-start
  25.7 19.9 %all-to-all-start.1 = ((f32[32,8,128]{2,1,0:T(8,128)}), f32[32,8,128]{2,1,0:T(8,128)S(1)}, u32[]{:S(2)}, u32[]{:S(2)}) async-start(f32[32,8,128]{2,1,0:T(8,128)} %bitcast.8), calls=%async_computation.1 | async-start | bytes 262144 | tf_op jit(solution)/shard_map/all_to_all | solution.py:516
  35.4 21.0 %collective-permute-start = (f32[72,512]{1,0:T(8,128)S(1)}, f32[72,512]{1,0:T(8,128)S(1)}, u32[]{:S(2)}, u32[]{:S(2)}) collective-permute-start(f32[72,512]{1,0:T(8,128)S(1)} %get-tuple-element.20.own_ref), channel_id=1, source_target_pairs={{0,1},{1,2},{2,3},{3,4},{4,5},{5,6},{6,7},{7,8},{8,9},{9,10},{10,1... | collective-permute-start | bytes 442376 | tf_op jit(solution)/shard_map/ppermute | solution.py:510
  37.9 18.4 %collective-permute-start.1 = (f32[72,512]{1,0:T(8,128)S(1)}, f32[72,512]{1,0:T(8,128)S(1)}, u32[]{:S(2)}, u32[]{:S(2)}) collective-permute-start(f32[72,512]{1,0:T(8,128)S(1)} %get-tuple-element.20.own_ref), channel_id=1, source_target_pairs={{1,0},{2,1},{3,2},{4,3},{5,4},{6,5},{7,6},{8,7},{9,8},{10,9},{11,1... | collective-permute-start | bytes 442376 | tf_op jit(solution)/shard_map/ppermute | solution.py:511
  49.3 25.0 %all-to-all-start.2 = ((f32[16,8,128]{2,1,0:T(8,128)}), f32[16,8,128]{2,1,0:T(8,128)S(1)}, u32[]{:S(2)}, u32[]{:S(2)}) async-start(f32[16,8,128]{2,1,0:T(8,128)} %bitcast.4), calls=%async_computation.2 | async-start | bytes 131072 | tf_op jit(solution)/shard_map/all_to_all | solution.py:526

commit v3 on v2

--- a/solution.py
+++ b/solution.py
@@ -124,14 +124,24 @@
 
 def leaf_equivalents(charges, kern, up):
     block = lax.broadcasted_iota(jnp.int32, (RHS, 256), 1) // SLOTS
+    keep = [(block == g).astype(F32).astype(BF) for g in range(8)]
+    pieces = split(charges)
     out = []
     for half in range(2):
         lanes = slice(half * 256, half * 256 + 256)
-        own = charges[:, lanes]
-        spread = split(jnp.concatenate([jnp.where(block == g, own, 0.0) for g in range(8)], axis=0))
+        spread = [jnp.concatenate([piece[:, lanes] * keep[g] for g in range(8)], axis=0) for piece in pieces]
         check = mm3(spread, (kern[0][:, lanes], kern[1][:, lanes]), dot_nt)
         out.append(mm3(split(check), up))
     return out
+
+
+def store_equivalents(halves, e_ref, first):
+    for half in range(2):
+        e_high, e_low = split(halves[half])
+        for g in range(8):
+            start = first + (half * 8 + g) * 2 * RHS
+            e_ref[start : start + RHS, :] = e_high[g * RHS : g * RHS + RHS]
+            e_ref[start + RHS : start + 2 * RHS, :] = e_low[g * RHS : g * RHS + RHS]
 
 
 def pack(rows):
@@ -173,8 +183,8 @@
 
 def head_kernel(
     off_hbm, q_hbm, counts_hbm, up_hbm, down_hbm, col_hbm, row_hbm,
-    out_ref, halo_ref, up_ref, down_ref, col_ref, row_ref,
-    off_ref, q_ref, counts_ref, pad_ref, tab_ref, sems,
+    out_ref, halo_ref, up_ref, down_ref, col_ref, row_ref, e_hbm,
+    off_ref, q_ref, counts_ref, pad_ref, tab_ref, e_ref, sems,
 ):
     moves = [
         pltpu.make_async_copy(src, dst, sems.at[n])
@@ -207,20 +217,24 @@
     up = padded(up_ref, pad_ref, 18.0 / TERMS)
     up = (up[0][:, :], up[1][:, :])
     halves = leaf_equivalents(charges, kern, up)
-    equiv = [split(h) for h in halves]
+    store_equivalents(halves, e_ref, 0)
+    e_move = pltpu.make_async_copy(e_ref, e_hbm, sems.at[7])
+    e_move.start()
     acc = jnp.zeros((RHS, LANE), F32)
     for (x, y, z), kern in box_kernels(
         (1.5, 0.5, -0.5, -1.5), (0.5, -0.5), (0.5, -0.5), 6.0, 0.9, col_ref, row_ref, tab_ref
     ):
-        half, g = (x >> 1), (x & 1) + 2 * y + 4 * z
-        rows = slice(g * RHS, g * RHS + RHS)
-        acc = acc + mm3((equiv[half][0][rows, :SUB], equiv[half][1][rows, :SUB]), split(kern))
+        start = ((x >> 1) * 8 + (x & 1) + 2 * y + 4 * z) * 2 * RHS
+        high, low = split(kern)
+        wide = dot(e_ref[start : start + 2 * RHS, :][:, :SUB], high)
+        acc = acc + wide[:RHS] + wide[RHS:] + dot(e_ref[start : start + RHS, :][:, :SUB], low)
     up60 = padded(up_ref, pad_ref, 60.0 / TERMS)
     out_ref[...] = pack(mm3(split(acc[:, :SUB]), up60))
     moves[-1].wait()
-
-
-def group_up_kernel(x_ref, maps_ref, up_ref, out_ref, pad_ref):
+    e_move.wait()
+
+
+def group_up_kernel(x_ref, maps_ref, up_ref, out_hbm, pad_ref, out_ref, sem):
     acc = (jnp.zeros((16, LANE), F32), jnp.zeros((16, LANE), F32))
     for e in range(INNER):
         acc = tile_dot(x_ref[8 * e : 8 * e + 8, :], maps_ref[e, 0], maps_ref[e, 1], acc)
@@ -231,6 +245,9 @@
     tile = jnp.where(top, equiv[:, :128], pltpu.roll(equiv[:, 128:], 4, 0))
     for p in range(OUTER):
         out_ref[8 * p : 8 * p + 8, :] = tile
+    move = pltpu.make_async_copy(out_ref, out_hbm, sem)
+    move.start()
+    move.wait()
 
 
 def box_order(rows):
@@ -260,27 +277,36 @@
     px, pz, py = row >> 5, (row >> 4) & 1, (row >> 2) & 3
     dest = (py & 1) + pz * 2 + px * 4 + (py >> 1) * 8
 
-    def step(turn, acc):
-        dx = turn // 3 - 1
-        dz = turn % 3 - 1
+    def valid(dx, dz):
         sx, sy, sz = px - dx, py - (lane - 3), pz - dz
         inside = (sx >= 0) & (sx < 2) & (sy >= 0) & (sy < 4) & (sz >= 0) & (sz < 2)
         source = (sy & 1) + sz * 2 + sx * 4 + (sy >> 1) * 8
-        mask = (inside & (jnp.abs(source - dest) >= 2)).astype(F32)
+        return (inside & (jnp.abs(source - dest) >= 2)).astype(F32)
+
+    def moved(dx, dy, dz, mask):
+        q = dy % 4
+        start = pl.multiple_of(RHS - (dx * 2 + dz) * 16 - 4 * (dy - q), 16)
+        keep = two(jnp.broadcast_to(mask[:, dy + 3 : dy + 4], (RHS, 128))).astype(BF)
+        rows = [(shifted_ref[q, n, pl.ds(start, RHS), :] * keep)[:, :SUB] for n in range(2)]
+        return rows
+
+    def both_ways(dx, dz, steps, acc):
         plane = square_of(0, dx.astype(F32) * 4.0, 3.0, 3.0, cols, row_ref)
-        plane = plane + square_of(2, dz.astype(F32) * 2.0, 3.0, 3.0, cols, row_ref)
-        tab_ref[7] = plane
-        for dy in range(-3, 4):
-            q = dy % 4
-            start = pl.multiple_of(RHS - (dx * 2 + dz) * 16 - 4 * (dy - q), 16)
-            keep = two(jnp.broadcast_to(mask[:, dy + 3 : dy + 4], (RHS, 128))).astype(BF)
-            high = shifted_ref[q, 0, pl.ds(start, RHS), :] * keep
-            low = shifted_ref[q, 1, pl.ds(start, RHS), :] * keep
+        tab_ref[7] = plane + square_of(2, dz.astype(F32) * 2.0, 3.0, 3.0, cols, row_ref)
+        ahead, behind = valid(dx, dz), valid(-dx, -dz)
+        forward, backward = acc
+        for dy in steps:
             kern = split(lax.rsqrt(tab_ref[7] + tab_ref[dy + 3]))
-            acc = acc + mm3((high[:, :SUB], low[:, :SUB]), kern)
-        return acc
-
-    out_ref[...] = index_order(lax.fori_loop(0, 9, step, jnp.zeros((RHS, LANE), F32)))
+            forward = forward + mm3(moved(dx, dy, dz, ahead), kern)
+            kern = (kern[0][:, :SUB], kern[1][:, :SUB])
+            backward = backward + mm3(moved(-dx, -dy, -dz, behind), kern, dot_nt)
+        return forward, backward
+
+    zero = jnp.int32(0)
+    acc = both_ways(zero, zero, (1, 2, 3), (jnp.zeros((RHS, LANE), F32), jnp.zeros((RHS, SUB), F32)))
+    acc = lax.fori_loop(5, 9, lambda n, acc: both_ways(n // 3 - 1, n % 3 - 1, range(-3, 4), acc), acc)
+    back = jnp.concatenate([acc[1], jnp.zeros((RHS, LANE - SUB), F32)], axis=1)
+    out_ref[...] = index_order(acc[0] + back)
 
 
 def local_kernel(x_ref, peers_ref, down_ref, col_ref, row_ref, out_ref, pad_ref, tab_ref):
@@ -316,23 +342,17 @@
     out_ref[...] = pack(mm3(split(total[:, :SUB]), padded(down_ref, pad_ref, 60.0 / TERMS)))
 
 
-def up_maps_kernel(flow_ref, col_ref, row_ref, out_ref, tab_ref):
-    for (x, y, z), kern in box_kernels(
-        (2.0, -2.0), (3.0, 1.0, -1.0, -3.0), (1.0, -1.0), 20.0, 3.0, col_ref, row_ref, tab_ref
-    ):
-        d = (y & 1) + z * 2 + x * 4 + (y >> 1) * 8
-        high, low = split(kern)
-        out_ref[d, 0, :, :] = high
-        out_ref[d, 1, :, :] = low
-
-
-def operator_kernel(own_ref, down_ref, col_ref, row_ref, w_ref, m_ref, pad_ref, tab_ref):
-    off = own_ref[RHS : RHS + 3, :]
+def operator_kernel(
+    flow_ref, off_ref, down_ref, col_ref, row_ref, up_ref, w_hbm, m_hbm, w_ref, m_ref, pad_ref, tab_ref, sems
+):
+    kern = split(leaf_kernel(off_ref[RHS : RHS + 3, :], col_ref))
     down = padded(down_ref, pad_ref, 18.0 / TERMS)
     down = (down[0][:, :SUB], down[1][:, :SUB])
-    weights = split(mm3(down, split(leaf_kernel(off, col_ref))))
+    weights = split(mm3(down, kern))
     w_ref[0, :, :] = weights[0]
     w_ref[1, :, :] = weights[1]
+    w_move = pltpu.make_async_copy(w_ref, w_hbm, sems.at[0])
+    w_move.start()
     block = lax.broadcasted_iota(jnp.int32, (SUB, 256), 1) // SLOTS
     found = [jnp.zeros((SUB, 256), F32)] * 2
     for (x, y, z), kern in box_kernels(
@@ -347,9 +367,20 @@
         m_high, m_low = split(found[half])
         m_ref[0, :, lanes] = m_high
         m_ref[1, :, lanes] = m_low
-
-
-def near_kernel(near_ref, left_ref, own_ref, right_ref, out_ref, mask_ref, high_ref, low_ref):
+    m_move = pltpu.make_async_copy(m_ref, m_hbm, sems.at[1])
+    m_move.start()
+    for (x, y, z), kern in box_kernels(
+        (2.0, -2.0), (3.0, 1.0, -1.0, -3.0), (1.0, -1.0), 20.0, 3.0, col_ref, row_ref, tab_ref
+    ):
+        e = (y & 1) + z * 2 + x * 4 + (y >> 1) * 8
+        high, low = split(kern)
+        up_ref[e, 0, :, :] = high
+        up_ref[e, 1, :, :] = low
+    w_move.wait()
+    m_move.wait()
+
+
+def near_field(near_ref, left_ref, own_ref, right_ref, out_ref, mask_ref, high_ref, low_ref):
     offs = jnp.concatenate([own_ref[RHS:ROWS, :], jnp.zeros((120, POINTS), F32)], axis=0).T
     inner = lax.axis_index("inner")
     device = lax.axis_index("outer") * INNER + inner
@@ -390,19 +421,30 @@
     out_ref[...] = flipped[:RHS] + flipped[RHS:]
 
 
-def far_kernel(far_ref, left_ref, own_ref, right_ref, w_ref, up_ref, near_ref, col_ref, row_ref, out_ref, pad_ref, e_ref, dl_ref, xtab_ref, tab_ref):
+def field_kernel(
+    far_ref, near_ref, own_ref, swap_ref, cross_ref, up_ref, col_ref, row_ref, w_hbm, m_hbm, e_hbm, out_ref, m_ref,
+    pad_ref, e_ref, dl_ref, xtab_ref, tab_ref, w_ref, left_ref, right_ref, mask_ref, high_ref, low_ref, sems,
+):
+    middle = LEAVES * 2 * RHS
+    moves = [
+        pltpu.make_async_copy(e_hbm, e_ref.at[middle : 2 * middle], sems.at[0]),
+        pltpu.make_async_copy(w_hbm, w_ref, sems.at[1]),
+        pltpu.make_async_copy(m_hbm, m_ref, sems.at[2]),
+    ]
+    for move in moves:
+        move.start()
+    odd = lax.rem(lax.axis_index("inner"), 2) == 1
+    left_ref[...] = jnp.where(odd, swap_ref[...], cross_ref[...])
+    right_ref[...] = jnp.where(odd, cross_ref[...], swap_ref[...])
+    near_field(near_ref, left_ref, own_ref, right_ref, out_ref, mask_ref, high_ref, low_ref)
     inner = lax.axis_index("inner")
     device = lax.axis_index("outer") * INNER + inner
     up = padded(up_ref, pad_ref, 18.0 / TERMS)
-    for side, ref in enumerate((left_ref, own_ref, right_ref)):
+    for side, ref in ((0, left_ref), (2, right_ref)):
         kern = split(leaf_kernel(ref[RHS : RHS + 3, :], col_ref))
-        halves = leaf_equivalents(ref[0:RHS, :], kern, up)
-        for half in range(2):
-            e_high, e_low = split(halves[half])
-            for g in range(8):
-                start = ((side * 2 + half) * 8 + g) * 2 * RHS
-                e_ref[start : start + RHS, :] = e_high[g * RHS : g * RHS + RHS]
-                e_ref[start + RHS : start + 2 * RHS, :] = e_low[g * RHS : g * RHS + RHS]
+        store_equivalents(leaf_equivalents(ref[0:RHS, :], kern, up), e_ref, side * middle)
+    for move in moves:
+        move.wait()
     first = (device - 1) * LEAVES
     boxes = [corner((device + side) * LEAVES, 4) for side in (-1, 0, 1)]
     boxes = [[(boxes[1][c] - box[c]).astype(F32) for c in range(3)] for box in boxes]
@@ -444,7 +486,7 @@
         rows = slice(half * 8 * RHS, (half + 1) * 8 * RHS)
         local = (dl_ref[0, rows, :][:, :SUB], dl_ref[1, rows, :][:, :SUB])
         res = mm3(local, (w_ref[0, :, lanes], w_ref[1, :, lanes]))
-        acc = near_ref[:, lanes]
+        acc = out_ref[:, lanes]
         for g in range(8):
             acc = acc + jnp.where(block == g, res[g * RHS : (g + 1) * RHS], 0.0)
         out_ref[:, lanes] = acc
@@ -457,19 +499,24 @@
 
 VM = pl.BlockSpec(memory_space=pltpu.VMEM)
 SM = pl.BlockSpec(memory_space=pltpu.SMEM)
-
-
-def call(kernel, name, outs, specs, scratch, vmem, *args):
+HB = pl.BlockSpec(memory_space=pltpu.HBM)
+
+
+def call(kernel, name, outs, specs, scratch, vmem, *args, out_specs=None):
     return pl.pallas_call(
         kernel,
         name=name,
         out_shape=outs,
         in_specs=specs,
-        out_specs=jax.tree.map(lambda _: VM, outs),
+        out_specs=out_specs or jax.tree.map(lambda _: VM, outs),
         scratch_shapes=scratch,
         compiler_params=pltpu.CompilerParams(vmem_limit_bytes=vmem * 1024 * 1024),
         cost_estimate=pl.CostEstimate(flops=1000, bytes_accessed=1000, transcendentals=0),
     )(*args)
+
+
+def in_hbm(x):
+    return pltpu.with_memory_space_constraint(x, pltpu.HBM)
 
 
 def tie(value, *others):
@@ -486,32 +533,37 @@
     def tables(n):
         return pltpu.VMEM((n, SUB, LANE), F32)
 
-    def maps(n):
-        return sds((n, 2, SUB, LANE), BF)
-
     inputs = (offsets, charges, counts, upward, downward, jnp.asarray(col_np), jnp.asarray(row_np))
-    dev_equiv, own, upward, downward, col, row = call(
+    equiv_rows = LEAVES * 2 * RHS
+    dev_equiv, own, upward, downward, col, row, equiv = call(
         head_kernel, "leaf_and_device_equiv",
-        (flow, sds((ROWS, POINTS), F32), square, square, sds((SUB, 128), F32), sds((8, LANE), F32)),
-        [pl.BlockSpec(memory_space=pltpu.HBM)] * 7,
+        (flow, sds((ROWS, POINTS), F32), square, square, sds((SUB, 128), F32), sds((8, LANE), F32), pltpu.HBM((equiv_rows, LANE), BF)),
+        [HB] * 7,
         [
             pltpu.VMEM((3, POINTS), F32),
             pltpu.VMEM((RHS, POINTS), F32),
             pltpu.SMEM((LEAVES,), jnp.int32),
             pad,
             tables(10),
-            pltpu.SemaphoreType.DMA((7,)),
+            pltpu.VMEM((equiv_rows, LANE), BF),
+            pltpu.SemaphoreType.DMA((8,)),
         ],
-        16, *(pltpu.with_memory_space_constraint(a, pltpu.HBM) for a in inputs),
+        16, *map(in_hbm, inputs), out_specs=(VM, VM, VM, VM, VM, VM, HB),
     )
     peers_equiv = lax.all_to_all(dev_equiv, "inner", 0, 0, tiled=True)
-    up_maps = call(up_maps_kernel, "up_maps", maps(INNER), [VM, VM, VM], [tables(14)], 12, dev_equiv, col, row)
-    ends = INNER - 1
-    left = lax.ppermute(own, "inner", [(i, i + 1) for i in range(ends)])
-    right = lax.ppermute(own, "inner", [(i + 1, i) for i in range(ends)])
+    leaf_maps = pltpu.HBM((2, SUB, POINTS), BF)
+    up_maps, weights, evaluate = call(
+        operator_kernel, "evaluation_and_group_maps", (sds((INNER, 2, SUB, LANE), BF), leaf_maps, leaf_maps),
+        [VM, VM, VM, VM, VM],
+        [pltpu.VMEM((2, SUB, POINTS), BF), pltpu.VMEM((2, SUB, POINTS), BF), pad, tables(14), pltpu.SemaphoreType.DMA((2,))],
+        14, dev_equiv, own, downward, col, row, out_specs=(VM, HB, HB),
+    )
+    swap = lax.ppermute(own, "inner", [(i, i ^ 1) for i in range(INNER)])
+    cross = lax.ppermute(own, "inner", [(i, ((i + 1) ^ 1) - 1) for i in range(1, INNER - 1)])
     group_equiv = call(
-        group_up_kernel, "group_equiv", sds((8 * OUTER, 128), F32), [VM, VM, VM], [pad], 6,
-        peers_equiv, up_maps, upward,
+        group_up_kernel, "group_equiv", pltpu.HBM((8 * OUTER, 128), F32), [VM, VM, VM],
+        [pad, pltpu.VMEM((8 * OUTER, 128), F32), pltpu.SemaphoreType.DMA], 6,
+        peers_equiv, up_maps, upward, out_specs=HB,
     )
     groups = lax.all_to_all(group_equiv, "outer", 0, 0, tiled=True)
     peers_part = call(
@@ -524,25 +576,24 @@
         groups, peers_part, downward, col, row,
     )
     dev_local = lax.all_to_all(local, "inner", 0, 0, tiled=True)
-    weights, evaluate = call(
-        operator_kernel, "evaluation_maps", (sds((2, SUB, POINTS), BF), sds((2, SUB, POINTS), BF)),
-        [VM, VM, VM, VM], [pad, tables(10)], 12, own, downward, col, row,
-    )
-    near_part = call(
-        near_kernel, "near_field", sds((RHS, POINTS), F32), [VM, VM, VM, VM],
-        [pltpu.VMEM((LEAVES, 3 * POINTS), F32), pltpu.VMEM((POINTS, 3 * POINTS), BF), pltpu.VMEM((POINTS, 3 * POINTS), BF)],
-        14, near, left, own, right,
-    )
-    base = call(
-        far_kernel, "far_field", sds((RHS, POINTS), F32), [SM, VM, VM, VM, VM, VM, VM, VM, VM],
+    base, evaluate = call(
+        field_kernel, "near_and_far_field", (sds((RHS, POINTS), F32), sds((2, SUB, POINTS), BF)),
+        [SM, VM, VM, VM, VM, VM, VM, VM, HB, HB, HB],
         [
             pad,
             pltpu.VMEM((3 * LEAVES * 2 * RHS, LANE), BF),
             pltpu.VMEM((2, LEAVES * RHS, LANE), BF),
             tables(21),
             tables(30),
+            pltpu.VMEM((2, SUB, POINTS), BF),
+            pltpu.VMEM((ROWS, POINTS), F32),
+            pltpu.VMEM((ROWS, POINTS), F32),
+            pltpu.VMEM((LEAVES, 3 * POINTS), F32),
+            pltpu.VMEM((POINTS, 3 * POINTS), BF),
+            pltpu.VMEM((POINTS, 3 * POINTS), BF),
+            pltpu.SemaphoreType.DMA((3,)),
         ],
-        24, far, left, own, right, weights, upward, near_part, col, row,
+        32, far, near, own, swap, cross, upward, col, row, in_hbm(weights), in_hbm(evaluate), in_hbm(equiv),
     )
     return call(tail_kernel, "potential", sds((RHS, POINTS), F32), [VM, VM, VM], [], 4, dev_local, base, evaluate)
 

time: 75.6 us -> 71.8 us (0.950)
  waiting for transfers between devices: 6.13 us -> 3.55 us
    all_to_all x1, waiting for transfers between devices: 6.12 us -> 3.54 us  [shards(): peers_equiv = lax.all_to_all(dev_equiv, 'inner', 0, 0, tiled=True)]
    pallas_call x9 -> x7, Pallas kernels: 37.2 us -> 36.8 us  [call(): pl.pallas_call(kernel, name=name, out_shape=outs, in_specs=specs, out_spe...]
  transfers between devices with their start and end apart: 5 -> 5, of which waited for: 1 -> 1; matrix products, arithmetic and copies ran while one was open for 0% -> 0% of each run, Pallas kernels for 41% -> 42%
where the time goes in v3:
time: 71.8 us; the launch traced here: 71.4 us
  Pallas kernels  36.8 us (51%)
  starting transfers between devices  30.9 us (43%)
  waiting for transfers between devices  3.55 us (5%)
    pallas_call x7, Pallas kernels, call(): pl.pallas_call(kernel, name=name, out_shape=outs, in_specs=specs, out_spe...  36.8 us
    all_to_all x1, starting transfers between devices, shards(): peers_equiv = lax.all_to_all(dev_equiv, 'inner', 0, 0, tiled=True)  11.8 us
    all_to_all x1, starting transfers between devices, shards(): groups = lax.all_to_all(group_equiv, 'outer', 0, 0, tiled=True)  9.68 us
    all_to_all x1, starting transfers between devices, shards(): dev_local = lax.all_to_all(local, 'inner', 0, 0, tiled=True)  4.93 us
    all_to_all x1, waiting for transfers between devices, shards(): peers_equiv = lax.all_to_all(dev_equiv, 'inner', 0, 0, tiled=True)  3.54 us
    ppermute x1, starting transfers between devices, shards(): swap = lax.ppermute(own, 'inner', [(i, i ^ 1) for i in range(INNER)])  2.35 us
    ppermute x1, starting transfers between devices, shards(): lax.ppermute(own, 'inner', [(i, (i + 1 ^ 1) - 1) for i in range(1, INNER...  2.11 us
  transfers between devices with their start and end apart: 5, of which 1 were waited for; matrix products, arithmetic and copies ran while one was open for 0% of the time, Pallas kernels for 42%

profile of v3, /device:TPU:1, one launch (start us, length us, event | category | flops | bytes accessed | tf_op | source)
XLA Modules:
  0.0 71.4 jit_solution(5022833902783373034)
XLA Ops:
  0.0 0.0 copy-start
  0.0 0.0 copy-start.1
  0.0 4.4 %leaf_and_device_equiv.1 = (f32[128,128]{1,0:T(8,128)}, f32[72,512]{1,0:T(8,128)S(1)}, f32[165,165]{1,0:T(8,128)S(1)}, f32[165,165]{1,0:T(8,128)S(1)}, f32[176,1...) custom-call(f32[3,512]{1,0:T(4,128)} %off_hbm.1, f32[64,512]{1,0:T(8,128)} %q_hbm.1, s32[16]{0:T(128)} %counts_hbm.1, ...), custom_call_target="tpu_custom_call" | custom-call | flops 1000 | bytes 1000 | tf_op jit(solution)/shard_map/leaf_and_device_equiv/pallas_call | solution.py:506
  4.4 11.8 %all-to-all-start = ((f32[16,8,128]{2,1,0:T(8,128)}), f32[16,8,128]{2,1,0:T(8,128)S(1)}, u32[]{:S(2)}, u32[]{:S(2)}) async-start(f32[16,8,128]{2,1,0:T(8,128)} %bitcast), calls=%async_computation | async-start | bytes 131072 | tf_op jit(solution)/shard_map/all_to_all | solution.py:553
  16.3 4.3 %evaluation_and_group_maps.1 = (bf16[16,2,176,256]{3,2,1,0:T(8,128)(2,1)S(1)}, bf16[2,176,512]{2,1,0:T(8,128)(2,1)}, bf16[2,176,512]{2,1,0:T(8,128)(2,1)}) custom-call(f32[128,128]{1,0:T(8,128)} %get-tuple-element.18.flow_ref, f32[72,512]{1,0:T(8,128)S(1)} %get-tuple-element.19.off_ref.own_ref, f32[165,165]{1,0:T(8,128)S(1)} %get-tuple-element.20.down_ref, ...), custom_call_target="tpu_custom_call" | custom-call | flops 1000 | bytes 1000 | tf_op jit(solution)/shard_map/evaluation_and_group_maps/pallas_call | solution.py:506
  20.5 3.5 %all-to-all-done = f32[16,8,128]{2,1,0:T(8,128)S(1)} async-done(((f32[16,8,128]{2,1,0:T(8,128)}), f32[16,8,128]{2,1,0:T(8,128)S(1)}, u32[]{:S(2)}, u32[]{:S(2)}) %all-to-all-start) | async-done | bytes 65568 | tf_op jit(solution)/shard_map/all_to_all | solution.py:553
  24.1 1.4 %group_equiv.1 = f32[256,128]{1,0:T(8,128)} custom-call(f32[128,128]{1,0:T(8,128)S(1)} %bitcast.6, bf16[16,2,176,256]{3,2,1,0:T(8,128)(2,1)S(1)} %get-tuple-element.23.maps_ref, f32[165,165]{1,0:T(8,128)S(1)} %get-tuple-element.24.up_ref), custom_call_target="tpu_custom_call" | custom-call | flops 1000 | bytes 1000 | tf_op jit(solution)/shard_map/group_equiv/pallas_call | solution.py:506
  25.4 9.7 %all-to-all-start.1 = ((f32[32,8,128]{2,1,0:T(8,128)}), f32[32,8,128]{2,1,0:T(8,128)S(1)}, u32[]{:S(2)}, u32[]{:S(2)}) async-start(f32[32,8,128]{2,1,0:T(8,128)} %bitcast.10), calls=%async_computation.1 | async-start | bytes 262144 | tf_op jit(solution)/shard_map/all_to_all | solution.py:568
  35.1 2.4 %collective-permute-start = (f32[72,512]{1,0:T(8,128)S(1)}, f32[72,512]{1,0:T(8,128)S(1)}, u32[]{:S(2)}, u32[]{:S(2)}) collective-permute-start(f32[72,512]{1,0:T(8,128)S(1)} %get-tuple-element.19.off_ref.own_ref), channel_id=1, source_target_pairs={{0,1},{1,0},{2,3},{3,2},{4,5},{5,4},{6,7},{7,6},{8,9},{9,8},{10,11... | collective-permute-start | bytes 442376 | tf_op jit(solution)/shard_map/ppermute | solution.py:561
  37.5 2.1 %collective-permute-start.1 = (f32[72,512]{1,0:T(8,128)S(1)}, f32[72,512]{1,0:T(8,128)S(1)}, u32[]{:S(2)}, u32[]{:S(2)}) collective-permute-start(f32[72,512]{1,0:T(8,128)S(1)} %get-tuple-element.19.off_ref.own_ref), channel_id=1, source_target_pairs={{1,2},{2,1},{3,4},{4,3},{5,6},{6,5},{7,8},{8,7},{9,10},{10,9},{11,... | collective-permute-start | bytes 442376 | tf_op jit(solution)/shard_map/ppermute | solution.py:562
  39.6 5.2 %device_to_device.1.peers_ref = f32[64,256]{1,0:T(8,128)S(1)} custom-call(f32[128,128]{1,0:T(8,128)S(1)} %bitcast.7, f32[176,128]{1,0:T(8,128)S(1)} %get-tuple-element.21.col_ref, f32[8,256]{1,0:T(8,128)S(1)} %get-tuple-element.22.row_ref), custom_call_target="tpu_custom_call" | custom-call | flops 1000 | bytes 1000 | tf_op jit(solution)/shard_map/device_to_device/pallas_call | solution.py:506
  44.8 0.0 all-to-all-done.1
  44.8 3.7 %group_and_device_local.1 = f32[128,128]{1,0:T(8,128)} custom-call(f32[256,128]{1,0:T(8,128)S(1)} %bitcast.8, f32[64,256]{1,0:T(8,128)S(1)} %device_to_device.1.peers_ref, f32[165,165]{1,0:T(8,128)S(1)} %get-tuple-element.20.down_ref, f32[176,128]{1,0:T(8,128)S(1)} %get-tuple-element.21.col_ref, f32[8,256]{1,0:T(8,128)S(1)} %get-tuple-element.22.row_ref), custom_call_target="tpu_custom_call" | custom-call | flops 1000 | bytes 1000 | tf_op jit(solution)/shard_map/group_and_device_local/pallas_call | solution.py:506
  48.5 4.9 %all-to-all-start.2 = ((f32[16,8,128]{2,1,0:T(8,128)}), f32[16,8,128]{2,1,0:T(8,128)S(1)}, u32[]{:S(2)}, u32[]{:S(2)}) async-start(f32[16,8,128]{2,1,0:T(8,128)} %bitcast.4), calls=%async_computation.2 | async-start | bytes 131072 | tf_op jit(solution)/shard_map/all_to_all | solution.py:578
  53.4 0.0 collective-permute-done.swap_ref
  53.4 0.0 collective-permute-done.1.cross_ref
  53.4 0.0 copy-done
  53.5 0.0 copy-done.1
  53.5 17.0 %near_and_far_field.1 = (f32[64,512]{1,0:T(8,128)S(1)}, bf16[2,176,512]{2,1,0:T(8,128)(2,1)S(1)}) custom-call(s32[16,12]{1,0:T(8,128)S(1)} %copy-done, s32[16,12]{1,0:T(8,128)S(1)} %copy-done.1, f32[72,512]{1,0:T(8,128)S(1)} %get-tuple-element.19.off_ref.own_ref, f32[72,512]{1,0:T(8,128)S(1)} %collective-permute-done.swap_ref, ...), custom_call_target="tpu_custom_call" | custom-call | flops 1000 | bytes 1000 | tf_op jit(solution)/shard_map/near_and_far_field/pallas_call | solution.py:506
  70.5 0.0 all-to-all-done.2
  70.5 0.9 %potential.1 = f32[64,512]{1,0:T(8,128)} custom-call(f32[128,128]{1,0:T(8,128)S(1)} %bitcast.9, f32[64,512]{1,0:T(8,128)S(1)} %get-tuple-element.29.base_ref, bf16[2,176,512]{2,1,0:T(8,128)(2,1)S(1)} %get-tuple-element.30.m_ref), custom_call_target="tpu_custom_call" | custom-call | flops 1000 | bytes 1000 | tf_op jit(solution)/shard_map/potential/pallas_call | solution.py:506
Async XLA Ops:
  0.0 53.4 %copy-start = (s32[16,12]{1,0:T(8,128)S(1)}, s32[16,12]{1,0:T(8,128)}, u32[]{:S(2)}) copy-start(s32[16,12]{1,0:T(8,128)} %far_ref.1) | copy-start | bytes 2308
  0.0 53.5 %copy-start.1 = (s32[16,12]{1,0:T(8,128)S(1)}, s32[16,12]{1,0:T(8,128)}, u32[]{:S(2)}) copy-start(s32[16,12]{1,0:T(8,128)} %near_ref.1) | copy-start | bytes 2308
  4.4 19.7 %all-to-all-start = ((f32[16,8,128]{2,1,0:T(8,128)}), f32[16,8,128]{2,1,0:T(8,128)S(1)}, u32[]{:S(2)}, u32[]{:S(2)}) async-start(f32[16,8,128]{2,1,0:T(8,128)} %bitcast), calls=%async_computation | async-start | bytes 131072 | tf_op jit(solution)/shard_map/all_to_all | solution.py:553
  25.4 19.3 %all-to-all-start.1 = ((f32[32,8,128]{2,1,0:T(8,128)}), f32[32,8,128]{2,1,0:T(8,128)S(1)}, u32[]{:S(2)}, u32[]{:S(2)}) async-start(f32[32,8,128]{2,1,0:T(8,128)} %bitcast.10), calls=%async_computation.1 | async-start | bytes 262144 | tf_op jit(solution)/shard_map/all_to_all | solution.py:568
  35.1 18.3 %collective-permute-start = (f32[72,512]{1,0:T(8,128)S(1)}, f32[72,512]{1,0:T(8,128)S(1)}, u32[]{:S(2)}, u32[]{:S(2)}) collective-permute-start(f32[72,512]{1,0:T(8,128)S(1)} %get-tuple-element.19.off_ref.own_ref), channel_id=1, source_target_pairs={{0,1},{1,0},{2,3},{3,2},{4,5},{5,4},{6,7},{7,6},{8,9},{9,8},{10,11... | collective-permute-start | bytes 442376 | tf_op jit(solution)/shard_map/ppermute | solution.py:561
  37.5 15.9 %collective-permute-start.1 = (f32[72,512]{1,0:T(8,128)S(1)}, f32[72,512]{1,0:T(8,128)S(1)}, u32[]{:S(2)}, u32[]{:S(2)}) collective-permute-start(f32[72,512]{1,0:T(8,128)S(1)} %get-tuple-element.19.off_ref.own_ref), channel_id=1, source_target_pairs={{1,2},{2,1},{3,4},{4,3},{5,6},{6,5},{7,8},{8,7},{9,10},{10,9},{11,... | collective-permute-start | bytes 442376 | tf_op jit(solution)/shard_map/ppermute | solution.py:562
  48.5 22.0 %all-to-all-start.2 = ((f32[16,8,128]{2,1,0:T(8,128)}), f32[16,8,128]{2,1,0:T(8,128)S(1)}, u32[]{:S(2)}, u32[]{:S(2)}) async-start(f32[16,8,128]{2,1,0:T(8,128)} %bitcast.4), calls=%async_computation.2 | async-start | bytes 131072 | tf_op jit(solution)/shard_map/all_to_all | solution.py:578

commit v4 on v3

--- a/solution.py
+++ b/solution.py
@@ -285,31 +285,29 @@
 
     def moved(dx, dy, dz, mask):
         q = dy % 4
-        start = pl.multiple_of(RHS - (dx * 2 + dz) * 16 - 4 * (dy - q), 16)
+        start = RHS - (dx * 2 + dz) * 16 - 4 * (dy - q)
         keep = two(jnp.broadcast_to(mask[:, dy + 3 : dy + 4], (RHS, 128))).astype(BF)
-        rows = [(shifted_ref[q, n, pl.ds(start, RHS), :] * keep)[:, :SUB] for n in range(2)]
+        rows = [(shifted_ref[q, n, start : start + RHS, :] * keep)[:, :SUB] for n in range(2)]
         return rows
 
-    def both_ways(dx, dz, steps, acc):
-        plane = square_of(0, dx.astype(F32) * 4.0, 3.0, 3.0, cols, row_ref)
-        tab_ref[7] = plane + square_of(2, dz.astype(F32) * 2.0, 3.0, 3.0, cols, row_ref)
+    acc = (jnp.zeros((RHS, LANE), F32), jnp.zeros((RHS, SUB), F32))
+    planes = [(0, 0, (1, 2, 3))] + [(dx, dz, range(-3, 4)) for dx, dz in ((0, 1), (1, -1), (1, 0), (1, 1))]
+    for n, (dx, dz, steps) in enumerate(planes):
+        plane = square_of(0, dx * 4.0, 3.0, 3.0, cols, row_ref)
+        tab_ref[7 + n] = plane + square_of(2, dz * 2.0, 3.0, 3.0, cols, row_ref)
         ahead, behind = valid(dx, dz), valid(-dx, -dz)
-        forward, backward = acc
         for dy in steps:
-            kern = split(lax.rsqrt(tab_ref[7] + tab_ref[dy + 3]))
-            forward = forward + mm3(moved(dx, dy, dz, ahead), kern)
+            kern = split(lax.rsqrt(tab_ref[7 + n] + tab_ref[dy + 3]))
+            forward = acc[0] + mm3(moved(dx, dy, dz, ahead), kern)
             kern = (kern[0][:, :SUB], kern[1][:, :SUB])
-            backward = backward + mm3(moved(-dx, -dy, -dz, behind), kern, dot_nt)
-        return forward, backward
-
-    zero = jnp.int32(0)
-    acc = both_ways(zero, zero, (1, 2, 3), (jnp.zeros((RHS, LANE), F32), jnp.zeros((RHS, SUB), F32)))
-    acc = lax.fori_loop(5, 9, lambda n, acc: both_ways(n // 3 - 1, n % 3 - 1, range(-3, 4), acc), acc)
+            acc = (forward, acc[1] + mm3(moved(-dx, -dy, -dz, behind), kern, dot_nt))
     back = jnp.concatenate([acc[1], jnp.zeros((RHS, LANE - SUB), F32)], axis=1)
     out_ref[...] = index_order(acc[0] + back)
 
 
-def local_kernel(x_ref, peers_ref, down_ref, col_ref, row_ref, out_ref, pad_ref, tab_ref):
+def local_kernel(x_ref, peers_ref, down_ref, col_ref, row_ref, up_hbm, out_ref, pad_ref, tab_ref, up_ref, sem):
+    move = pltpu.make_async_copy(up_hbm, up_ref, sem)
+    move.start()
     outer = lax.axis_index("outer")
     own = [p.astype(F32) for p in corner(outer * 256, 8)]
     cols = columns(col_ref)
@@ -329,22 +327,29 @@
     both = jnp.concatenate([check, check], axis=0)
     group = mm3(split(both[:, :SUB]), padded(down_ref, pad_ref, 200.0 / TERMS))[:8]
     pieces = jnp.concatenate(split(group[:, :SUB]), axis=0)
-    top = lax.broadcasted_iota(jnp.int32, (8, LANE), 0) < 4
-    found = [None] * INNER
+    top = lax.broadcasted_iota(jnp.int32, (8, SUB), 0) < 4
+    move.wait()
+    found = []
+    for d in range(INNER):
+        part = dot_nt(pieces, up_ref[d, 0][:, :SUB]) + dot_nt(pieces, up_ref[d, 1][:, :SUB])
+        found.append(part[:8] + part[8:])
+    merged = [jnp.where(top, found[2 * m], pltpu.roll(found[2 * m + 1], 4, 0)) for m in range(INNER // 2)]
+    total = jnp.concatenate(merged, axis=0) + peers_ref[:, :SUB]
+    out_ref[...] = pack(mm3(split(total), padded(down_ref, pad_ref, 60.0 / TERMS)))
+
+
+def operator_kernel(
+    flow_ref, off_ref, down_ref, col_ref, row_ref, up_ref, w_hbm, m_hbm, up_hbm, w_ref, m_ref, pad_ref, tab_ref, sems
+):
     for (x, y, z), kern in box_kernels(
-        (-2.0, 2.0), (-3.0, -1.0, 1.0, 3.0), (-1.0, 1.0), 3.0, 20.0, col_ref, row_ref, tab_ref
+        (2.0, -2.0), (3.0, 1.0, -1.0, -3.0), (1.0, -1.0), 20.0, 3.0, col_ref, row_ref, tab_ref
     ):
+        e = (y & 1) + z * 2 + x * 4 + (y >> 1) * 8
         high, low = split(kern)
-        part = dot(pieces, high) + dot(pieces, low)
-        found[(y & 1) + z * 2 + x * 4 + (y >> 1) * 8] = part[:8] + part[8:]
-    merged = [jnp.where(top, found[2 * m], pltpu.roll(found[2 * m + 1], 4, 0)) for m in range(INNER // 2)]
-    total = jnp.concatenate(merged, axis=0) + peers_ref[...]
-    out_ref[...] = pack(mm3(split(total[:, :SUB]), padded(down_ref, pad_ref, 60.0 / TERMS)))
-
-
-def operator_kernel(
-    flow_ref, off_ref, down_ref, col_ref, row_ref, up_ref, w_hbm, m_hbm, w_ref, m_ref, pad_ref, tab_ref, sems
-):
+        up_ref[e, 0, :, :] = high
+        up_ref[e, 1, :, :] = low
+    up_move = pltpu.make_async_copy(up_ref, up_hbm, sems.at[2])
+    up_move.start()
     kern = split(leaf_kernel(off_ref[RHS : RHS + 3, :], col_ref))
     down = padded(down_ref, pad_ref, 18.0 / TERMS)
     down = (down[0][:, :SUB], down[1][:, :SUB])
@@ -369,13 +374,7 @@
         m_ref[1, :, lanes] = m_low
     m_move = pltpu.make_async_copy(m_ref, m_hbm, sems.at[1])
     m_move.start()
-    for (x, y, z), kern in box_kernels(
-        (2.0, -2.0), (3.0, 1.0, -1.0, -3.0), (1.0, -1.0), 20.0, 3.0, col_ref, row_ref, tab_ref
-    ):
-        e = (y & 1) + z * 2 + x * 4 + (y >> 1) * 8
-        high, low = split(kern)
-        up_ref[e, 0, :, :] = high
-        up_ref[e, 1, :, :] = low
+    up_move.wait()
     w_move.wait()
     m_move.wait()
 
@@ -461,18 +460,25 @@
 
     def one_leaf(g, carry):
         own = local_leaf(g)
-        acc = jnp.zeros((RHS, LANE), F32)
-        for k in range(12):
-            window = far_ref[g, k] - first
-            side = window >> 4
-            place = local_leaf(window & 15)
-            x = side * 7 + 3 + own[0] - place[0]
-            yz = side * 9 + 4 + (own[1] - place[1]) * 3 + own[2] - place[2]
-            k_high, k_low = split(lax.rsqrt(xtab_ref[x] + tab_ref[yz]))
-            start = pl.multiple_of(window * (2 * RHS), 2 * RHS)
-            equiv = e_ref[pl.ds(start, 2 * RHS), :][:, :SUB]
-            wide = dot(equiv, k_high)
-            acc = acc + wide[:RHS] + wide[RHS:] + dot(equiv[:RHS], k_low)
+        wide = jnp.zeros((2 * RHS, LANE), F32)
+        narrow = jnp.zeros((RHS, LANE), F32)
+        rest = jnp.zeros((LANE - SUB, LANE), BF)
+        for k in range(0, 12, 4):
+            tops, lows, equivs = [], [], []
+            for n in range(k, k + 4):
+                window = far_ref[g, n] - first
+                side = window >> 4
+                place = local_leaf(window & 15)
+                x = side * 7 + 3 + own[0] - place[0]
+                yz = side * 9 + 4 + (own[1] - place[1]) * 3 + own[2] - place[2]
+                k_high, k_low = split(lax.rsqrt(xtab_ref[x] + tab_ref[yz]))
+                tops += [k_high, rest]
+                lows += [k_low, rest]
+                equivs.append(e_ref[pl.ds(pl.multiple_of(window * (2 * RHS), 2 * RHS), 2 * RHS), :])
+            equiv = jnp.concatenate(equivs, axis=1)
+            wide = wide + dot(equiv, jnp.concatenate(tops, axis=0))
+            narrow = narrow + dot(equiv[:RHS], jnp.concatenate(lows, axis=0))
+        acc = wide[:RHS] + wide[RHS:] + narrow
         high, low = split(acc)
         start = pl.multiple_of(g * RHS, RHS)
         dl_ref[0, pl.ds(start, RHS), :] = high
@@ -552,11 +558,12 @@
     )
     peers_equiv = lax.all_to_all(dev_equiv, "inner", 0, 0, tiled=True)
     leaf_maps = pltpu.HBM((2, SUB, POINTS), BF)
-    up_maps, weights, evaluate = call(
-        operator_kernel, "evaluation_and_group_maps", (sds((INNER, 2, SUB, LANE), BF), leaf_maps, leaf_maps),
+    up_shape = (INNER, 2, SUB, LANE)
+    up_maps, weights, evaluate, up_copy = call(
+        operator_kernel, "evaluation_and_group_maps", (sds(up_shape, BF), leaf_maps, leaf_maps, pltpu.HBM(up_shape, BF)),
         [VM, VM, VM, VM, VM],
-        [pltpu.VMEM((2, SUB, POINTS), BF), pltpu.VMEM((2, SUB, POINTS), BF), pad, tables(14), pltpu.SemaphoreType.DMA((2,))],
-        14, dev_equiv, own, downward, col, row, out_specs=(VM, HB, HB),
+        [pltpu.VMEM((2, SUB, POINTS), BF), pltpu.VMEM((2, SUB, POINTS), BF), pad, tables(14), pltpu.SemaphoreType.DMA((3,))],
+        14, dev_equiv, own, downward, col, row, out_specs=(VM, HB, HB, HB),
     )
     swap = lax.ppermute(own, "inner", [(i, i ^ 1) for i in range(INNER)])
     cross = lax.ppermute(own, "inner", [(i, ((i + 1) ^ 1) - 1) for i in range(1, INNER - 1)])
@@ -568,12 +575,13 @@
     groups = lax.all_to_all(group_equiv, "outer", 0, 0, tiled=True)
     peers_part = call(
         peers_kernel, "device_to_device", sds((RHS, LANE), F32), [VM, VM, VM],
-        [tables(8), pltpu.VMEM((4, 2, 3 * RHS, LANE), BF)], 6, peers_equiv, col, row,
+        [tables(12), pltpu.VMEM((4, 2, 3 * RHS, LANE), BF)], 10, peers_equiv, col, row,
     )
     groups = tie(groups, peers_part)
     local = call(
-        local_kernel, "group_and_device_local", flow, [VM, VM, VM, VM, VM], [pad, tables(14)], 8,
-        groups, peers_part, downward, col, row,
+        local_kernel, "group_and_device_local", flow, [VM, VM, VM, VM, VM, HB],
+        [pad, tables(14), pltpu.VMEM(up_shape, BF), pltpu.SemaphoreType.DMA], 12,
+        groups, peers_part, downward, col, row, in_hbm(up_copy),
     )
     dev_local = lax.all_to_all(local, "inner", 0, 0, tiled=True)
     base, evaluate = call(

time: 71.8 us -> 72.4 us (level)
  starting transfers between devices: 30.9 us -> 31.7 us
  transfers between devices with their start and end apart: 5 -> 5, of which waited for: 1 -> 2; matrix products, arithmetic and copies ran while one was open for 0% -> 0% of each run, Pallas kernels for 42% -> 41%
where the time goes in v4:
time: 72.4 us; the launch traced here: 72 us
  Pallas kernels  36.5 us (50%)
  starting transfers between devices  31.7 us (44%)
  waiting for transfers between devices  3.7 us (5%)
    pallas_call x7, Pallas kernels, call(): pl.pallas_call(kernel, name=name, out_shape=outs, in_specs=specs, out_spe...  36.5 us
    all_to_all x1, starting transfers between devices, shards(): peers_equiv = lax.all_to_all(dev_equiv, 'inner', 0, 0, tiled=True)  11.8 us
    all_to_all x1, starting transfers between devices, shards(): groups = lax.all_to_all(group_equiv, 'outer', 0, 0, tiled=True)  9.68 us
    all_to_all x1, starting transfers between devices, shards(): dev_local = lax.all_to_all(local, 'inner', 0, 0, tiled=True)  5.51 us
    all_to_all x1, waiting for transfers between devices, shards(): peers_equiv = lax.all_to_all(dev_equiv, 'inner', 0, 0, tiled=True)  3.49 us
    ppermute x1, starting transfers between devices, shards(): swap = lax.ppermute(own, 'inner', [(i, i ^ 1) for i in range(INNER)])  2.35 us
    ppermute x1, starting transfers between devices, shards(): lax.ppermute(own, 'inner', [(i, (i + 1 ^ 1) - 1) for i in range(1, INNER...  2.29 us
  transfers between devices with their start and end apart: 5, of which 2 were waited for; matrix products, arithmetic and copies ran while one was open for 0% of the time, Pallas kernels for 41%

profile of v4, /device:TPU:1, one launch (start us, length us, event | category | flops | bytes accessed | tf_op | source)
XLA Modules:
  0.0 72.0 jit_solution(13412555801704798473)
XLA Ops:
  0.0 4.4 %leaf_and_device_equiv.1 = (f32[128,128]{1,0:T(8,128)}, f32[72,512]{1,0:T(8,128)S(1)}, f32[165,165]{1,0:T(8,128)S(1)}, f32[165,165]{1,0:T(8,128)S(1)}, f32[176,1...) custom-call(f32[3,512]{1,0:T(4,128)} %off_hbm.1, f32[64,512]{1,0:T(8,128)} %q_hbm.1, s32[16]{0:T(128)} %counts_hbm.1, ...), custom_call_target="tpu_custom_call" | custom-call | flops 1000 | bytes 1000 | tf_op jit(solution)/shard_map/leaf_and_device_equiv/pallas_call | solution.py:512
  4.4 11.8 %all-to-all-start = ((f32[16,8,128]{2,1,0:T(8,128)}), f32[16,8,128]{2,1,0:T(8,128)S(1)}, u32[]{:S(2)}, u32[]{:S(2)}) async-start(f32[16,8,128]{2,1,0:T(8,128)} %bitcast), calls=%async_computation | async-start | bytes 131072 | tf_op jit(solution)/shard_map/all_to_all | solution.py:559
  16.2 4.3 %evaluation_and_group_maps.1 = (bf16[16,2,176,256]{3,2,1,0:T(8,128)(2,1)S(1)}, bf16[2,176,512]{2,1,0:T(8,128)(2,1)}, bf16[2,176,512]{2,1,0:T(8,128)(2,1)}, bf16[16,2,176,256]{3,2,1,0:T(8,128)(2,1)}) custom-call(f32[128,128]{1,0:T(8,128)} %get-tuple-element.19.flow_ref, f32[72,512]{1,0:T(8,128)S(1)} %get-tuple-element.20.off_ref.own_ref, ...), custom_call_target="tpu_custom_call" | custom-call | flops 1000 | bytes 1000 | tf_op jit(solution)/shard_map/evaluation_and_group_maps/pallas_call | solution.py:512
  20.5 3.5 %all-to-all-done = f32[16,8,128]{2,1,0:T(8,128)S(1)} async-done(((f32[16,8,128]{2,1,0:T(8,128)}), f32[16,8,128]{2,1,0:T(8,128)S(1)}, u32[]{:S(2)}, u32[]{:S(2)}) %all-to-all-start) | async-done | bytes 65568 | tf_op jit(solution)/shard_map/all_to_all | solution.py:559
  24.0 0.0 copy-start
  24.0 0.0 copy-start.1
  24.0 1.4 %group_equiv.1 = f32[256,128]{1,0:T(8,128)} custom-call(f32[128,128]{1,0:T(8,128)S(1)} %bitcast.6, bf16[16,2,176,256]{3,2,1,0:T(8,128)(2,1)S(1)} %get-tuple-element.24.maps_ref, f32[165,165]{1,0:T(8,128)S(1)} %get-tuple-element.25.up_ref), custom_call_target="tpu_custom_call" | custom-call | flops 1000 | bytes 1000 | tf_op jit(solution)/shard_map/group_equiv/pallas_call | solution.py:512
  25.4 9.7 %all-to-all-start.1 = ((f32[32,8,128]{2,1,0:T(8,128)}), f32[32,8,128]{2,1,0:T(8,128)S(1)}, u32[]{:S(2)}, u32[]{:S(2)}) async-start(f32[32,8,128]{2,1,0:T(8,128)} %bitcast.10), calls=%async_computation.1 | async-start | bytes 262144 | tf_op jit(solution)/shard_map/all_to_all | solution.py:575
  35.1 2.4 %collective-permute-start = (f32[72,512]{1,0:T(8,128)S(1)}, f32[72,512]{1,0:T(8,128)S(1)}, u32[]{:S(2)}, u32[]{:S(2)}) collective-permute-start(f32[72,512]{1,0:T(8,128)S(1)} %get-tuple-element.20.off_ref.own_ref), channel_id=1, source_target_pairs={{0,1},{1,0},{2,3},{3,2},{4,5},{5,4},{6,7},{7,6},{8,9},{9,8},{10,11... | collective-permute-start | bytes 442376 | tf_op jit(solution)/shard_map/ppermute | solution.py:568
  37.5 2.3 %collective-permute-start.1 = (f32[72,512]{1,0:T(8,128)S(1)}, f32[72,512]{1,0:T(8,128)S(1)}, u32[]{:S(2)}, u32[]{:S(2)}) collective-permute-start(f32[72,512]{1,0:T(8,128)S(1)} %get-tuple-element.20.off_ref.own_ref), channel_id=1, source_target_pairs={{1,2},{2,1},{3,4},{4,3},{5,6},{6,5},{7,8},{8,7},{9,10},{10,9},{11,... | collective-permute-start | bytes 442376 | tf_op jit(solution)/shard_map/ppermute | solution.py:569
  39.8 4.3 %device_to_device.1.peers_ref = f32[64,256]{1,0:T(8,128)S(1)} custom-call(f32[128,128]{1,0:T(8,128)S(1)} %bitcast.7, f32[176,128]{1,0:T(8,128)S(1)} %get-tuple-element.22.col_ref, f32[8,256]{1,0:T(8,128)S(1)} %get-tuple-element.23.row_ref), custom_call_target="tpu_custom_call" | custom-call | flops 1000 | bytes 1000 | tf_op jit(solution)/shard_map/device_to_device/pallas_call | solution.py:512
  44.1 0.2 all-to-all-done.1
  44.3 4.8 %group_and_device_local.1 = f32[128,128]{1,0:T(8,128)} custom-call(f32[256,128]{1,0:T(8,128)S(1)} %bitcast.8, f32[64,256]{1,0:T(8,128)S(1)} %device_to_device.1.peers_ref, f32[165,165]{1,0:T(8,128)S(1)} %get-tuple-element.21.down_ref, f32[176,128]{1,0:T(8,128)S(1)} %get-tuple-element.22.col_ref, f32[8,256]{1,0:T(8,128)S(1)} %get-tuple-element.23.row_ref, ...), custom_call_target="tpu_custom_call" | custom-call | flops 1000 | bytes 1000 | tf_op jit(solution)/shard_map/group_and_device_local/pallas_call | solution.py:512
  49.0 5.5 %all-to-all-start.2 = ((f32[16,8,128]{2,1,0:T(8,128)}), f32[16,8,128]{2,1,0:T(8,128)S(1)}, u32[]{:S(2)}, u32[]{:S(2)}) async-start(f32[16,8,128]{2,1,0:T(8,128)} %bitcast.4), calls=%async_computation.2 | async-start | bytes 131072 | tf_op jit(solution)/shard_map/all_to_all | solution.py:586
  54.6 0.0 collective-permute-done.swap_ref
  54.6 0.0 collective-permute-done.1.cross_ref
  54.6 0.0 copy-done
  54.6 0.0 copy-done.1
  54.6 16.5 %near_and_far_field.1 = (f32[64,512]{1,0:T(8,128)S(1)}, bf16[2,176,512]{2,1,0:T(8,128)(2,1)S(1)}) custom-call(s32[16,12]{1,0:T(8,128)S(1)} %copy-done, s32[16,12]{1,0:T(8,128)S(1)} %copy-done.1, f32[72,512]{1,0:T(8,128)S(1)} %get-tuple-element.20.off_ref.own_ref, f32[72,512]{1,0:T(8,128)S(1)} %collective-permute-done.swap_ref, ...), custom_call_target="tpu_custom_call" | custom-call | flops 1000 | bytes 1000 | tf_op jit(solution)/shard_map/near_and_far_field/pallas_call | solution.py:512
  71.1 0.0 all-to-all-done.2
  71.1 0.9 %potential.1 = f32[64,512]{1,0:T(8,128)} custom-call(f32[128,128]{1,0:T(8,128)S(1)} %bitcast.9, f32[64,512]{1,0:T(8,128)S(1)} %get-tuple-element.31.base_ref, bf16[2,176,512]{2,1,0:T(8,128)(2,1)S(1)} %get-tuple-element.32.m_ref), custom_call_target="tpu_custom_call" | custom-call | flops 1000 | bytes 1000 | tf_op jit(solution)/shard_map/potential/pallas_call | solution.py:512
Async XLA Ops:
  4.4 19.7 %all-to-all-start = ((f32[16,8,128]{2,1,0:T(8,128)}), f32[16,8,128]{2,1,0:T(8,128)S(1)}, u32[]{:S(2)}, u32[]{:S(2)}) async-start(f32[16,8,128]{2,1,0:T(8,128)} %bitcast), calls=%async_computation | async-start | bytes 131072 | tf_op jit(solution)/shard_map/all_to_all | solution.py:559
  24.0 30.5 %copy-start = (s32[16,12]{1,0:T(8,128)S(1)}, s32[16,12]{1,0:T(8,128)}, u32[]{:S(2)}) copy-start(s32[16,12]{1,0:T(8,128)} %far_ref.1) | copy-start | bytes 2308
  24.0 30.5 %copy-start.1 = (s32[16,12]{1,0:T(8,128)S(1)}, s32[16,12]{1,0:T(8,128)}, u32[]{:S(2)}) copy-start(s32[16,12]{1,0:T(8,128)} %near_ref.1) | copy-start | bytes 2308
  25.4 18.8 %all-to-all-start.1 = ((f32[32,8,128]{2,1,0:T(8,128)}), f32[32,8,128]{2,1,0:T(8,128)S(1)}, u32[]{:S(2)}, u32[]{:S(2)}) async-start(f32[32,8,128]{2,1,0:T(8,128)} %bitcast.10), calls=%async_computation.1 | async-start | bytes 262144 | tf_op jit(solution)/shard_map/all_to_all | solution.py:575
  35.1 19.4 %collective-permute-start = (f32[72,512]{1,0:T(8,128)S(1)}, f32[72,512]{1,0:T(8,128)S(1)}, u32[]{:S(2)}, u32[]{:S(2)}) collective-permute-start(f32[72,512]{1,0:T(8,128)S(1)} %get-tuple-element.20.off_ref.own_ref), channel_id=1, source_target_pairs={{0,1},{1,0},{2,3},{3,2},{4,5},{5,4},{6,7},{7,6},{8,9},{9,8},{10,11... | collective-permute-start | bytes 442376 | tf_op jit(solution)/shard_map/ppermute | solution.py:568
  37.5 17.1 %collective-permute-start.1 = (f32[72,512]{1,0:T(8,128)S(1)}, f32[72,512]{1,0:T(8,128)S(1)}, u32[]{:S(2)}, u32[]{:S(2)}) collective-permute-start(f32[72,512]{1,0:T(8,128)S(1)} %get-tuple-element.20.off_ref.own_ref), channel_id=1, source_target_pairs={{1,2},{2,1},{3,4},{4,3},{5,6},{6,5},{7,8},{8,7},{9,10},{10,9},{11,... | collective-permute-start | bytes 442376 | tf_op jit(solution)/shard_map/ppermute | solution.py:569
  49.0 22.1 %all-to-all-start.2 = ((f32[16,8,128]{2,1,0:T(8,128)}), f32[16,8,128]{2,1,0:T(8,128)S(1)}, u32[]{:S(2)}, u32[]{:S(2)}) async-start(f32[16,8,128]{2,1,0:T(8,128)} %bitcast.4), calls=%async_computation.2 | async-start | bytes 131072 | tf_op jit(solution)/shard_map/all_to_all | solution.py:586

commit v5 on v4

--- a/solution.py
+++ b/solution.py
@@ -19,6 +19,8 @@
 POINTS = LEAVES * SLOTS
 ROWS = 72
 INNER = 16
+EQUIV = LEAVES * RHS
+HALO = EQUIV + 2 * ROWS
 OUTER = 32
 PART = RHS // INNER
 BF = jnp.bfloat16
@@ -130,18 +132,17 @@
     for half in range(2):
         lanes = slice(half * 256, half * 256 + 256)
         spread = [jnp.concatenate([piece[:, lanes] * keep[g] for g in range(8)], axis=0) for piece in pieces]
-        check = mm3(spread, (kern[0][:, lanes], kern[1][:, lanes]), dot_nt)
+        high, low = kern[0][:, lanes], kern[1][:, lanes]
+        spread = jnp.concatenate([spread[0], spread[1], spread[0]], axis=1)
+        check = dot_nt(spread, jnp.concatenate([high, high, low], axis=1))
         out.append(mm3(split(check), up))
     return out
 
 
-def store_equivalents(halves, e_ref, first):
-    for half in range(2):
-        e_high, e_low = split(halves[half])
-        for g in range(8):
-            start = first + (half * 8 + g) * 2 * RHS
-            e_ref[start : start + RHS, :] = e_high[g * RHS : g * RHS + RHS]
-            e_ref[start + RHS : start + 2 * RHS, :] = e_low[g * RHS : g * RHS + RHS]
+def store_equivalents(rows, e_ref, first):
+    high, low = split(rows)
+    e_ref[pl.ds(first, RHS), :] = high
+    e_ref[pl.ds(first + RHS, RHS), :] = low
 
 
 def pack(rows):
@@ -183,8 +184,8 @@
 
 def head_kernel(
     off_hbm, q_hbm, counts_hbm, up_hbm, down_hbm, col_hbm, row_hbm,
-    out_ref, halo_ref, up_ref, down_ref, col_ref, row_ref, e_hbm,
-    off_ref, q_ref, counts_ref, pad_ref, tab_ref, e_ref, sems,
+    out_ref, halo_ref, up_ref, down_ref, col_ref, row_ref, beside_hbm,
+    off_ref, q_ref, counts_ref, pad_ref, tab_ref, e_ref, beside_ref, sems,
 ):
     moves = [
         pltpu.make_async_copy(src, dst, sems.at[n])
@@ -213,12 +214,17 @@
     halo_ref[0:RHS, :] = charges
     halo_ref[RHS:ROWS, :] = jnp.zeros((ROWS - RHS, POINTS), F32)
     halo_ref[RHS : RHS + 3, :] = off_ref[...]
+    beside_ref[EQUIV : EQUIV + ROWS, :] = halo_ref[:, :256]
+    beside_ref[EQUIV + ROWS : HALO, :] = halo_ref[:, 256:]
     kern = split(leaf_kernel(off_ref[...], col_ref))
     up = padded(up_ref, pad_ref, 18.0 / TERMS)
     up = (up[0][:, :], up[1][:, :])
     halves = leaf_equivalents(charges, kern, up)
-    store_equivalents(halves, e_ref, 0)
-    e_move = pltpu.make_async_copy(e_ref, e_hbm, sems.at[7])
+    for half in range(2):
+        beside_ref[half * 8 * RHS : (half + 1) * 8 * RHS, :] = halves[half]
+        for g in range(8):
+            store_equivalents(halves[half][g * RHS : (g + 1) * RHS], e_ref, (half * 8 + g) * 2 * RHS)
+    e_move = pltpu.make_async_copy(beside_ref, beside_hbm, sems.at[7])
     e_move.start()
     acc = jnp.zeros((RHS, LANE), F32)
     for (x, y, z), kern in box_kernels(
@@ -305,9 +311,7 @@
     out_ref[...] = index_order(acc[0] + back)
 
 
-def local_kernel(x_ref, peers_ref, down_ref, col_ref, row_ref, up_hbm, out_ref, pad_ref, tab_ref, up_ref, sem):
-    move = pltpu.make_async_copy(up_hbm, up_ref, sem)
-    move.start()
+def local_kernel(x_ref, peers_ref, down_ref, col_ref, row_ref, out_ref, pad_ref, tab_ref):
     outer = lax.axis_index("outer")
     own = [p.astype(F32) for p in corner(outer * 256, 8)]
     cols = columns(col_ref)
@@ -327,19 +331,21 @@
     both = jnp.concatenate([check, check], axis=0)
     group = mm3(split(both[:, :SUB]), padded(down_ref, pad_ref, 200.0 / TERMS))[:8]
     pieces = jnp.concatenate(split(group[:, :SUB]), axis=0)
-    top = lax.broadcasted_iota(jnp.int32, (8, SUB), 0) < 4
-    move.wait()
-    found = []
-    for d in range(INNER):
-        part = dot_nt(pieces, up_ref[d, 0][:, :SUB]) + dot_nt(pieces, up_ref[d, 1][:, :SUB])
-        found.append(part[:8] + part[8:])
+    top = lax.broadcasted_iota(jnp.int32, (8, LANE), 0) < 4
+    found = [None] * INNER
+    for (x, y, z), kern in box_kernels(
+        (-2.0, 2.0), (-3.0, -1.0, 1.0, 3.0), (-1.0, 1.0), 3.0, 20.0, col_ref, row_ref, tab_ref
+    ):
+        high, low = split(kern)
+        part = dot(pieces, high) + dot(pieces, low)
+        found[(y & 1) + z * 2 + x * 4 + (y >> 1) * 8] = part[:8] + part[8:]
     merged = [jnp.where(top, found[2 * m], pltpu.roll(found[2 * m + 1], 4, 0)) for m in range(INNER // 2)]
-    total = jnp.concatenate(merged, axis=0) + peers_ref[:, :SUB]
-    out_ref[...] = pack(mm3(split(total), padded(down_ref, pad_ref, 60.0 / TERMS)))
+    total = jnp.concatenate(merged, axis=0) + peers_ref[...]
+    out_ref[...] = pack(mm3(split(total[:, :SUB]), padded(down_ref, pad_ref, 60.0 / TERMS)))
 
 
 def operator_kernel(
-    flow_ref, off_ref, down_ref, col_ref, row_ref, up_ref, w_hbm, m_hbm, up_hbm, w_ref, m_ref, pad_ref, tab_ref, sems
+    flow_ref, off_ref, down_ref, col_ref, row_ref, up_ref, w_hbm, m_hbm, w_ref, m_ref, pad_ref, tab_ref, sems
 ):
     for (x, y, z), kern in box_kernels(
         (2.0, -2.0), (3.0, 1.0, -1.0, -3.0), (1.0, -1.0), 20.0, 3.0, col_ref, row_ref, tab_ref
@@ -348,8 +354,6 @@
         high, low = split(kern)
         up_ref[e, 0, :, :] = high
         up_ref[e, 1, :, :] = low
-    up_move = pltpu.make_async_copy(up_ref, up_hbm, sems.at[2])
-    up_move.start()
     kern = split(leaf_kernel(off_ref[RHS : RHS + 3, :], col_ref))
     down = padded(down_ref, pad_ref, 18.0 / TERMS)
     down = (down[0][:, :SUB], down[1][:, :SUB])
@@ -374,7 +378,6 @@
         m_ref[1, :, lanes] = m_low
     m_move = pltpu.make_async_copy(m_ref, m_hbm, sems.at[1])
     m_move.start()
-    up_move.wait()
     w_move.wait()
     m_move.wait()
 
@@ -421,29 +424,30 @@
 
 
 def field_kernel(
-    far_ref, near_ref, own_ref, swap_ref, cross_ref, up_ref, col_ref, row_ref, w_hbm, m_hbm, e_hbm, out_ref, m_ref,
-    pad_ref, e_ref, dl_ref, xtab_ref, tab_ref, w_ref, left_ref, right_ref, mask_ref, high_ref, low_ref, sems,
+    far_ref, near_ref, own_ref, col_ref, row_ref, own_hbm, swap_hbm, cross_hbm, w_hbm, m_hbm, out_ref, m_ref,
+    e_ref, dl_ref, xtab_ref, tab_ref, w_ref, left_ref, right_ref, mask_ref, high_ref, low_ref,
+    self_ref, swap_ref, cross_ref, sems,
 ):
-    middle = LEAVES * 2 * RHS
+    points, equivs = pl.ds(EQUIV, 2 * ROWS), pl.ds(0, EQUIV)
     moves = [
-        pltpu.make_async_copy(e_hbm, e_ref.at[middle : 2 * middle], sems.at[0]),
-        pltpu.make_async_copy(w_hbm, w_ref, sems.at[1]),
-        pltpu.make_async_copy(m_hbm, m_ref, sems.at[2]),
+        pltpu.make_async_copy(src, dst, sems.at[n])
+        for n, (src, dst) in enumerate(
+            (
+                (swap_hbm.at[points], swap_ref.at[points]),
+                (cross_hbm.at[points], cross_ref.at[points]),
+                (own_hbm.at[equivs], self_ref),
+                (swap_hbm.at[equivs], swap_ref.at[equivs]),
+                (cross_hbm.at[equivs], cross_ref.at[equivs]),
+                (w_hbm, w_ref),
+                (m_hbm, m_ref),
+            )
+        )
     ]
     for move in moves:
         move.start()
-    odd = lax.rem(lax.axis_index("inner"), 2) == 1
-    left_ref[...] = jnp.where(odd, swap_ref[...], cross_ref[...])
-    right_ref[...] = jnp.where(odd, cross_ref[...], swap_ref[...])
-    near_field(near_ref, left_ref, own_ref, right_ref, out_ref, mask_ref, high_ref, low_ref)
     inner = lax.axis_index("inner")
     device = lax.axis_index("outer") * INNER + inner
-    up = padded(up_ref, pad_ref, 18.0 / TERMS)
-    for side, ref in ((0, left_ref), (2, right_ref)):
-        kern = split(leaf_kernel(ref[RHS : RHS + 3, :], col_ref))
-        store_equivalents(leaf_equivalents(ref[0:RHS, :], kern, up), e_ref, side * middle)
-    for move in moves:
-        move.wait()
+    odd = lax.rem(inner, 2) == 1
     first = (device - 1) * LEAVES
     boxes = [corner((device + side) * LEAVES, 4) for side in (-1, 0, 1)]
     boxes = [[(boxes[1][c] - box[c]).astype(F32) for c in range(3)] for box in boxes]
@@ -457,6 +461,26 @@
             ysq = square_of(1, boxes[side][1] + (b - 1.0), 0.9, 1.8, cols, row_ref)
             for c in range(3):
                 tab_ref[side * 9 + b * 3 + c] = ysq + tab_ref[27 + c]
+    moves[0].wait()
+    moves[1].wait()
+    for half in range(2):
+        lanes = slice(half * 256, half * 256 + 256)
+        rows = slice(EQUIV + half * ROWS, EQUIV + (half + 1) * ROWS)
+        swap, cross = swap_ref[rows, :], cross_ref[rows, :]
+        left_ref[:, lanes] = jnp.where(odd, swap, cross)
+        right_ref[:, lanes] = jnp.where(odd, cross, swap)
+    near_field(near_ref, left_ref, own_ref, right_ref, out_ref, mask_ref, high_ref, low_ref)
+    for move in moves[2:]:
+        move.wait()
+    middle = 2 * EQUIV
+    swap_at = pl.multiple_of(jnp.where(odd, 0, 2 * middle), 2 * RHS)
+    cross_at = pl.multiple_of(jnp.where(odd, 2 * middle, 0), 2 * RHS)
+    for ref, place in ((self_ref, middle), (swap_ref, swap_at), (cross_ref, cross_at)):
+        for g in range(LEAVES):
+            start = place + g * 2 * RHS
+            if ref is not self_ref:
+                start = pl.multiple_of(start, 2 * RHS)
+            store_equivalents(ref[g * RHS : (g + 1) * RHS, :], e_ref, start)
 
     def one_leaf(g, carry):
         own = local_leaf(g)
@@ -540,10 +564,9 @@
         return pltpu.VMEM((n, SUB, LANE), F32)
 
     inputs = (offsets, charges, counts, upward, downward, jnp.asarray(col_np), jnp.asarray(row_np))
-    equiv_rows = LEAVES * 2 * RHS
-    dev_equiv, own, upward, downward, col, row, equiv = call(
+    dev_equiv, own, upward, downward, col, row, beside = call(
         head_kernel, "leaf_and_device_equiv",
-        (flow, sds((ROWS, POINTS), F32), square, square, sds((SUB, 128), F32), sds((8, LANE), F32), pltpu.HBM((equiv_rows, LANE), BF)),
+        (flow, sds((ROWS, POINTS), F32), square, square, sds((SUB, 128), F32), sds((8, LANE), F32), pltpu.HBM((HALO, LANE), F32)),
         [HB] * 7,
         [
             pltpu.VMEM((3, POINTS), F32),
@@ -551,22 +574,22 @@
             pltpu.SMEM((LEAVES,), jnp.int32),
             pad,
             tables(10),
-            pltpu.VMEM((equiv_rows, LANE), BF),
+            pltpu.VMEM((2 * EQUIV, LANE), BF),
+            pltpu.VMEM((HALO, LANE), F32),
             pltpu.SemaphoreType.DMA((8,)),
         ],
         16, *map(in_hbm, inputs), out_specs=(VM, VM, VM, VM, VM, VM, HB),
     )
     peers_equiv = lax.all_to_all(dev_equiv, "inner", 0, 0, tiled=True)
     leaf_maps = pltpu.HBM((2, SUB, POINTS), BF)
-    up_shape = (INNER, 2, SUB, LANE)
-    up_maps, weights, evaluate, up_copy = call(
-        operator_kernel, "evaluation_and_group_maps", (sds(up_shape, BF), leaf_maps, leaf_maps, pltpu.HBM(up_shape, BF)),
+    up_maps, weights, evaluate = call(
+        operator_kernel, "evaluation_and_group_maps", (sds((INNER, 2, SUB, LANE), BF), leaf_maps, leaf_maps),
         [VM, VM, VM, VM, VM],
-        [pltpu.VMEM((2, SUB, POINTS), BF), pltpu.VMEM((2, SUB, POINTS), BF), pad, tables(14), pltpu.SemaphoreType.DMA((3,))],
-        14, dev_equiv, own, downward, col, row, out_specs=(VM, HB, HB, HB),
-    )
-    swap = lax.ppermute(own, "inner", [(i, i ^ 1) for i in range(INNER)])
-    cross = lax.ppermute(own, "inner", [(i, ((i + 1) ^ 1) - 1) for i in range(1, INNER - 1)])
+        [pltpu.VMEM((2, SUB, POINTS), BF), pltpu.VMEM((2, SUB, POINTS), BF), pad, tables(14), pltpu.SemaphoreType.DMA((2,))],
+        14, dev_equiv, own, downward, col, row, out_specs=(VM, HB, HB),
+    )
+    swap = lax.ppermute(beside, "inner", [(i, i ^ 1) for i in range(INNER)])
+    cross = lax.ppermute(beside, "inner", [(i, ((i + 1) ^ 1) - 1) for i in range(1, INNER - 1)])
     group_equiv = call(
         group_up_kernel, "group_equiv", pltpu.HBM((8 * OUTER, 128), F32), [VM, VM, VM],
         [pad, pltpu.VMEM((8 * OUTER, 128), F32), pltpu.SemaphoreType.DMA], 6,
@@ -579,18 +602,16 @@
     )
     groups = tie(groups, peers_part)
     local = call(
-        local_kernel, "group_and_device_local", flow, [VM, VM, VM, VM, VM, HB],
-        [pad, tables(14), pltpu.VMEM(up_shape, BF), pltpu.SemaphoreType.DMA], 12,
-        groups, peers_part, downward, col, row, in_hbm(up_copy),
+        local_kernel, "group_and_device_local", flow, [VM, VM, VM, VM, VM], [pad, tables(14)], 8,
+        groups, peers_part, downward, col, row,
     )
     dev_local = lax.all_to_all(local, "inner", 0, 0, tiled=True)
     base, evaluate = call(
         field_kernel, "near_and_far_field", (sds((RHS, POINTS), F32), sds((2, SUB, POINTS), BF)),
-        [SM, VM, VM, VM, VM, VM, VM, VM, HB, HB, HB],
+        [SM, VM, VM, VM, VM, HB, HB, HB, HB, HB],
         [
-            pad,
-            pltpu.VMEM((3 * LEAVES * 2 * RHS, LANE), BF),
-            pltpu.VMEM((2, LEAVES * RHS, LANE), BF),
+            pltpu.VMEM((6 * EQUIV, LANE), BF),
+            pltpu.VMEM((2, EQUIV, LANE), BF),
             tables(21),
             tables(30),
             pltpu.VMEM((2, SUB, POINTS), BF),
@@ -599,9 +620,12 @@
             pltpu.VMEM((LEAVES, 3 * POINTS), F32),
             pltpu.VMEM((POINTS, 3 * POINTS), BF),
             pltpu.VMEM((POINTS, 3 * POINTS), BF),
-            pltpu.SemaphoreType.DMA((3,)),
+            pltpu.VMEM((EQUIV, LANE), F32),
+            pltpu.VMEM((HALO, LANE), F32),
+            pltpu.VMEM((HALO, LANE), F32),
+            pltpu.SemaphoreType.DMA((7,)),
         ],
-        32, far, near, own, swap, cross, upward, col, row, in_hbm(weights), in_hbm(evaluate), in_hbm(equiv),
+        36, far, near, own, col, row, *map(in_hbm, (beside, swap, cross, weights, evaluate)),
     )
     return call(tail_kernel, "potential", sds((RHS, POINTS), F32), [VM, VM, VM], [], 4, dev_local, base, evaluate)
 

time: 72.4 us -> 82.4 us (1.14)
  waiting for transfers between devices: 3.7 us -> 13.8 us
  Pallas kernels: 36.5 us -> 34.7 us
  starting transfers between devices: 31.7 us -> 33.4 us
    ppermute x2, starting transfers between devices: 4.64 us -> 10.7 us  [the longest x1 8.79 us: shards(): swap = lax.ppermute(beside, 'inner', [(i, i ^ 1) for i in range(INNER)])]
    all_to_all x1, starting transfers between devices: 11.8 us -> 6.15 us  [shards(): peers_equiv = lax.all_to_all(dev_equiv, 'inner', 0, 0, tiled=True)]
    all_to_all x1, waiting for transfers between devices: 3.49 us -> 9.16 us  [shards(): peers_equiv = lax.all_to_all(dev_equiv, 'inner', 0, 0, tiled=True)]
    all_to_all x1, waiting for transfers between devices: 0.2 us -> 4.67 us  [shards(): groups = lax.all_to_all(group_equiv, 'outer', 0, 0, tiled=True)]
    pallas_call x7, Pallas kernels: 36.5 us -> 34.7 us  [call(): pl.pallas_call(kernel, name=name, out_shape=outs, in_specs=specs, out_spe...]
    all_to_all x1, starting transfers between devices: 5.51 us -> 6.55 us  [shards(): dev_local = lax.all_to_all(local, 'inner', 0, 0, tiled=True)]
  transfers between devices with their start and end apart: 5 -> 5, of which waited for: 2 -> 2; matrix products, arithmetic and copies ran while one was open for 0% -> 0% of each run, Pallas kernels for 41% -> 35%
where the time goes in v5:
time: 82.4 us; the launch traced here: 82 us
  Pallas kernels  34.7 us (42%)
  starting transfers between devices  33.4 us (41%)
  waiting for transfers between devices  13.8 us (17%)
    pallas_call x7, Pallas kernels, call(): pl.pallas_call(kernel, name=name, out_shape=outs, in_specs=specs, out_spe...  34.7 us
    all_to_all x1, starting transfers between devices, shards(): groups = lax.all_to_all(group_equiv, 'outer', 0, 0, tiled=True)  9.98 us
    all_to_all x1, waiting for transfers between devices, shards(): peers_equiv = lax.all_to_all(dev_equiv, 'inner', 0, 0, tiled=True)  9.16 us
    ppermute x1, starting transfers between devices, shards(): swap = lax.ppermute(beside, 'inner', [(i, i ^ 1) for i in range(INNER)])  8.79 us
    all_to_all x1, starting transfers between devices, shards(): dev_local = lax.all_to_all(local, 'inner', 0, 0, tiled=True)  6.55 us
    all_to_all x1, starting transfers between devices, shards(): peers_equiv = lax.all_to_all(dev_equiv, 'inner', 0, 0, tiled=True)  6.15 us
    all_to_all x1, waiting for transfers between devices, shards(): groups = lax.all_to_all(group_equiv, 'outer', 0, 0, tiled=True)  4.67 us
    ppermute x1, starting transfers between devices, shards(): lax.ppermute(beside, 'inner', [(i, (i + 1 ^ 1) - 1) for i in range(1, INN...  1.92 us
  transfers between devices with their start and end apart: 5, of which 2 were waited for; matrix products, arithmetic and copies ran while one was open for 0% of the time, Pallas kernels for 35%

profile of v5, /device:TPU:1, one launch (start us, length us, event | category | flops | bytes accessed | tf_op | source)
XLA Modules:
  0.0 82.0 jit_solution(4919628907736505289)
XLA Ops:
  0.0 5.3 %leaf_and_device_equiv.1 = (f32[128,128]{1,0:T(8,128)}, f32[72,512]{1,0:T(8,128)S(1)}, f32[165,165]{1,0:T(8,128)S(1)}, f32[165,165]{1,0:T(8,128)S(1)}, f32[176,1...) custom-call(f32[3,512]{1,0:T(4,128)} %off_hbm.1, f32[64,512]{1,0:T(8,128)} %q_hbm.1, s32[16]{0:T(128)} %counts_hbm.1, ...), custom_call_target="tpu_custom_call" | custom-call | flops 1000 | bytes 1000 | tf_op jit(solution)/shard_map/leaf_and_device_equiv/pallas_call | solution.py:536
  5.3 8.8 %collective-permute-start = (f32[1168,256]{1,0:T(8,128)}, f32[1168,256]{1,0:T(8,128)}, u32[]{:S(2)}, u32[]{:S(2)}) collective-permute-start(f32[1168,256]{1,0:T(8,128)} %get-tuple-element.26.own_hbm), channel_id=1, source_target_pairs={{0,1},{1,0},{2,3},{3,2},{4,5},{5,4},{6,7},{7,6},{8,9},{9,8},{10,11... | collective-permute-start | bytes 3588104 | tf_op jit(solution)/shard_map/ppermute | solution.py:591
  14.1 1.9 %collective-permute-start.1 = (f32[1168,256]{1,0:T(8,128)}, f32[1168,256]{1,0:T(8,128)}, u32[]{:S(2)}, u32[]{:S(2)}) collective-permute-start(f32[1168,256]{1,0:T(8,128)} %get-tuple-element.26.own_hbm), channel_id=1, source_target_pairs={{1,2},{2,1},{3,4},{4,3},{5,6},{6,5},{7,8},{8,7},{9,10},{10,9},{11,... | collective-permute-start | bytes 3588104 | tf_op jit(solution)/shard_map/ppermute | solution.py:592
  16.0 6.1 %all-to-all-start = ((f32[16,8,128]{2,1,0:T(8,128)}), f32[16,8,128]{2,1,0:T(8,128)S(1)}, u32[]{:S(2)}, u32[]{:S(2)}) async-start(f32[16,8,128]{2,1,0:T(8,128)} %bitcast), calls=%async_computation | async-start | bytes 131072 | tf_op jit(solution)/shard_map/all_to_all | solution.py:583
  22.1 4.3 %evaluation_and_group_maps.1 = (bf16[16,2,176,256]{3,2,1,0:T(8,128)(2,1)S(1)}, bf16[2,176,512]{2,1,0:T(8,128)(2,1)}, bf16[2,176,512]{2,1,0:T(8,128)(2,1)}) custom-call(f32[128,128]{1,0:T(8,128)} %get-tuple-element.18.flow_ref, f32[72,512]{1,0:T(8,128)S(1)} %get-tuple-element.19.off_ref.own_ref, f32[165,165]{1,0:T(8,128)S(1)} %get-tuple-element.20.down_ref, ...), custom_call_target="tpu_custom_call" | custom-call | flops 1000 | bytes 1000 | tf_op jit(solution)/shard_map/evaluation_and_group_maps/pallas_call | solution.py:536
  26.4 9.2 %all-to-all-done = f32[16,8,128]{2,1,0:T(8,128)S(1)} async-done(((f32[16,8,128]{2,1,0:T(8,128)}), f32[16,8,128]{2,1,0:T(8,128)S(1)}, u32[]{:S(2)}, u32[]{:S(2)}) %all-to-all-start) | async-done | bytes 65568 | tf_op jit(solution)/shard_map/all_to_all | solution.py:583
  35.6 0.0 copy-start
  35.6 0.0 copy-start.1
  35.6 1.4 %group_equiv.1 = f32[256,128]{1,0:T(8,128)} custom-call(f32[128,128]{1,0:T(8,128)S(1)} %bitcast.6, bf16[16,2,176,256]{3,2,1,0:T(8,128)(2,1)S(1)} %get-tuple-element.23.maps_ref, f32[165,165]{1,0:T(8,128)S(1)} %get-tuple-element.24.up_ref), custom_call_target="tpu_custom_call" | custom-call | flops 1000 | bytes 1000 | tf_op jit(solution)/shard_map/group_equiv/pallas_call | solution.py:536
  37.0 10.0 %all-to-all-start.1 = ((f32[32,8,128]{2,1,0:T(8,128)}), f32[32,8,128]{2,1,0:T(8,128)S(1)}, u32[]{:S(2)}, u32[]{:S(2)}) async-start(f32[32,8,128]{2,1,0:T(8,128)} %bitcast.10), calls=%async_computation.1 | async-start | bytes 262144 | tf_op jit(solution)/shard_map/all_to_all | solution.py:598
  46.9 4.3 %device_to_device.1.peers_ref = f32[64,256]{1,0:T(8,128)S(1)} custom-call(f32[128,128]{1,0:T(8,128)S(1)} %bitcast.7, f32[176,128]{1,0:T(8,128)S(1)} %get-tuple-element.21.col_ref, f32[8,256]{1,0:T(8,128)S(1)} %get-tuple-element.22.row_ref), custom_call_target="tpu_custom_call" | custom-call | flops 1000 | bytes 1000 | tf_op jit(solution)/shard_map/device_to_device/pallas_call | solution.py:536
  51.2 4.7 %all-to-all-done.1 = f32[32,8,128]{2,1,0:T(8,128)S(1)} async-done(((f32[32,8,128]{2,1,0:T(8,128)}), f32[32,8,128]{2,1,0:T(8,128)S(1)}, u32[]{:S(2)}, u32[]{:S(2)}) %all-to-all-start.1) | async-done | bytes 131104 | tf_op jit(solution)/shard_map/all_to_all | solution.py:598
  55.9 3.7 %group_and_device_local.1 = f32[128,128]{1,0:T(8,128)} custom-call(f32[256,128]{1,0:T(8,128)S(1)} %bitcast.8, f32[64,256]{1,0:T(8,128)S(1)} %device_to_device.1.peers_ref, f32[165,165]{1,0:T(8,128)S(1)} %get-tuple-element.20.down_ref, f32[176,128]{1,0:T(8,128)S(1)} %get-tuple-element.21.col_ref, f32[8,256]{1,0:T(8,128)S(1)} %get-tuple-element.22.row_ref), custom_call_target="tpu_custom_call" | custom-call | flops 1000 | bytes 1000 | tf_op jit(solution)/shard_map/group_and_device_local/pallas_call | solution.py:536
  59.6 6.6 %all-to-all-start.2 = ((f32[16,8,128]{2,1,0:T(8,128)}), f32[16,8,128]{2,1,0:T(8,128)S(1)}, u32[]{:S(2)}, u32[]{:S(2)}) async-start(f32[16,8,128]{2,1,0:T(8,128)} %bitcast.4), calls=%async_computation.2 | async-start | bytes 131072 | tf_op jit(solution)/shard_map/all_to_all | solution.py:608
  66.2 0.0 collective-permute-done.swap_hbm
  66.2 0.0 collective-permute-done.1.cross_hbm
  66.2 0.0 copy-done
  66.2 0.0 copy-done.1
  66.2 14.9 %near_and_far_field.1 = (f32[64,512]{1,0:T(8,128)S(1)}, bf16[2,176,512]{2,1,0:T(8,128)(2,1)S(1)}) custom-call(s32[16,12]{1,0:T(8,128)S(1)} %copy-done, s32[16,12]{1,0:T(8,128)S(1)} %copy-done.1, f32[72,512]{1,0:T(8,128)S(1)} %get-tuple-element.19.off_ref.own_ref, f32[176,128]{1,0:T(8,128)S(1)} %get-tuple-element.21.col_ref, ...), custom_call_target="tpu_custom_call" | custom-call | flops 1000 | bytes 1000 | tf_op jit(solution)/shard_map/near_and_far_field/pallas_call | solution.py:536
  81.2 0.0 all-to-all-done.2
  81.2 0.9 %potential.1 = f32[64,512]{1,0:T(8,128)} custom-call(f32[128,128]{1,0:T(8,128)S(1)} %bitcast.9, f32[64,512]{1,0:T(8,128)S(1)} %get-tuple-element.29.base_ref, bf16[2,176,512]{2,1,0:T(8,128)(2,1)S(1)} %get-tuple-element.30.m_ref), custom_call_target="tpu_custom_call" | custom-call | flops 1000 | bytes 1000 | tf_op jit(solution)/shard_map/potential/pallas_call | solution.py:536
Async XLA Ops:
  5.3 60.9 %collective-permute-start = (f32[1168,256]{1,0:T(8,128)}, f32[1168,256]{1,0:T(8,128)}, u32[]{:S(2)}, u32[]{:S(2)}) collective-permute-start(f32[1168,256]{1,0:T(8,128)} %get-tuple-element.26.own_hbm), channel_id=1, source_target_pairs={{0,1},{1,0},{2,3},{3,2},{4,5},{5,4},{6,7},{7,6},{8,9},{9,8},{10,11... | collective-permute-start | bytes 3588104 | tf_op jit(solution)/shard_map/ppermute | solution.py:591
  14.1 52.1 %collective-permute-start.1 = (f32[1168,256]{1,0:T(8,128)}, f32[1168,256]{1,0:T(8,128)}, u32[]{:S(2)}, u32[]{:S(2)}) collective-permute-start(f32[1168,256]{1,0:T(8,128)} %get-tuple-element.26.own_hbm), channel_id=1, source_target_pairs={{1,2},{2,1},{3,4},{4,3},{5,6},{6,5},{7,8},{8,7},{9,10},{10,9},{11,... | collective-permute-start | bytes 3588104 | tf_op jit(solution)/shard_map/ppermute | solution.py:592
  16.0 19.6 %all-to-all-start = ((f32[16,8,128]{2,1,0:T(8,128)}), f32[16,8,128]{2,1,0:T(8,128)S(1)}, u32[]{:S(2)}, u32[]{:S(2)}) async-start(f32[16,8,128]{2,1,0:T(8,128)} %bitcast), calls=%async_computation | async-start | bytes 131072 | tf_op jit(solution)/shard_map/all_to_all | solution.py:583
  35.6 30.6 %copy-start = (s32[16,12]{1,0:T(8,128)S(1)}, s32[16,12]{1,0:T(8,128)}, u32[]{:S(2)}) copy-start(s32[16,12]{1,0:T(8,128)} %far_ref.1) | copy-start | bytes 2308
  35.6 30.6 %copy-start.1 = (s32[16,12]{1,0:T(8,128)S(1)}, s32[16,12]{1,0:T(8,128)}, u32[]{:S(2)}) copy-start(s32[16,12]{1,0:T(8,128)} %near_ref.1) | copy-start | bytes 2308
  37.0 19.0 %all-to-all-start.1 = ((f32[32,8,128]{2,1,0:T(8,128)}), f32[32,8,128]{2,1,0:T(8,128)S(1)}, u32[]{:S(2)}, u32[]{:S(2)}) async-start(f32[32,8,128]{2,1,0:T(8,128)} %bitcast.10), calls=%async_computation.1 | async-start | bytes 262144 | tf_op jit(solution)/shard_map/all_to_all | solution.py:598
  59.6 21.5 %all-to-all-start.2 = ((f32[16,8,128]{2,1,0:T(8,128)}), f32[16,8,128]{2,1,0:T(8,128)S(1)}, u32[]{:S(2)}, u32[]{:S(2)}) async-start(f32[16,8,128]{2,1,0:T(8,128)} %bitcast.4), calls=%async_computation.2 | async-start | bytes 131072 | tf_op jit(solution)/shard_map/all_to_all | solution.py:608

commit v6 on v4

--- a/solution.py
+++ b/solution.py
@@ -130,7 +130,9 @@
     for half in range(2):
         lanes = slice(half * 256, half * 256 + 256)
         spread = [jnp.concatenate([piece[:, lanes] * keep[g] for g in range(8)], axis=0) for piece in pieces]
-        check = mm3(spread, (kern[0][:, lanes], kern[1][:, lanes]), dot_nt)
+        high, low = kern[0][:, lanes], kern[1][:, lanes]
+        spread = jnp.concatenate([spread[0], spread[1], spread[0]], axis=1)
+        check = dot_nt(spread, jnp.concatenate([high, high, low], axis=1))
         out.append(mm3(split(check), up))
     return out
 
@@ -305,9 +307,7 @@
     out_ref[...] = index_order(acc[0] + back)
 
 
-def local_kernel(x_ref, peers_ref, down_ref, col_ref, row_ref, up_hbm, out_ref, pad_ref, tab_ref, up_ref, sem):
-    move = pltpu.make_async_copy(up_hbm, up_ref, sem)
-    move.start()
+def local_kernel(x_ref, peers_ref, down_ref, col_ref, row_ref, out_ref, pad_ref, tab_ref):
     outer = lax.axis_index("outer")
     own = [p.astype(F32) for p in corner(outer * 256, 8)]
     cols = columns(col_ref)
@@ -327,19 +327,21 @@
     both = jnp.concatenate([check, check], axis=0)
     group = mm3(split(both[:, :SUB]), padded(down_ref, pad_ref, 200.0 / TERMS))[:8]
     pieces = jnp.concatenate(split(group[:, :SUB]), axis=0)
-    top = lax.broadcasted_iota(jnp.int32, (8, SUB), 0) < 4
-    move.wait()
-    found = []
-    for d in range(INNER):
-        part = dot_nt(pieces, up_ref[d, 0][:, :SUB]) + dot_nt(pieces, up_ref[d, 1][:, :SUB])
-        found.append(part[:8] + part[8:])
+    top = lax.broadcasted_iota(jnp.int32, (8, LANE), 0) < 4
+    found = [None] * INNER
+    for (x, y, z), kern in box_kernels(
+        (-2.0, 2.0), (-3.0, -1.0, 1.0, 3.0), (-1.0, 1.0), 3.0, 20.0, col_ref, row_ref, tab_ref
+    ):
+        high, low = split(kern)
+        part = dot(pieces, high) + dot(pieces, low)
+        found[(y & 1) + z * 2 + x * 4 + (y >> 1) * 8] = part[:8] + part[8:]
     merged = [jnp.where(top, found[2 * m], pltpu.roll(found[2 * m + 1], 4, 0)) for m in range(INNER // 2)]
-    total = jnp.concatenate(merged, axis=0) + peers_ref[:, :SUB]
-    out_ref[...] = pack(mm3(split(total), padded(down_ref, pad_ref, 60.0 / TERMS)))
+    total = jnp.concatenate(merged, axis=0) + peers_ref[...]
+    out_ref[...] = pack(mm3(split(total[:, :SUB]), padded(down_ref, pad_ref, 60.0 / TERMS)))
 
 
 def operator_kernel(
-    flow_ref, off_ref, down_ref, col_ref, row_ref, up_ref, w_hbm, m_hbm, up_hbm, w_ref, m_ref, pad_ref, tab_ref, sems
+    flow_ref, off_ref, down_ref, col_ref, row_ref, up_ref, w_hbm, m_hbm, w_ref, m_ref, pad_ref, tab_ref, sems
 ):
     for (x, y, z), kern in box_kernels(
         (2.0, -2.0), (3.0, 1.0, -1.0, -3.0), (1.0, -1.0), 20.0, 3.0, col_ref, row_ref, tab_ref
@@ -348,8 +350,6 @@
         high, low = split(kern)
         up_ref[e, 0, :, :] = high
         up_ref[e, 1, :, :] = low
-    up_move = pltpu.make_async_copy(up_ref, up_hbm, sems.at[2])
-    up_move.start()
     kern = split(leaf_kernel(off_ref[RHS : RHS + 3, :], col_ref))
     down = padded(down_ref, pad_ref, 18.0 / TERMS)
     down = (down[0][:, :SUB], down[1][:, :SUB])
@@ -374,7 +374,6 @@
         m_ref[1, :, lanes] = m_low
     m_move = pltpu.make_async_copy(m_ref, m_hbm, sems.at[1])
     m_move.start()
-    up_move.wait()
     w_move.wait()
     m_move.wait()
 
@@ -558,12 +557,11 @@
     )
     peers_equiv = lax.all_to_all(dev_equiv, "inner", 0, 0, tiled=True)
     leaf_maps = pltpu.HBM((2, SUB, POINTS), BF)
-    up_shape = (INNER, 2, SUB, LANE)
-    up_maps, weights, evaluate, up_copy = call(
-        operator_kernel, "evaluation_and_group_maps", (sds(up_shape, BF), leaf_maps, leaf_maps, pltpu.HBM(up_shape, BF)),
+    up_maps, weights, evaluate = call(
+        operator_kernel, "evaluation_and_group_maps", (sds((INNER, 2, SUB, LANE), BF), leaf_maps, leaf_maps),
         [VM, VM, VM, VM, VM],
-        [pltpu.VMEM((2, SUB, POINTS), BF), pltpu.VMEM((2, SUB, POINTS), BF), pad, tables(14), pltpu.SemaphoreType.DMA((3,))],
-        14, dev_equiv, own, downward, col, row, out_specs=(VM, HB, HB, HB),
+        [pltpu.VMEM((2, SUB, POINTS), BF), pltpu.VMEM((2, SUB, POINTS), BF), pad, tables(14), pltpu.SemaphoreType.DMA((2,))],
+        14, dev_equiv, own, downward, col, row, out_specs=(VM, HB, HB),
     )
     swap = lax.ppermute(own, "inner", [(i, i ^ 1) for i in range(INNER)])
     cross = lax.ppermute(own, "inner", [(i, ((i + 1) ^ 1) - 1) for i in range(1, INNER - 1)])
@@ -579,9 +577,8 @@
     )
     groups = tie(groups, peers_part)
     local = call(
-        local_kernel, "group_and_device_local", flow, [VM, VM, VM, VM, VM, HB],
-        [pad, tables(14), pltpu.VMEM(up_shape, BF), pltpu.SemaphoreType.DMA], 12,
-        groups, peers_part, downward, col, row, in_hbm(up_copy),
+        local_kernel, "group_and_device_local", flow, [VM, VM, VM, VM, VM], [pad, tables(14)], 8,
+        groups, peers_part, downward, col, row,
     )
     dev_local = lax.all_to_all(local, "inner", 0, 0, tiled=True)
     base, evaluate = call(

time: 72.4 us -> 71.2 us (0.983)
  Pallas kernels: 36.5 us -> 35.4 us
    pallas_call x7, Pallas kernels: 36.5 us -> 35.4 us  [call(): pl.pallas_call(kernel, name=name, out_shape=outs, in_specs=specs, out_spe...]
where the time goes in v6:
time: 71.2 us; the launch traced here: 70.8 us
  Pallas kernels  35.4 us (50%)
  starting transfers between devices  31.6 us (44%)
  waiting for transfers between devices  3.74 us (5%)
    pallas_call x7, Pallas kernels, call(): pl.pallas_call(kernel, name=name, out_shape=outs, in_specs=specs, out_spe...  35.4 us
    all_to_all x1, starting transfers between devices, shards(): peers_equiv = lax.all_to_all(dev_equiv, 'inner', 0, 0, tiled=True)  11.8 us
    all_to_all x1, starting transfers between devices, shards(): groups = lax.all_to_all(group_equiv, 'outer', 0, 0, tiled=True)  9.68 us
    all_to_all x1, starting transfers between devices, shards(): dev_local = lax.all_to_all(local, 'inner', 0, 0, tiled=True)  5.44 us
    all_to_all x1, waiting for transfers between devices, shards(): peers_equiv = lax.all_to_all(dev_equiv, 'inner', 0, 0, tiled=True)  3.54 us
    ppermute x1, starting transfers between devices, shards(): swap = lax.ppermute(own, 'inner', [(i, i ^ 1) for i in range(INNER)])  2.35 us
    ppermute x1, starting transfers between devices, shards(): lax.ppermute(own, 'inner', [(i, (i + 1 ^ 1) - 1) for i in range(1, INNER...  2.29 us
  transfers between devices with their start and end apart: 5, of which 2 were waited for; matrix products, arithmetic and copies ran while one was open for 0% of the time, Pallas kernels for 41%

profile of v6, /device:TPU:1, one launch (start us, length us, event | category | flops | bytes accessed | tf_op | source)
XLA Modules:
  0.0 70.8 jit_solution(9818383681658275841)
XLA Ops:
  0.0 0.0 copy-start
  0.0 0.0 copy-start.1
  0.0 4.4 %leaf_and_device_equiv.1 = (f32[128,128]{1,0:T(8,128)}, f32[72,512]{1,0:T(8,128)S(1)}, f32[165,165]{1,0:T(8,128)S(1)}, f32[165,165]{1,0:T(8,128)S(1)}, f32[176,1...) custom-call(f32[3,512]{1,0:T(4,128)} %off_hbm.1, f32[64,512]{1,0:T(8,128)} %q_hbm.1, s32[16]{0:T(128)} %counts_hbm.1, ...), custom_call_target="tpu_custom_call" | custom-call | flops 1000 | bytes 1000 | tf_op jit(solution)/shard_map/leaf_and_device_equiv/pallas_call | solution.py:511
  4.4 11.8 %all-to-all-start = ((f32[16,8,128]{2,1,0:T(8,128)}), f32[16,8,128]{2,1,0:T(8,128)S(1)}, u32[]{:S(2)}, u32[]{:S(2)}) async-start(f32[16,8,128]{2,1,0:T(8,128)} %bitcast), calls=%async_computation | async-start | bytes 131072 | tf_op jit(solution)/shard_map/all_to_all | solution.py:558
  16.2 4.3 %evaluation_and_group_maps.1 = (bf16[16,2,176,256]{3,2,1,0:T(8,128)(2,1)S(1)}, bf16[2,176,512]{2,1,0:T(8,128)(2,1)}, bf16[2,176,512]{2,1,0:T(8,128)(2,1)}) custom-call(f32[128,128]{1,0:T(8,128)} %get-tuple-element.18.flow_ref, f32[72,512]{1,0:T(8,128)S(1)} %get-tuple-element.19.off_ref.own_ref, f32[165,165]{1,0:T(8,128)S(1)} %get-tuple-element.20.down_ref, ...), custom_call_target="tpu_custom_call" | custom-call | flops 1000 | bytes 1000 | tf_op jit(solution)/shard_map/evaluation_and_group_maps/pallas_call | solution.py:511
  20.5 3.5 %all-to-all-done = f32[16,8,128]{2,1,0:T(8,128)S(1)} async-done(((f32[16,8,128]{2,1,0:T(8,128)}), f32[16,8,128]{2,1,0:T(8,128)S(1)}, u32[]{:S(2)}, u32[]{:S(2)}) %all-to-all-start) | async-done | bytes 65568 | tf_op jit(solution)/shard_map/all_to_all | solution.py:558
  24.1 1.4 %group_equiv.1 = f32[256,128]{1,0:T(8,128)} custom-call(f32[128,128]{1,0:T(8,128)S(1)} %bitcast.6, bf16[16,2,176,256]{3,2,1,0:T(8,128)(2,1)S(1)} %get-tuple-element.23.maps_ref, f32[165,165]{1,0:T(8,128)S(1)} %get-tuple-element.24.up_ref), custom_call_target="tpu_custom_call" | custom-call | flops 1000 | bytes 1000 | tf_op jit(solution)/shard_map/group_equiv/pallas_call | solution.py:511
  25.4 9.7 %all-to-all-start.1 = ((f32[32,8,128]{2,1,0:T(8,128)}), f32[32,8,128]{2,1,0:T(8,128)S(1)}, u32[]{:S(2)}, u32[]{:S(2)}) async-start(f32[32,8,128]{2,1,0:T(8,128)} %bitcast.10), calls=%async_computation.1 | async-start | bytes 262144 | tf_op jit(solution)/shard_map/all_to_all | solution.py:573
  35.1 2.4 %collective-permute-start = (f32[72,512]{1,0:T(8,128)S(1)}, f32[72,512]{1,0:T(8,128)S(1)}, u32[]{:S(2)}, u32[]{:S(2)}) collective-permute-start(f32[72,512]{1,0:T(8,128)S(1)} %get-tuple-element.19.off_ref.own_ref), channel_id=1, source_target_pairs={{0,1},{1,0},{2,3},{3,2},{4,5},{5,4},{6,7},{7,6},{8,9},{9,8},{10,11... | collective-permute-start | bytes 442376 | tf_op jit(solution)/shard_map/ppermute | solution.py:566
  37.5 2.3 %collective-permute-start.1 = (f32[72,512]{1,0:T(8,128)S(1)}, f32[72,512]{1,0:T(8,128)S(1)}, u32[]{:S(2)}, u32[]{:S(2)}) collective-permute-start(f32[72,512]{1,0:T(8,128)S(1)} %get-tuple-element.19.off_ref.own_ref), channel_id=1, source_target_pairs={{1,2},{2,1},{3,4},{4,3},{5,6},{6,5},{7,8},{8,7},{9,10},{10,9},{11,... | collective-permute-start | bytes 442376 | tf_op jit(solution)/shard_map/ppermute | solution.py:567
  39.8 4.3 %device_to_device.1.peers_ref = f32[64,256]{1,0:T(8,128)S(1)} custom-call(f32[128,128]{1,0:T(8,128)S(1)} %bitcast.7, f32[176,128]{1,0:T(8,128)S(1)} %get-tuple-element.21.col_ref, f32[8,256]{1,0:T(8,128)S(1)} %get-tuple-element.22.row_ref), custom_call_target="tpu_custom_call" | custom-call | flops 1000 | bytes 1000 | tf_op jit(solution)/shard_map/device_to_device/pallas_call | solution.py:511
  44.1 0.2 all-to-all-done.1
  44.3 3.7 %group_and_device_local.1 = f32[128,128]{1,0:T(8,128)} custom-call(f32[256,128]{1,0:T(8,128)S(1)} %bitcast.8, f32[64,256]{1,0:T(8,128)S(1)} %device_to_device.1.peers_ref, f32[165,165]{1,0:T(8,128)S(1)} %get-tuple-element.20.down_ref, f32[176,128]{1,0:T(8,128)S(1)} %get-tuple-element.21.col_ref, f32[8,256]{1,0:T(8,128)S(1)} %get-tuple-element.22.row_ref), custom_call_target="tpu_custom_call" | custom-call | flops 1000 | bytes 1000 | tf_op jit(solution)/shard_map/group_and_device_local/pallas_call | solution.py:511
  48.0 5.4 %all-to-all-start.2 = ((f32[16,8,128]{2,1,0:T(8,128)}), f32[16,8,128]{2,1,0:T(8,128)S(1)}, u32[]{:S(2)}, u32[]{:S(2)}) async-start(f32[16,8,128]{2,1,0:T(8,128)} %bitcast.4), calls=%async_computation.2 | async-start | bytes 131072 | tf_op jit(solution)/shard_map/all_to_all | solution.py:583
  53.4 0.0 collective-permute-done.swap_ref
  53.4 0.0 collective-permute-done.1.cross_ref
  53.4 0.0 copy-done
  53.4 0.0 copy-done.1
  53.5 16.5 %near_and_far_field.1 = (f32[64,512]{1,0:T(8,128)S(1)}, bf16[2,176,512]{2,1,0:T(8,128)(2,1)S(1)}) custom-call(s32[16,12]{1,0:T(8,128)S(1)} %copy-done, s32[16,12]{1,0:T(8,128)S(1)} %copy-done.1, f32[72,512]{1,0:T(8,128)S(1)} %get-tuple-element.19.off_ref.own_ref, f32[72,512]{1,0:T(8,128)S(1)} %collective-permute-done.swap_ref, ...), custom_call_target="tpu_custom_call" | custom-call | flops 1000 | bytes 1000 | tf_op jit(solution)/shard_map/near_and_far_field/pallas_call | solution.py:511
  70.0 0.0 all-to-all-done.2
  70.0 0.9 %potential.1 = f32[64,512]{1,0:T(8,128)} custom-call(f32[128,128]{1,0:T(8,128)S(1)} %bitcast.9, f32[64,512]{1,0:T(8,128)S(1)} %get-tuple-element.29.base_ref, bf16[2,176,512]{2,1,0:T(8,128)(2,1)S(1)} %get-tuple-element.30.m_ref), custom_call_target="tpu_custom_call" | custom-call | flops 1000 | bytes 1000 | tf_op jit(solution)/shard_map/potential/pallas_call | solution.py:511
Async XLA Ops:
  0.0 53.4 %copy-start = (s32[16,12]{1,0:T(8,128)S(1)}, s32[16,12]{1,0:T(8,128)}, u32[]{:S(2)}) copy-start(s32[16,12]{1,0:T(8,128)} %far_ref.1) | copy-start | bytes 2308
  0.0 53.4 %copy-start.1 = (s32[16,12]{1,0:T(8,128)S(1)}, s32[16,12]{1,0:T(8,128)}, u32[]{:S(2)}) copy-start(s32[16,12]{1,0:T(8,128)} %near_ref.1) | copy-start | bytes 2308
  4.4 19.7 %all-to-all-start = ((f32[16,8,128]{2,1,0:T(8,128)}), f32[16,8,128]{2,1,0:T(8,128)S(1)}, u32[]{:S(2)}, u32[]{:S(2)}) async-start(f32[16,8,128]{2,1,0:T(8,128)} %bitcast), calls=%async_computation | async-start | bytes 131072 | tf_op jit(solution)/shard_map/all_to_all | solution.py:558
  25.4 18.8 %all-to-all-start.1 = ((f32[32,8,128]{2,1,0:T(8,128)}), f32[32,8,128]{2,1,0:T(8,128)S(1)}, u32[]{:S(2)}, u32[]{:S(2)}) async-start(f32[32,8,128]{2,1,0:T(8,128)} %bitcast.10), calls=%async_computation.1 | async-start | bytes 262144 | tf_op jit(solution)/shard_map/all_to_all | solution.py:573
  35.1 18.3 %collective-permute-start = (f32[72,512]{1,0:T(8,128)S(1)}, f32[72,512]{1,0:T(8,128)S(1)}, u32[]{:S(2)}, u32[]{:S(2)}) collective-permute-start(f32[72,512]{1,0:T(8,128)S(1)} %get-tuple-element.19.off_ref.own_ref), channel_id=1, source_target_pairs={{0,1},{1,0},{2,3},{3,2},{4,5},{5,4},{6,7},{7,6},{8,9},{9,8},{10,11... | collective-permute-start | bytes 442376 | tf_op jit(solution)/shard_map/ppermute | solution.py:566
  37.5 15.9 %collective-permute-start.1 = (f32[72,512]{1,0:T(8,128)S(1)}, f32[72,512]{1,0:T(8,128)S(1)}, u32[]{:S(2)}, u32[]{:S(2)}) collective-permute-start(f32[72,512]{1,0:T(8,128)S(1)} %get-tuple-element.19.off_ref.own_ref), channel_id=1, source_target_pairs={{1,2},{2,1},{3,4},{4,3},{5,6},{6,5},{7,8},{8,7},{9,10},{10,9},{11,... | collective-permute-start | bytes 442376 | tf_op jit(solution)/shard_map/ppermute | solution.py:567
  48.0 22.0 %all-to-all-start.2 = ((f32[16,8,128]{2,1,0:T(8,128)}), f32[16,8,128]{2,1,0:T(8,128)S(1)}, u32[]{:S(2)}, u32[]{:S(2)}) async-start(f32[16,8,128]{2,1,0:T(8,128)} %bitcast.4), calls=%async_computation.2 | async-start | bytes 131072 | tf_op jit(solution)/shard_map/all_to_all | solution.py:583

commit v7 on v6

--- a/solution.py
+++ b/solution.py
@@ -21,6 +21,8 @@
 INNER = 16
 OUTER = 32
 PART = RHS // INNER
+EARLY = 6
+HALF_E = LEAVES * 2 * RHS
 BF = jnp.bfloat16
 F32 = jnp.float32
 
@@ -419,30 +421,73 @@
     out_ref[...] = flipped[:RHS] + flipped[RHS:]
 
 
-def field_kernel(
-    far_ref, near_ref, own_ref, swap_ref, cross_ref, up_ref, col_ref, row_ref, w_hbm, m_hbm, e_hbm, out_ref, m_ref,
-    pad_ref, e_ref, dl_ref, xtab_ref, tab_ref, w_ref, left_ref, right_ref, mask_ref, high_ref, low_ref, sems,
-):
-    middle = LEAVES * 2 * RHS
-    moves = [
-        pltpu.make_async_copy(e_hbm, e_ref.at[middle : 2 * middle], sems.at[0]),
-        pltpu.make_async_copy(w_hbm, w_ref, sems.at[1]),
-        pltpu.make_async_copy(m_hbm, m_ref, sems.at[2]),
-    ]
-    for move in moves:
-        move.start()
+def side_moves(sources, places, sems):
+    return [pltpu.make_async_copy(src, dst, sems.at[n]) for n, (src, dst) in enumerate(zip(sources, places))]
+
+
+def from_sides(own_ref, up_ref, col_ref, out_ref, e_ref, starts, work):
+    near_ref, swap_ref, cross_ref, pad_ref, left_ref, right_ref, mask_ref, high_ref, low_ref = work
     odd = lax.rem(lax.axis_index("inner"), 2) == 1
     left_ref[...] = jnp.where(odd, swap_ref[...], cross_ref[...])
     right_ref[...] = jnp.where(odd, cross_ref[...], swap_ref[...])
     near_field(near_ref, left_ref, own_ref, right_ref, out_ref, mask_ref, high_ref, low_ref)
+    up = padded(up_ref, pad_ref, 18.0 / TERMS)
+    for start, ref in zip(starts, (left_ref, right_ref)):
+        kern = split(leaf_kernel(ref[RHS : RHS + 3, :], col_ref))
+        store_equivalents(leaf_equivalents(ref[0:RHS, :], kern, up), e_ref, start)
+
+
+def early_kernel(
+    own_ref, up_ref, col_ref, near_hbm, swap_ref, cross_ref, base_hbm, e_hbm, swap_hbm, cross_hbm,
+    base_ref, e_ref, near_ref, *work
+):
+    *work, sems, keep_sems = work
+    keeps = side_moves((swap_ref, cross_ref), (swap_hbm, cross_hbm), keep_sems)
+    for move in keeps:
+        move.start()
+    work = (near_ref, swap_ref, cross_ref, *work)
+
+    @pl.when(lax.axis_index("inner") < EARLY)
+    def _():
+        for step in ("start", "wait"):
+            for move in side_moves((near_hbm,), (near_ref,), sems):
+                getattr(move, step)()
+        from_sides(own_ref, up_ref, col_ref, base_ref, e_ref, (0, HALF_E), work)
+        for step in ("start", "wait"):
+            for move in side_moves((base_ref, e_ref), (base_hbm, e_hbm), sems):
+                getattr(move, step)()
+
+    for move in keeps:
+        move.wait()
+
+
+def field_kernel(
+    far_ref, own_ref, up_ref, col_ref, row_ref, near_hbm, swap_hbm, cross_hbm, w_hbm, m_hbm, e_hbm, base_hbm, sides_hbm,
+    out_ref, m_ref, e_ref, dl_ref, xtab_ref, tab_ref, w_ref, *work,
+):
+    *work, sems, early_sems, late_sems = work
     inner = lax.axis_index("inner")
     device = lax.axis_index("outer") * INNER + inner
-    up = padded(up_ref, pad_ref, 18.0 / TERMS)
-    for side, ref in ((0, left_ref), (2, right_ref)):
-        kern = split(leaf_kernel(ref[RHS : RHS + 3, :], col_ref))
-        store_equivalents(leaf_equivalents(ref[0:RHS, :], kern, up), e_ref, side * middle)
+    moves = side_moves((e_hbm, w_hbm, m_hbm), (e_ref.at[HALF_E : 2 * HALF_E], w_ref, m_ref), sems)
+    early = side_moves(
+        (base_hbm, sides_hbm.at[0:HALF_E], sides_hbm.at[HALF_E : 2 * HALF_E]),
+        (out_ref, e_ref.at[0:HALF_E], e_ref.at[2 * HALF_E : 3 * HALF_E]),
+        early_sems,
+    )
+    late = side_moves((near_hbm, swap_hbm, cross_hbm), work, late_sems)
     for move in moves:
-        move.wait()
+        move.start()
+
+    @pl.when(inner < EARLY)
+    def _():
+        for move in early:
+            move.start()
+
+    @pl.when(inner >= EARLY)
+    def _():
+        for move in late:
+            move.start()
+
     first = (device - 1) * LEAVES
     boxes = [corner((device + side) * LEAVES, 4) for side in (-1, 0, 1)]
     boxes = [[(boxes[1][c] - box[c]).astype(F32) for c in range(3)] for box in boxes]
@@ -456,6 +501,20 @@
             ysq = square_of(1, boxes[side][1] + (b - 1.0), 0.9, 1.8, cols, row_ref)
             for c in range(3):
                 tab_ref[side * 9 + b * 3 + c] = ysq + tab_ref[27 + c]
+
+    @pl.when(inner < EARLY)
+    def _():
+        for move in early:
+            move.wait()
+
+    @pl.when(inner >= EARLY)
+    def _():
+        for move in late:
+            move.wait()
+        from_sides(own_ref, up_ref, col_ref, out_ref, e_ref, (0, 2 * HALF_E), work)
+
+    for move in moves:
+        move.wait()
 
     def one_leaf(g, carry):
         own = local_leaf(g)
@@ -555,7 +614,31 @@
         ],
         16, *map(in_hbm, inputs), out_specs=(VM, VM, VM, VM, VM, VM, HB),
     )
-    peers_equiv = lax.all_to_all(dev_equiv, "inner", 0, 0, tiled=True)
+    swap = lax.ppermute(own, "inner", [(i, i ^ 1) for i in range(INNER)])
+    cross = lax.ppermute(own, "inner", [(i, ((i + 1) ^ 1) - 1) for i in range(1, INNER - 1)])
+    points = pltpu.VMEM((ROWS, POINTS), F32)
+    spread = pltpu.VMEM((POINTS, 3 * POINTS), BF)
+    side = [
+        pltpu.VMEM((LEAVES, 12), jnp.int32),
+        points,
+        points,
+        pad,
+        points,
+        points,
+        pltpu.VMEM((LEAVES, 3 * POINTS), F32),
+        spread,
+        spread,
+    ]
+    dma = pltpu.SemaphoreType.DMA((3,))
+    near = in_hbm(near)
+    halo = pltpu.HBM((ROWS, POINTS), F32)
+    early_base, early_sides, swap, cross = call(
+        early_kernel, "early_near_field", (pltpu.HBM((RHS, POINTS), F32), pltpu.HBM((2 * HALF_E, LANE), BF), halo, halo),
+        [VM, VM, VM, HB, VM, VM],
+        [pltpu.VMEM((RHS, POINTS), F32), pltpu.VMEM((2 * HALF_E, LANE), BF), side[0], *side[3:], dma, dma],
+        20, own, upward, col, near, swap, cross, out_specs=(HB, HB, HB, HB),
+    )
+    peers_equiv = lax.all_to_all(tie(dev_equiv, early_base, early_sides), "inner", 0, 0, tiled=True)
     leaf_maps = pltpu.HBM((2, SUB, POINTS), BF)
     up_maps, weights, evaluate = call(
         operator_kernel, "evaluation_and_group_maps", (sds((INNER, 2, SUB, LANE), BF), leaf_maps, leaf_maps),
@@ -563,8 +646,6 @@
         [pltpu.VMEM((2, SUB, POINTS), BF), pltpu.VMEM((2, SUB, POINTS), BF), pad, tables(14), pltpu.SemaphoreType.DMA((2,))],
         14, dev_equiv, own, downward, col, row, out_specs=(VM, HB, HB),
     )
-    swap = lax.ppermute(own, "inner", [(i, i ^ 1) for i in range(INNER)])
-    cross = lax.ppermute(own, "inner", [(i, ((i + 1) ^ 1) - 1) for i in range(1, INNER - 1)])
     group_equiv = call(
         group_up_kernel, "group_equiv", pltpu.HBM((8 * OUTER, 128), F32), [VM, VM, VM],
         [pad, pltpu.VMEM((8 * OUTER, 128), F32), pltpu.SemaphoreType.DMA], 6,
@@ -583,22 +664,20 @@
     dev_local = lax.all_to_all(local, "inner", 0, 0, tiled=True)
     base, evaluate = call(
         field_kernel, "near_and_far_field", (sds((RHS, POINTS), F32), sds((2, SUB, POINTS), BF)),
-        [SM, VM, VM, VM, VM, VM, VM, VM, HB, HB, HB],
+        [SM, VM, VM, VM, VM, HB, HB, HB, HB, HB, HB, HB, HB],
         [
-            pad,
-            pltpu.VMEM((3 * LEAVES * 2 * RHS, LANE), BF),
+            pltpu.VMEM((3 * HALF_E, LANE), BF),
             pltpu.VMEM((2, LEAVES * RHS, LANE), BF),
             tables(21),
             tables(30),
             pltpu.VMEM((2, SUB, POINTS), BF),
-            pltpu.VMEM((ROWS, POINTS), F32),
-            pltpu.VMEM((ROWS, POINTS), F32),
-            pltpu.VMEM((LEAVES, 3 * POINTS), F32),
-            pltpu.VMEM((POINTS, 3 * POINTS), BF),
-            pltpu.VMEM((POINTS, 3 * POINTS), BF),
-            pltpu.SemaphoreType.DMA((3,)),
+            *side,
+            dma,
+            dma,
+            dma,
         ],
-        32, far, near, own, swap, cross, upward, col, row, in_hbm(weights), in_hbm(evaluate), in_hbm(equiv),
+        32, far, own, upward, col, row, near, *map(in_hbm, (swap, cross)),
+        *map(in_hbm, (weights, evaluate, equiv, early_base, early_sides)),
     )
     return call(tail_kernel, "potential", sds((RHS, POINTS), F32), [VM, VM, VM], [], 4, dev_local, base, evaluate)
 

time: 71.2 us -> 79.4 us (1.12)
  waiting for transfers between devices: 3.74 us -> 11.1 us
  Pallas kernels: 35.4 us -> 39.2 us
  starting transfers between devices: 31.6 us -> 28.3 us
    all_to_all x1, starting transfers between devices: 11.8 us -> 3.41 us  [shards(): lax.all_to_all(tie(dev_equiv, early_base, early_sides), 'inner', 0, 0, ti...]
    ppermute x1, starting transfers between devices: 2.35 us -> 8.79 us  [shards(): swap = lax.ppermute(own, 'inner', [(i, i ^ 1) for i in range(INNER)])]
    ppermute x1, waiting for transfers between devices: 0.01 us -> 4.52 us  [shards(): lax.ppermute(own, 'inner', [(i, (i + 1 ^ 1) - 1) for i in range(1, INNER...]
    all_to_all x1, waiting for transfers between devices: 0.2 us -> 4.67 us  [shards(): groups = lax.all_to_all(group_equiv, 'outer', 0, 0, tiled=True)]
    pallas_call x7 -> x8, Pallas kernels: 35.4 us -> 39.2 us  [call(): pl.pallas_call(kernel, name=name, out_shape=outs, in_specs=specs, out_spe...]
    all_to_all x1, waiting for transfers between devices: 3.54 us -> 1.93 us  [shards(): lax.all_to_all(tie(dev_equiv, early_base, early_sides), 'inner', 0, 0, ti...]
    all_to_all x1, starting transfers between devices: 9.68 us -> 8.74 us  [shards(): groups = lax.all_to_all(group_equiv, 'outer', 0, 0, tiled=True)]
  transfers between devices with their start and end apart: 5 -> 5, of which waited for: 2 -> 3; matrix products, arithmetic and copies ran while one was open for 0% -> 0% of each run, Pallas kernels for 41% -> 29%
where the time goes in v7:
time: 79.4 us; the launch traced here: 78.7 us
  Pallas kernels  39.2 us (49%)
  starting transfers between devices  28.3 us (36%)
  waiting for transfers between devices  11.1 us (14%)
    pallas_call x8, Pallas kernels, call(): pl.pallas_call(kernel, name=name, out_shape=outs, in_specs=specs, out_spe...  39.2 us
    ppermute x1, starting transfers between devices, shards(): swap = lax.ppermute(own, 'inner', [(i, i ^ 1) for i in range(INNER)])  8.79 us
    all_to_all x1, starting transfers between devices, shards(): groups = lax.all_to_all(group_equiv, 'outer', 0, 0, tiled=True)  8.74 us
    all_to_all x1, starting transfers between devices, shards(): dev_local = lax.all_to_all(local, 'inner', 0, 0, tiled=True)  5.44 us
    all_to_all x1, waiting for transfers between devices, shards(): groups = lax.all_to_all(group_equiv, 'outer', 0, 0, tiled=True)  4.67 us
    ppermute x1, waiting for transfers between devices, shards(): lax.ppermute(own, 'inner', [(i, (i + 1 ^ 1) - 1) for i in range(1, INNER...  4.52 us
    all_to_all x1, starting transfers between devices, shards(): lax.all_to_all(tie(dev_equiv, early_base, early_sides), 'inner', 0, 0, ti...  3.41 us
    all_to_all x1, waiting for transfers between devices, shards(): lax.all_to_all(tie(dev_equiv, early_base, early_sides), 'inner', 0, 0, ti...  1.93 us
  transfers between devices with their start and end apart: 5, of which 3 were waited for; matrix products, arithmetic and copies ran while one was open for 0% of the time, Pallas kernels for 29%

profile of v7, /device:TPU:1, one launch (start us, length us, event | category | flops | bytes accessed | tf_op | source)
XLA Modules:
  0.0 78.7 jit_solution(15702927505547170856)
XLA Ops:
  0.0 4.4 %leaf_and_device_equiv.1 = (f32[128,128]{1,0:T(8,128)}, f32[72,512]{1,0:T(8,128)S(1)}, f32[165,165]{1,0:T(8,128)S(1)}, f32[165,165]{1,0:T(8,128)S(1)}, f32[176,1...) custom-call(f32[3,512]{1,0:T(4,128)} %off_hbm.1, f32[64,512]{1,0:T(8,128)} %q_hbm.1, s32[16]{0:T(128)} %counts_hbm.1, ...), custom_call_target="tpu_custom_call" | custom-call | flops 1000 | bytes 1000 | tf_op jit(solution)/shard_map/leaf_and_device_equiv/pallas_call | solution.py:570
  4.4 8.8 %collective-permute-start = (f32[72,512]{1,0:T(8,128)S(1)}, f32[72,512]{1,0:T(8,128)S(1)}, u32[]{:S(2)}, u32[]{:S(2)}) collective-permute-start(f32[72,512]{1,0:T(8,128)S(1)} %get-tuple-element.24.own_ref.off_ref), channel_id=1, source_target_pairs={{0,1},{1,0},{2,3},{3,2},{4,5},{5,4},{6,7},{7,6},{8,9},{9,8},{10,11... | collective-permute-start | bytes 442376 | tf_op jit(solution)/shard_map/ppermute | solution.py:617
  13.2 1.9 %collective-permute-start.1 = (f32[72,512]{1,0:T(8,128)S(1)}, f32[72,512]{1,0:T(8,128)S(1)}, u32[]{:S(2)}, u32[]{:S(2)}) collective-permute-start(f32[72,512]{1,0:T(8,128)S(1)} %get-tuple-element.24.own_ref.off_ref), channel_id=1, source_target_pairs={{1,2},{2,1},{3,4},{4,3},{5,6},{6,5},{7,8},{8,7},{9,10},{10,9},{11,... | collective-permute-start | bytes 442376 | tf_op jit(solution)/shard_map/ppermute | solution.py:618
  15.1 0.0 collective-permute-done.swap_ref
  15.1 4.5 %collective-permute-done.1.cross_ref = f32[72,512]{1,0:T(8,128)S(1)} collective-permute-done((f32[72,512]{1,0:T(8,128)S(1)}, f32[72,512]{1,0:T(8,128)S(1)}, u32[]{:S(2)}, u32[]{:S(2)}) %collective-permute-start.1) | collective-permute-done | bytes 147488 | tf_op jit(solution)/shard_map/ppermute | solution.py:618
  19.6 0.0 copy-start
  19.6 6.2 %early_near_field.1 = (f32[64,512]{1,0:T(8,128)}, bf16[4096,256]{1,0:T(8,128)(2,1)}, f32[72,512]{1,0:T(8,128)}, f32[72,512]{1,0:T(8,128)}) custom-call(f32[72,512]{1,0:T(8,128)S(1)} %get-tuple-element.24.own_ref.off_ref, f32[165,165]{1,0:T(8,128)S(1)} %get-tuple-element.25.up_ref, f32[176,128]{1,0:T(8,128)S(1)} %get-tuple-element.26.col_ref, ...), custom_call_target="tpu_custom_call" | custom-call | flops 1000 | bytes 1000 | tf_op jit(solution)/shard_map/early_near_field/pallas_call | solution.py:570
  25.9 3.4 %all-to-all-start = ((f32[16,8,128]{2,1,0:T(8,128)}), f32[16,8,128]{2,1,0:T(8,128)S(1)}, u32[]{:S(2)}, u32[]{:S(2)}) async-start(f32[16,8,128]{2,1,0:T(8,128)} %bitcast), calls=%async_computation | async-start | bytes 131072 | tf_op jit(solution)/shard_map/all_to_all | solution.py:641
  29.3 4.3 %evaluation_and_group_maps.1 = (bf16[16,2,176,256]{3,2,1,0:T(8,128)(2,1)S(1)}, bf16[2,176,512]{2,1,0:T(8,128)(2,1)}, bf16[2,176,512]{2,1,0:T(8,128)(2,1)}) custom-call(f32[128,128]{1,0:T(8,128)} %get-tuple-element.29.flow_ref, f32[72,512]{1,0:T(8,128)S(1)} %get-tuple-element.24.own_ref.off_ref, f32[165,165]{1,0:T(8,128)S(1)} %get-tuple-element.30.down_ref, ...), custom_call_target="tpu_custom_call" | custom-call | flops 1000 | bytes 1000 | tf_op jit(solution)/shard_map/evaluation_and_group_maps/pallas_call | solution.py:570
  33.6 1.9 %all-to-all-done = f32[16,8,128]{2,1,0:T(8,128)S(1)} async-done(((f32[16,8,128]{2,1,0:T(8,128)}), f32[16,8,128]{2,1,0:T(8,128)S(1)}, u32[]{:S(2)}, u32[]{:S(2)}) %all-to-all-start) | async-done | bytes 65568 | tf_op jit(solution)/shard_map/all_to_all | solution.py:641
  35.5 1.4 %group_equiv.1 = f32[256,128]{1,0:T(8,128)} custom-call(f32[128,128]{1,0:T(8,128)S(1)} %bitcast.6, bf16[16,2,176,256]{3,2,1,0:T(8,128)(2,1)S(1)} %get-tuple-element.32.maps_ref, f32[165,165]{1,0:T(8,128)S(1)} %get-tuple-element.25.up_ref), custom_call_target="tpu_custom_call" | custom-call | flops 1000 | bytes 1000 | tf_op jit(solution)/shard_map/group_equiv/pallas_call | solution.py:570
  36.9 8.7 %all-to-all-start.1 = ((f32[32,8,128]{2,1,0:T(8,128)}), f32[32,8,128]{2,1,0:T(8,128)S(1)}, u32[]{:S(2)}, u32[]{:S(2)}) async-start(f32[32,8,128]{2,1,0:T(8,128)} %bitcast.10), calls=%async_computation.1 | async-start | bytes 262144 | tf_op jit(solution)/shard_map/all_to_all | solution.py:654
  45.6 4.3 %device_to_device.1.peers_ref = f32[64,256]{1,0:T(8,128)S(1)} custom-call(f32[128,128]{1,0:T(8,128)S(1)} %bitcast.7, f32[176,128]{1,0:T(8,128)S(1)} %get-tuple-element.26.col_ref, f32[8,256]{1,0:T(8,128)S(1)} %get-tuple-element.31.row_ref), custom_call_target="tpu_custom_call" | custom-call | flops 1000 | bytes 1000 | tf_op jit(solution)/shard_map/device_to_device/pallas_call | solution.py:570
  49.9 4.7 %all-to-all-done.1 = f32[32,8,128]{2,1,0:T(8,128)S(1)} async-done(((f32[32,8,128]{2,1,0:T(8,128)}), f32[32,8,128]{2,1,0:T(8,128)S(1)}, u32[]{:S(2)}, u32[]{:S(2)}) %all-to-all-start.1) | async-done | bytes 131104 | tf_op jit(solution)/shard_map/all_to_all | solution.py:654
  54.6 3.7 %group_and_device_local.1 = f32[128,128]{1,0:T(8,128)} custom-call(f32[256,128]{1,0:T(8,128)S(1)} %bitcast.8, f32[64,256]{1,0:T(8,128)S(1)} %device_to_device.1.peers_ref, f32[165,165]{1,0:T(8,128)S(1)} %get-tuple-element.30.down_ref, f32[176,128]{1,0:T(8,128)S(1)} %get-tuple-element.26.col_ref, f32[8,256]{1,0:T(8,128)S(1)} %get-tuple-element.31.row_ref), custom_call_target="tpu_custom_call" | custom-call | flops 1000 | bytes 1000 | tf_op jit(solution)/shard_map/group_and_device_local/pallas_call | solution.py:570
  58.3 5.4 %all-to-all-start.2 = ((f32[16,8,128]{2,1,0:T(8,128)}), f32[16,8,128]{2,1,0:T(8,128)S(1)}, u32[]{:S(2)}, u32[]{:S(2)}) async-start(f32[16,8,128]{2,1,0:T(8,128)} %bitcast.4), calls=%async_computation.2 | async-start | bytes 131072 | tf_op jit(solution)/shard_map/all_to_all | solution.py:664
  63.7 0.0 copy-done
  63.7 14.1 %near_and_far_field.1 = (f32[64,512]{1,0:T(8,128)S(1)}, bf16[2,176,512]{2,1,0:T(8,128)(2,1)S(1)}) custom-call(s32[16,12]{1,0:T(8,128)S(1)} %copy-done, f32[72,512]{1,0:T(8,128)S(1)} %get-tuple-element.24.own_ref.off_ref, f32[165,165]{1,0:T(8,128)S(1)} %get-tuple-element.25.up_ref, f32[176,128]{1,0:T(8,128)S(1)} %get-tuple-element.26.col_ref, ...), custom_call_target="tpu_custom_call" | custom-call | flops 1000 | bytes 1000 | tf_op jit(solution)/shard_map/near_and_far_field/pallas_call | solution.py:570
  77.8 0.0 all-to-all-done.2
  77.8 0.9 %potential.1 = f32[64,512]{1,0:T(8,128)} custom-call(f32[128,128]{1,0:T(8,128)S(1)} %bitcast.9, f32[64,512]{1,0:T(8,128)S(1)} %get-tuple-element.39.base_ref, bf16[2,176,512]{2,1,0:T(8,128)(2,1)S(1)} %get-tuple-element.40.m_ref), custom_call_target="tpu_custom_call" | custom-call | flops 1000 | bytes 1000 | tf_op jit(solution)/shard_map/potential/pallas_call | solution.py:570
Async XLA Ops:
  4.4 10.7 %collective-permute-start = (f32[72,512]{1,0:T(8,128)S(1)}, f32[72,512]{1,0:T(8,128)S(1)}, u32[]{:S(2)}, u32[]{:S(2)}) collective-permute-start(f32[72,512]{1,0:T(8,128)S(1)} %get-tuple-element.24.own_ref.off_ref), channel_id=1, source_target_pairs={{0,1},{1,0},{2,3},{3,2},{4,5},{5,4},{6,7},{7,6},{8,9},{9,8},{10,11... | collective-permute-start | bytes 442376 | tf_op jit(solution)/shard_map/ppermute | solution.py:617
  13.2 6.5 %collective-permute-start.1 = (f32[72,512]{1,0:T(8,128)S(1)}, f32[72,512]{1,0:T(8,128)S(1)}, u32[]{:S(2)}, u32[]{:S(2)}) collective-permute-start(f32[72,512]{1,0:T(8,128)S(1)} %get-tuple-element.24.own_ref.off_ref), channel_id=1, source_target_pairs={{1,2},{2,1},{3,4},{4,3},{5,6},{6,5},{7,8},{8,7},{9,10},{10,9},{11,... | collective-permute-start | bytes 442376 | tf_op jit(solution)/shard_map/ppermute | solution.py:618
  19.6 44.1 %copy-start = (s32[16,12]{1,0:T(8,128)S(1)}, s32[16,12]{1,0:T(8,128)}, u32[]{:S(2)}) copy-start(s32[16,12]{1,0:T(8,128)} %far_ref.1) | copy-start | bytes 2308
  25.9 9.6 %all-to-all-start = ((f32[16,8,128]{2,1,0:T(8,128)}), f32[16,8,128]{2,1,0:T(8,128)S(1)}, u32[]{:S(2)}, u32[]{:S(2)}) async-start(f32[16,8,128]{2,1,0:T(8,128)} %bitcast), calls=%async_computation | async-start | bytes 131072 | tf_op jit(solution)/shard_map/all_to_all | solution.py:641
  36.9 17.7 %all-to-all-start.1 = ((f32[32,8,128]{2,1,0:T(8,128)}), f32[32,8,128]{2,1,0:T(8,128)S(1)}, u32[]{:S(2)}, u32[]{:S(2)}) async-start(f32[32,8,128]{2,1,0:T(8,128)} %bitcast.10), calls=%async_computation.1 | async-start | bytes 262144 | tf_op jit(solution)/shard_map/all_to_all | solution.py:654
  58.3 19.5 %all-to-all-start.2 = ((f32[16,8,128]{2,1,0:T(8,128)}), f32[16,8,128]{2,1,0:T(8,128)S(1)}, u32[]{:S(2)}, u32[]{:S(2)}) async-start(f32[16,8,128]{2,1,0:T(8,128)} %bitcast.4), calls=%async_computation.2 | async-start | bytes 131072 | tf_op jit(solution)/shard_map/all_to_all | solution.py:664

commit v8 on v6

--- a/solution.py
+++ b/solution.py
@@ -290,9 +290,16 @@
         start = RHS - (dx * 2 + dz) * 16 - 4 * (dy - q)
         keep = two(jnp.broadcast_to(mask[:, dy + 3 : dy + 4], (RHS, 128))).astype(BF)
         rows = [(shifted_ref[q, n, start : start + RHS, :] * keep)[:, :SUB] for n in range(2)]
-        return rows
-
-    acc = (jnp.zeros((RHS, LANE), F32), jnp.zeros((RHS, SUB), F32))
+        return jnp.concatenate(rows, axis=0)
+
+    def add(acc, rows, kern, f):
+        return acc[0] + f(rows, kern[0]), acc[1] + f(rows[:RHS], kern[1])
+
+    def fold(acc):
+        return acc[0][:RHS] + acc[0][RHS:] + acc[1]
+
+    ahead_sum = (jnp.zeros((2 * RHS, LANE), F32), jnp.zeros((RHS, LANE), F32))
+    behind_sum = (jnp.zeros((2 * RHS, SUB), F32), jnp.zeros((RHS, SUB), F32))
     planes = [(0, 0, (1, 2, 3))] + [(dx, dz, range(-3, 4)) for dx, dz in ((0, 1), (1, -1), (1, 0), (1, 1))]
     for n, (dx, dz, steps) in enumerate(planes):
         plane = square_of(0, dx * 4.0, 3.0, 3.0, cols, row_ref)
@@ -300,11 +307,11 @@
         ahead, behind = valid(dx, dz), valid(-dx, -dz)
         for dy in steps:
             kern = split(lax.rsqrt(tab_ref[7 + n] + tab_ref[dy + 3]))
-            forward = acc[0] + mm3(moved(dx, dy, dz, ahead), kern)
+            ahead_sum = add(ahead_sum, moved(dx, dy, dz, ahead), kern, dot)
             kern = (kern[0][:, :SUB], kern[1][:, :SUB])
-            acc = (forward, acc[1] + mm3(moved(-dx, -dy, -dz, behind), kern, dot_nt))
-    back = jnp.concatenate([acc[1], jnp.zeros((RHS, LANE - SUB), F32)], axis=1)
-    out_ref[...] = index_order(acc[0] + back)
+            behind_sum = add(behind_sum, moved(-dx, -dy, -dz, behind), kern, dot_nt)
+    back = jnp.concatenate([fold(behind_sum), jnp.zeros((RHS, LANE - SUB), F32)], axis=1)
+    out_ref[...] = index_order(fold(ahead_sum) + back)
 
 
 def local_kernel(x_ref, peers_ref, down_ref, col_ref, row_ref, out_ref, pad_ref, tab_ref):
@@ -385,11 +392,10 @@
     base = (device - 1) * LEAVES
     total = 3 * POINTS
     lane = lax.broadcasted_iota(jnp.int32, (LEAVES, total), 1) // SLOTS
-    found = jnp.zeros((LEAVES, total), F32)
+    found = jnp.full((LEAVES, total), jnp.inf, F32)
     near = near_ref[...] - base
     for k in range(12):
-        found = jnp.where(lane == near[:, k : k + 1], 1.0, found)
-    mask_ref[...] = found
+        found = jnp.where(lane == near[:, k : k + 1], SOFTEN, found)
     leaf = lax.broadcasted_iota(jnp.int32, (1, POINTS), 1) // SLOTS
     within = local_leaf(leaf)
     own_box = corner(device * LEAVES, 4)
@@ -400,14 +406,16 @@
             box = corner((device + side) * LEAVES, 4)[c] - own_box[c]
             lanes.append(ref[RHS + c : RHS + c + 1, :] + (box + within[c]).astype(F32))
         sources.append(jnp.concatenate(lanes, axis=1))
+    norms = sources[0] * sources[0] + sources[1] * sources[1] + sources[2] * sources[2]
+    mask_ref[...] = found + norms
     for g in range(LEAVES):
         rows = slice(g * SLOTS, g * SLOTS + SLOTS)
         place = local_leaf(g)
-        dist = SOFTEN
+        target = [offs[rows, c : c + 1] + float(place[c]) for c in range(3)]
+        dist = mask_ref[g : g + 1, :] + (target[0] * target[0] + target[1] * target[1] + target[2] * target[2])
         for c in range(3):
-            diff = (offs[rows, c : c + 1] + float(place[c])) - sources[c]
-            dist = dist + diff * diff
-        k_high, k_low = split(lax.rsqrt(dist) * mask_ref[g : g + 1, :])
+            dist = dist + (-2.0 * target[c]) * sources[c]
+        k_high, k_low = split(lax.rsqrt(dist))
         high_ref[rows, :] = k_high
         low_ref[rows, :] = k_low
     charges = jnp.concatenate([r[0:RHS, :] for r in (left_ref, own_ref, right_ref)], axis=1)
@@ -498,8 +506,9 @@
 
 
 def tail_kernel(x_ref, base_ref, m_ref, out_ref):
-    local = split(unpack(x_ref[...])[:, :SUB])
-    out_ref[...] = base_ref[...] + mm3(local, (m_ref[0], m_ref[1]))
+    high, low = split(unpack(x_ref[...])[:, :SUB])
+    wide = dot(jnp.concatenate([high, low], axis=0), m_ref[0])
+    out_ref[...] = base_ref[...] + wide[:RHS] + wide[RHS:] + dot(high, m_ref[1])
 
 
 VM = pl.BlockSpec(memory_space=pltpu.VMEM)

time: 71.2 us -> 71.3 us (level)
  waiting for transfers between devices: 3.74 us -> 4.96 us
  Pallas kernels: 35.4 us -> 34.3 us
    all_to_all x1, waiting for transfers between devices: 0.2 us -> 1.41 us  [shards(): groups = lax.all_to_all(group_equiv, 'outer', 0, 0, tiled=True)]
    pallas_call x7, Pallas kernels: 35.4 us -> 34.3 us  [call(): pl.pallas_call(kernel, name=name, out_shape=outs, in_specs=specs, out_spe...]
  transfers between devices with their start and end apart: 5 -> 5, of which waited for: 2 -> 2; matrix products, arithmetic and copies ran while one was open for 0% -> 0% of each run, Pallas kernels for 41% -> 39%
where the time goes in v8:
time: 71.3 us; the launch traced here: 71 us
  Pallas kernels  34.3 us (48%)
  starting transfers between devices  31.6 us (44%)
  waiting for transfers between devices  4.96 us (7%)
    pallas_call x7, Pallas kernels, call(): pl.pallas_call(kernel, name=name, out_shape=outs, in_specs=specs, out_spe...  34.3 us
    all_to_all x1, starting transfers between devices, shards(): peers_equiv = lax.all_to_all(dev_equiv, 'inner', 0, 0, tiled=True)  11.8 us
    all_to_all x1, starting transfers between devices, shards(): groups = lax.all_to_all(group_equiv, 'outer', 0, 0, tiled=True)  9.68 us
    all_to_all x1, starting transfers between devices, shards(): dev_local = lax.all_to_all(local, 'inner', 0, 0, tiled=True)  5.57 us
    all_to_all x1, waiting for transfers between devices, shards(): peers_equiv = lax.all_to_all(dev_equiv, 'inner', 0, 0, tiled=True)  3.54 us
    ppermute x1, starting transfers between devices, shards(): swap = lax.ppermute(own, 'inner', [(i, i ^ 1) for i in range(INNER)])  2.35 us
    ppermute x1, starting transfers between devices, shards(): lax.ppermute(own, 'inner', [(i, (i + 1 ^ 1) - 1) for i in range(1, INNER...  2.11 us
  transfers between devices with their start and end apart: 5, of which 2 were waited for; matrix products, arithmetic and copies ran while one was open for 0% of the time, Pallas kernels for 39%

profile of v8, /device:TPU:1, one launch (start us, length us, event | category | flops | bytes accessed | tf_op | source)
XLA Modules:
  0.0 71.0 jit_solution(11373971400589369898)
XLA Ops:
  0.0 0.0 copy-start
  0.0 0.0 copy-start.1
  0.0 4.4 %leaf_and_device_equiv.1 = (f32[128,128]{1,0:T(8,128)}, f32[72,512]{1,0:T(8,128)S(1)}, f32[165,165]{1,0:T(8,128)S(1)}, f32[165,165]{1,0:T(8,128)S(1)}, f32[176,1...) custom-call(f32[3,512]{1,0:T(4,128)} %off_hbm.1, f32[64,512]{1,0:T(8,128)} %q_hbm.1, s32[16]{0:T(128)} %counts_hbm.1, ...), custom_call_target="tpu_custom_call" | custom-call | flops 1000 | bytes 1000 | tf_op jit(solution)/shard_map/leaf_and_device_equiv/pallas_call | solution.py:520
  4.4 11.8 %all-to-all-start = ((f32[16,8,128]{2,1,0:T(8,128)}), f32[16,8,128]{2,1,0:T(8,128)S(1)}, u32[]{:S(2)}, u32[]{:S(2)}) async-start(f32[16,8,128]{2,1,0:T(8,128)} %bitcast), calls=%async_computation | async-start | bytes 131072 | tf_op jit(solution)/shard_map/all_to_all | solution.py:567
  16.2 4.3 %evaluation_and_group_maps.1 = (bf16[16,2,176,256]{3,2,1,0:T(8,128)(2,1)S(1)}, bf16[2,176,512]{2,1,0:T(8,128)(2,1)}, bf16[2,176,512]{2,1,0:T(8,128)(2,1)}) custom-call(f32[128,128]{1,0:T(8,128)} %get-tuple-element.18.flow_ref, f32[72,512]{1,0:T(8,128)S(1)} %get-tuple-element.19.off_ref.own_ref, f32[165,165]{1,0:T(8,128)S(1)} %get-tuple-element.20.down_ref, ...), custom_call_target="tpu_custom_call" | custom-call | flops 1000 | bytes 1000 | tf_op jit(solution)/shard_map/evaluation_and_group_maps/pallas_call | solution.py:520
  20.5 3.5 %all-to-all-done = f32[16,8,128]{2,1,0:T(8,128)S(1)} async-done(((f32[16,8,128]{2,1,0:T(8,128)}), f32[16,8,128]{2,1,0:T(8,128)S(1)}, u32[]{:S(2)}, u32[]{:S(2)}) %all-to-all-start) | async-done | bytes 65568 | tf_op jit(solution)/shard_map/all_to_all | solution.py:567
  24.1 1.4 %group_equiv.1 = f32[256,128]{1,0:T(8,128)} custom-call(f32[128,128]{1,0:T(8,128)S(1)} %bitcast.6, bf16[16,2,176,256]{3,2,1,0:T(8,128)(2,1)S(1)} %get-tuple-element.23.maps_ref, f32[165,165]{1,0:T(8,128)S(1)} %get-tuple-element.24.up_ref), custom_call_target="tpu_custom_call" | custom-call | flops 1000 | bytes 1000 | tf_op jit(solution)/shard_map/group_equiv/pallas_call | solution.py:520
  25.4 9.7 %all-to-all-start.1 = ((f32[32,8,128]{2,1,0:T(8,128)}), f32[32,8,128]{2,1,0:T(8,128)S(1)}, u32[]{:S(2)}, u32[]{:S(2)}) async-start(f32[32,8,128]{2,1,0:T(8,128)} %bitcast.10), calls=%async_computation.1 | async-start | bytes 262144 | tf_op jit(solution)/shard_map/all_to_all | solution.py:582
  35.1 2.4 %collective-permute-start = (f32[72,512]{1,0:T(8,128)S(1)}, f32[72,512]{1,0:T(8,128)S(1)}, u32[]{:S(2)}, u32[]{:S(2)}) collective-permute-start(f32[72,512]{1,0:T(8,128)S(1)} %get-tuple-element.19.off_ref.own_ref), channel_id=1, source_target_pairs={{0,1},{1,0},{2,3},{3,2},{4,5},{5,4},{6,7},{7,6},{8,9},{9,8},{10,11... | collective-permute-start | bytes 442376 | tf_op jit(solution)/shard_map/ppermute | solution.py:575
  37.5 2.1 %collective-permute-start.1 = (f32[72,512]{1,0:T(8,128)S(1)}, f32[72,512]{1,0:T(8,128)S(1)}, u32[]{:S(2)}, u32[]{:S(2)}) collective-permute-start(f32[72,512]{1,0:T(8,128)S(1)} %get-tuple-element.19.off_ref.own_ref), channel_id=1, source_target_pairs={{1,2},{2,1},{3,4},{4,3},{5,6},{6,5},{7,8},{8,7},{9,10},{10,9},{11,... | collective-permute-start | bytes 442376 | tf_op jit(solution)/shard_map/ppermute | solution.py:576
  39.6 3.3 %device_to_device.1.peers_ref = f32[64,256]{1,0:T(8,128)S(1)} custom-call(f32[128,128]{1,0:T(8,128)S(1)} %bitcast.7, f32[176,128]{1,0:T(8,128)S(1)} %get-tuple-element.21.col_ref, f32[8,256]{1,0:T(8,128)S(1)} %get-tuple-element.22.row_ref), custom_call_target="tpu_custom_call" | custom-call | flops 1000 | bytes 1000 | tf_op jit(solution)/shard_map/device_to_device/pallas_call | solution.py:520
  42.9 1.4 %all-to-all-done.1 = f32[32,8,128]{2,1,0:T(8,128)S(1)} async-done(((f32[32,8,128]{2,1,0:T(8,128)}), f32[32,8,128]{2,1,0:T(8,128)S(1)}, u32[]{:S(2)}, u32[]{:S(2)}) %all-to-all-start.1) | async-done | bytes 131104 | tf_op jit(solution)/shard_map/all_to_all | solution.py:582
  44.3 3.7 %group_and_device_local.1 = f32[128,128]{1,0:T(8,128)} custom-call(f32[256,128]{1,0:T(8,128)S(1)} %bitcast.8, f32[64,256]{1,0:T(8,128)S(1)} %device_to_device.1.peers_ref, f32[165,165]{1,0:T(8,128)S(1)} %get-tuple-element.20.down_ref, f32[176,128]{1,0:T(8,128)S(1)} %get-tuple-element.21.col_ref, f32[8,256]{1,0:T(8,128)S(1)} %get-tuple-element.22.row_ref), custom_call_target="tpu_custom_call" | custom-call | flops 1000 | bytes 1000 | tf_op jit(solution)/shard_map/group_and_device_local/pallas_call | solution.py:520
  48.0 5.6 %all-to-all-start.2 = ((f32[16,8,128]{2,1,0:T(8,128)}), f32[16,8,128]{2,1,0:T(8,128)S(1)}, u32[]{:S(2)}, u32[]{:S(2)}) async-start(f32[16,8,128]{2,1,0:T(8,128)} %bitcast.4), calls=%async_computation.2 | async-start | bytes 131072 | tf_op jit(solution)/shard_map/all_to_all | solution.py:592
  53.6 0.0 collective-permute-done.swap_ref
  53.6 0.0 collective-permute-done.1.cross_ref
  53.6 0.0 copy-done
  53.6 0.0 copy-done.1
  53.6 16.5 %near_and_far_field.1 = (f32[64,512]{1,0:T(8,128)S(1)}, bf16[2,176,512]{2,1,0:T(8,128)(2,1)S(1)}) custom-call(s32[16,12]{1,0:T(8,128)S(1)} %copy-done, s32[16,12]{1,0:T(8,128)S(1)} %copy-done.1, f32[72,512]{1,0:T(8,128)S(1)} %get-tuple-element.19.off_ref.own_ref, f32[72,512]{1,0:T(8,128)S(1)} %collective-permute-done.swap_ref, ...), custom_call_target="tpu_custom_call" | custom-call | flops 1000 | bytes 1000 | tf_op jit(solution)/shard_map/near_and_far_field/pallas_call | solution.py:520
  70.1 0.0 all-to-all-done.2
  70.1 0.9 %potential.1 = f32[64,512]{1,0:T(8,128)} custom-call(f32[128,128]{1,0:T(8,128)S(1)} %bitcast.9, f32[64,512]{1,0:T(8,128)S(1)} %get-tuple-element.29.base_ref, bf16[2,176,512]{2,1,0:T(8,128)(2,1)S(1)} %get-tuple-element.30.m_ref), custom_call_target="tpu_custom_call" | custom-call | flops 1000 | bytes 1000 | tf_op jit(solution)/shard_map/potential/pallas_call | solution.py:520
Async XLA Ops:
  0.0 53.6 %copy-start = (s32[16,12]{1,0:T(8,128)S(1)}, s32[16,12]{1,0:T(8,128)}, u32[]{:S(2)}) copy-start(s32[16,12]{1,0:T(8,128)} %far_ref.1) | copy-start | bytes 2308
  0.0 53.6 %copy-start.1 = (s32[16,12]{1,0:T(8,128)S(1)}, s32[16,12]{1,0:T(8,128)}, u32[]{:S(2)}) copy-start(s32[16,12]{1,0:T(8,128)} %near_ref.1) | copy-start | bytes 2308
  4.4 19.7 %all-to-all-start = ((f32[16,8,128]{2,1,0:T(8,128)}), f32[16,8,128]{2,1,0:T(8,128)S(1)}, u32[]{:S(2)}, u32[]{:S(2)}) async-start(f32[16,8,128]{2,1,0:T(8,128)} %bitcast), calls=%async_computation | async-start | bytes 131072 | tf_op jit(solution)/shard_map/all_to_all | solution.py:567
  25.4 18.8 %all-to-all-start.1 = ((f32[32,8,128]{2,1,0:T(8,128)}), f32[32,8,128]{2,1,0:T(8,128)S(1)}, u32[]{:S(2)}, u32[]{:S(2)}) async-start(f32[32,8,128]{2,1,0:T(8,128)} %bitcast.10), calls=%async_computation.1 | async-start | bytes 262144 | tf_op jit(solution)/shard_map/all_to_all | solution.py:582
  35.1 18.4 %collective-permute-start = (f32[72,512]{1,0:T(8,128)S(1)}, f32[72,512]{1,0:T(8,128)S(1)}, u32[]{:S(2)}, u32[]{:S(2)}) collective-permute-start(f32[72,512]{1,0:T(8,128)S(1)} %get-tuple-element.19.off_ref.own_ref), channel_id=1, source_target_pairs={{0,1},{1,0},{2,3},{3,2},{4,5},{5,4},{6,7},{7,6},{8,9},{9,8},{10,11... | collective-permute-start | bytes 442376 | tf_op jit(solution)/shard_map/ppermute | solution.py:575
  37.5 16.1 %collective-permute-start.1 = (f32[72,512]{1,0:T(8,128)S(1)}, f32[72,512]{1,0:T(8,128)S(1)}, u32[]{:S(2)}, u32[]{:S(2)}) collective-permute-start(f32[72,512]{1,0:T(8,128)S(1)} %get-tuple-element.19.off_ref.own_ref), channel_id=1, source_target_pairs={{1,2},{2,1},{3,4},{4,3},{5,6},{6,5},{7,8},{8,7},{9,10},{10,9},{11,... | collective-permute-start | bytes 442376 | tf_op jit(solution)/shard_map/ppermute | solution.py:576
  48.0 22.1 %all-to-all-start.2 = ((f32[16,8,128]{2,1,0:T(8,128)}), f32[16,8,128]{2,1,0:T(8,128)S(1)}, u32[]{:S(2)}, u32[]{:S(2)}) async-start(f32[16,8,128]{2,1,0:T(8,128)} %bitcast.4), calls=%async_computation.2 | async-start | bytes 131072 | tf_op jit(solution)/shard_map/all_to_all | solution.py:592

commit v9 on v8

--- a/solution.py
+++ b/solution.py
@@ -68,7 +68,7 @@
     return diff * diff
 
 
-def box_kernels(xs, ys, zs, radius_t, radius_i, col_ref, row_ref, tab_ref):
+def box_tables(xs, ys, zs, radius_t, radius_i, col_ref, row_ref, tab_ref):
     cols = columns(col_ref)
     for n, shift in enumerate(xs):
         tab_ref[n] = square_of(0, shift, radius_t, radius_i, cols, row_ref)
@@ -80,10 +80,18 @@
         ysq = square_of(1, shift, radius_t, radius_i, cols, row_ref)
         for c in range(len(zs)):
             tab_ref[start + b * len(zs) + c] = ysq + tab_ref[zsq + c]
-    for b in range(len(ys)):
-        for c in range(len(zs)):
-            for a in range(len(xs)):
-                yield (a, b, c), lax.rsqrt(tab_ref[a] + tab_ref[start + b * len(zs) + c])
+
+
+def box_pairs(nx, ny, nz, tab_ref):
+    for b in range(ny):
+        for c in range(nz):
+            for a in range(nx):
+                yield (a, b, c), lax.rsqrt(tab_ref[a] + tab_ref[nx + nz + b * nz + c])
+
+
+def box_kernels(xs, ys, zs, radius_t, radius_i, col_ref, row_ref, tab_ref):
+    box_tables(xs, ys, zs, radius_t, radius_i, col_ref, row_ref, tab_ref)
+    yield from box_pairs(len(xs), len(ys), len(zs), tab_ref)
 
 
 def bits(ids, low, axis, top=14):
@@ -204,7 +212,10 @@
     ]
     for move in moves:
         move.start()
-    for move in moves[:-1]:
+    moves[4].wait()
+    moves[5].wait()
+    box_tables((1.5, 0.5, -0.5, -1.5), (0.5, -0.5), (0.5, -0.5), 6.0, 0.9, col_ref, row_ref, tab_ref)
+    for move in moves[:4]:
         move.wait()
     lane = lax.broadcasted_iota(jnp.int32, (8, POINTS), 1)
     limit = jnp.zeros((8, POINTS), jnp.int32)
@@ -223,15 +234,12 @@
     e_move = pltpu.make_async_copy(e_ref, e_hbm, sems.at[7])
     e_move.start()
     acc = jnp.zeros((RHS, LANE), F32)
-    for (x, y, z), kern in box_kernels(
-        (1.5, 0.5, -0.5, -1.5), (0.5, -0.5), (0.5, -0.5), 6.0, 0.9, col_ref, row_ref, tab_ref
-    ):
+    for (x, y, z), kern in box_pairs(4, 2, 2, tab_ref):
         start = ((x >> 1) * 8 + (x & 1) + 2 * y + 4 * z) * 2 * RHS
         high, low = split(kern)
         wide = dot(e_ref[start : start + 2 * RHS, :][:, :SUB], high)
         acc = acc + wide[:RHS] + wide[RHS:] + dot(e_ref[start : start + RHS, :][:, :SUB], low)
-    up60 = padded(up_ref, pad_ref, 60.0 / TERMS)
-    out_ref[...] = pack(mm3(split(acc[:, :SUB]), up60))
+    out_ref[...] = pack(mm3(split(acc[:, :SUB] * (60.0 / 18.0)), up))
     moves[-1].wait()
     e_move.wait()
 
@@ -332,7 +340,8 @@
         acc = tile_dot(x_ref[8 * p : 8 * p + 8, :] * weight, kern[0], kern[1], acc)
     check = tile_sum(acc)
     both = jnp.concatenate([check, check], axis=0)
-    group = mm3(split(both[:, :SUB]), padded(down_ref, pad_ref, 200.0 / TERMS))[:8]
+    down = padded(down_ref, pad_ref, 60.0 / TERMS)
+    group = mm3(split(both[:, :SUB] * (200.0 / 60.0)), down)[:8]
     pieces = jnp.concatenate(split(group[:, :SUB]), axis=0)
     top = lax.broadcasted_iota(jnp.int32, (8, LANE), 0) < 4
     found = [None] * INNER
@@ -344,7 +353,7 @@
         found[(y & 1) + z * 2 + x * 4 + (y >> 1) * 8] = part[:8] + part[8:]
     merged = [jnp.where(top, found[2 * m], pltpu.roll(found[2 * m + 1], 4, 0)) for m in range(INNER // 2)]
     total = jnp.concatenate(merged, axis=0) + peers_ref[...]
-    out_ref[...] = pack(mm3(split(total[:, :SUB]), padded(down_ref, pad_ref, 60.0 / TERMS)))
+    out_ref[...] = pack(mm3(split(total[:, :SUB]), down))
 
 
 def operator_kernel(
@@ -392,10 +401,11 @@
     base = (device - 1) * LEAVES
     total = 3 * POINTS
     lane = lax.broadcasted_iota(jnp.int32, (LEAVES, total), 1) // SLOTS
-    found = jnp.full((LEAVES, total), jnp.inf, F32)
+    found = jnp.zeros((LEAVES, total), F32)
     near = near_ref[...] - base
     for k in range(12):
-        found = jnp.where(lane == near[:, k : k + 1], SOFTEN, found)
+        found = jnp.where(lane == near[:, k : k + 1], 1.0, found)
+    mask_ref[...] = found
     leaf = lax.broadcasted_iota(jnp.int32, (1, POINTS), 1) // SLOTS
     within = local_leaf(leaf)
     own_box = corner(device * LEAVES, 4)
@@ -406,16 +416,14 @@
             box = corner((device + side) * LEAVES, 4)[c] - own_box[c]
             lanes.append(ref[RHS + c : RHS + c + 1, :] + (box + within[c]).astype(F32))
         sources.append(jnp.concatenate(lanes, axis=1))
-    norms = sources[0] * sources[0] + sources[1] * sources[1] + sources[2] * sources[2]
-    mask_ref[...] = found + norms
     for g in range(LEAVES):
         rows = slice(g * SLOTS, g * SLOTS + SLOTS)
         place = local_leaf(g)
-        target = [offs[rows, c : c + 1] + float(place[c]) for c in range(3)]
-        dist = mask_ref[g : g + 1, :] + (target[0] * target[0] + target[1] * target[1] + target[2] * target[2])
+        dist = SOFTEN
         for c in range(3):
-            dist = dist + (-2.0 * target[c]) * sources[c]
-        k_high, k_low = split(lax.rsqrt(dist))
+            diff = (offs[rows, c : c + 1] + float(place[c])) - sources[c]
+            dist = dist + diff * diff
+        k_high, k_low = split(lax.rsqrt(dist) * mask_ref[g : g + 1, :])
         high_ref[rows, :] = k_high
         low_ref[rows, :] = k_low
     charges = jnp.concatenate([r[0:RHS, :] for r in (left_ref, own_ref, right_ref)], axis=1)

time: 71.3 us -> 71.5 us (level)
  no operation moved by 1% of the time
where the time goes in v9:
time: 71.5 us; the launch traced here: 71.1 us
  Pallas kernels  34.5 us (48%)
  starting transfers between devices  31.6 us (44%)
  waiting for transfers between devices  4.97 us (7%)
    pallas_call x7, Pallas kernels, call(): pl.pallas_call(kernel, name=name, out_shape=outs, in_specs=specs, out_spe...  34.5 us
    all_to_all x1, starting transfers between devices, shards(): peers_equiv = lax.all_to_all(dev_equiv, 'inner', 0, 0, tiled=True)  11.8 us
    all_to_all x1, starting transfers between devices, shards(): groups = lax.all_to_all(group_equiv, 'outer', 0, 0, tiled=True)  9.68 us
    all_to_all x1, starting transfers between devices, shards(): dev_local = lax.all_to_all(local, 'inner', 0, 0, tiled=True)  5.57 us
    all_to_all x1, waiting for transfers between devices, shards(): peers_equiv = lax.all_to_all(dev_equiv, 'inner', 0, 0, tiled=True)  3.54 us
    ppermute x1, starting transfers between devices, shards(): swap = lax.ppermute(own, 'inner', [(i, i ^ 1) for i in range(INNER)])  2.35 us
    ppermute x1, starting transfers between devices, shards(): lax.ppermute(own, 'inner', [(i, (i + 1 ^ 1) - 1) for i in range(1, INNER...  2.11 us
  transfers between devices with their start and end apart: 5, of which 2 were waited for; matrix products, arithmetic and copies ran while one was open for 0% of the time, Pallas kernels for 39%

profile of v9, /device:TPU:1, one launch (start us, length us, event | category | flops | bytes accessed | tf_op | source)
XLA Modules:
  0.0 71.1 jit_solution(3360458905820726833)
XLA Ops:
  0.0 0.0 copy-start
  0.0 0.0 copy-start.1
  0.0 4.6 %leaf_and_device_equiv.1 = (f32[128,128]{1,0:T(8,128)}, f32[72,512]{1,0:T(8,128)S(1)}, f32[165,165]{1,0:T(8,128)S(1)}, f32[165,165]{1,0:T(8,128)S(1)}, f32[176,1...) custom-call(f32[3,512]{1,0:T(4,128)} %off_hbm.1, f32[64,512]{1,0:T(8,128)} %q_hbm.1, s32[16]{0:T(128)} %counts_hbm.1, ...), custom_call_target="tpu_custom_call" | custom-call | flops 1000 | bytes 1000 | tf_op jit(solution)/shard_map/leaf_and_device_equiv/pallas_call | solution.py:528
  4.6 11.8 %all-to-all-start = ((f32[16,8,128]{2,1,0:T(8,128)}), f32[16,8,128]{2,1,0:T(8,128)S(1)}, u32[]{:S(2)}, u32[]{:S(2)}) async-start(f32[16,8,128]{2,1,0:T(8,128)} %bitcast), calls=%async_computation | async-start | bytes 131072 | tf_op jit(solution)/shard_map/all_to_all | solution.py:575
  16.4 4.3 %evaluation_and_group_maps.1 = (bf16[16,2,176,256]{3,2,1,0:T(8,128)(2,1)S(1)}, bf16[2,176,512]{2,1,0:T(8,128)(2,1)}, bf16[2,176,512]{2,1,0:T(8,128)(2,1)}) custom-call(f32[128,128]{1,0:T(8,128)} %get-tuple-element.18.flow_ref, f32[72,512]{1,0:T(8,128)S(1)} %get-tuple-element.19.off_ref.own_ref, f32[165,165]{1,0:T(8,128)S(1)} %get-tuple-element.20.down_ref, ...), custom_call_target="tpu_custom_call" | custom-call | flops 1000 | bytes 1000 | tf_op jit(solution)/shard_map/evaluation_and_group_maps/pallas_call | solution.py:528
  20.7 3.5 %all-to-all-done = f32[16,8,128]{2,1,0:T(8,128)S(1)} async-done(((f32[16,8,128]{2,1,0:T(8,128)}), f32[16,8,128]{2,1,0:T(8,128)S(1)}, u32[]{:S(2)}, u32[]{:S(2)}) %all-to-all-start) | async-done | bytes 65568 | tf_op jit(solution)/shard_map/all_to_all | solution.py:575
  24.2 1.4 %group_equiv.1 = f32[256,128]{1,0:T(8,128)} custom-call(f32[128,128]{1,0:T(8,128)S(1)} %bitcast.6, bf16[16,2,176,256]{3,2,1,0:T(8,128)(2,1)S(1)} %get-tuple-element.23.maps_ref, f32[165,165]{1,0:T(8,128)S(1)} %get-tuple-element.24.up_ref), custom_call_target="tpu_custom_call" | custom-call | flops 1000 | bytes 1000 | tf_op jit(solution)/shard_map/group_equiv/pallas_call | solution.py:528
  25.6 9.7 %all-to-all-start.1 = ((f32[32,8,128]{2,1,0:T(8,128)}), f32[32,8,128]{2,1,0:T(8,128)S(1)}, u32[]{:S(2)}, u32[]{:S(2)}) async-start(f32[32,8,128]{2,1,0:T(8,128)} %bitcast.10), calls=%async_computation.1 | async-start | bytes 262144 | tf_op jit(solution)/shard_map/all_to_all | solution.py:590
  35.3 2.4 %collective-permute-start = (f32[72,512]{1,0:T(8,128)S(1)}, f32[72,512]{1,0:T(8,128)S(1)}, u32[]{:S(2)}, u32[]{:S(2)}) collective-permute-start(f32[72,512]{1,0:T(8,128)S(1)} %get-tuple-element.19.off_ref.own_ref), channel_id=1, source_target_pairs={{0,1},{1,0},{2,3},{3,2},{4,5},{5,4},{6,7},{7,6},{8,9},{9,8},{10,11... | collective-permute-start | bytes 442376 | tf_op jit(solution)/shard_map/ppermute | solution.py:583
  37.7 2.1 %collective-permute-start.1 = (f32[72,512]{1,0:T(8,128)S(1)}, f32[72,512]{1,0:T(8,128)S(1)}, u32[]{:S(2)}, u32[]{:S(2)}) collective-permute-start(f32[72,512]{1,0:T(8,128)S(1)} %get-tuple-element.19.off_ref.own_ref), channel_id=1, source_target_pairs={{1,2},{2,1},{3,4},{4,3},{5,6},{6,5},{7,8},{8,7},{9,10},{10,9},{11,... | collective-permute-start | bytes 442376 | tf_op jit(solution)/shard_map/ppermute | solution.py:584
  39.8 3.2 %device_to_device.1.peers_ref = f32[64,256]{1,0:T(8,128)S(1)} custom-call(f32[128,128]{1,0:T(8,128)S(1)} %bitcast.7, f32[176,128]{1,0:T(8,128)S(1)} %get-tuple-element.21.col_ref, f32[8,256]{1,0:T(8,128)S(1)} %get-tuple-element.22.row_ref), custom_call_target="tpu_custom_call" | custom-call | flops 1000 | bytes 1000 | tf_op jit(solution)/shard_map/device_to_device/pallas_call | solution.py:528
  43.0 1.4 %all-to-all-done.1 = f32[32,8,128]{2,1,0:T(8,128)S(1)} async-done(((f32[32,8,128]{2,1,0:T(8,128)}), f32[32,8,128]{2,1,0:T(8,128)S(1)}, u32[]{:S(2)}, u32[]{:S(2)}) %all-to-all-start.1) | async-done | bytes 131104 | tf_op jit(solution)/shard_map/all_to_all | solution.py:590
  44.5 3.7 %group_and_device_local.1 = f32[128,128]{1,0:T(8,128)} custom-call(f32[256,128]{1,0:T(8,128)S(1)} %bitcast.8, f32[64,256]{1,0:T(8,128)S(1)} %device_to_device.1.peers_ref, f32[165,165]{1,0:T(8,128)S(1)} %get-tuple-element.20.down_ref, f32[176,128]{1,0:T(8,128)S(1)} %get-tuple-element.21.col_ref, f32[8,256]{1,0:T(8,128)S(1)} %get-tuple-element.22.row_ref), custom_call_target="tpu_custom_call" | custom-call | flops 1000 | bytes 1000 | tf_op jit(solution)/shard_map/group_and_device_local/pallas_call | solution.py:528
  48.1 5.6 %all-to-all-start.2 = ((f32[16,8,128]{2,1,0:T(8,128)}), f32[16,8,128]{2,1,0:T(8,128)S(1)}, u32[]{:S(2)}, u32[]{:S(2)}) async-start(f32[16,8,128]{2,1,0:T(8,128)} %bitcast.4), calls=%async_computation.2 | async-start | bytes 131072 | tf_op jit(solution)/shard_map/all_to_all | solution.py:600
  53.7 0.0 collective-permute-done.swap_ref
  53.7 0.0 collective-permute-done.1.cross_ref
  53.7 0.0 copy-done
  53.7 0.0 copy-done.1
  53.8 16.5 %near_and_far_field.1 = (f32[64,512]{1,0:T(8,128)S(1)}, bf16[2,176,512]{2,1,0:T(8,128)(2,1)S(1)}) custom-call(s32[16,12]{1,0:T(8,128)S(1)} %copy-done, s32[16,12]{1,0:T(8,128)S(1)} %copy-done.1, f32[72,512]{1,0:T(8,128)S(1)} %get-tuple-element.19.off_ref.own_ref, f32[72,512]{1,0:T(8,128)S(1)} %collective-permute-done.swap_ref, ...), custom_call_target="tpu_custom_call" | custom-call | flops 1000 | bytes 1000 | tf_op jit(solution)/shard_map/near_and_far_field/pallas_call | solution.py:528
  70.3 0.0 all-to-all-done.2
  70.3 0.9 %potential.1 = f32[64,512]{1,0:T(8,128)} custom-call(f32[128,128]{1,0:T(8,128)S(1)} %bitcast.9, f32[64,512]{1,0:T(8,128)S(1)} %get-tuple-element.29.base_ref, bf16[2,176,512]{2,1,0:T(8,128)(2,1)S(1)} %get-tuple-element.30.m_ref), custom_call_target="tpu_custom_call" | custom-call | flops 1000 | bytes 1000 | tf_op jit(solution)/shard_map/potential/pallas_call | solution.py:528
Async XLA Ops:
  0.0 53.7 %copy-start = (s32[16,12]{1,0:T(8,128)S(1)}, s32[16,12]{1,0:T(8,128)}, u32[]{:S(2)}) copy-start(s32[16,12]{1,0:T(8,128)} %far_ref.1) | copy-start | bytes 2308
  0.0 53.7 %copy-start.1 = (s32[16,12]{1,0:T(8,128)S(1)}, s32[16,12]{1,0:T(8,128)}, u32[]{:S(2)}) copy-start(s32[16,12]{1,0:T(8,128)} %near_ref.1) | copy-start | bytes 2308
  4.6 19.6 %all-to-all-start = ((f32[16,8,128]{2,1,0:T(8,128)}), f32[16,8,128]{2,1,0:T(8,128)S(1)}, u32[]{:S(2)}, u32[]{:S(2)}) async-start(f32[16,8,128]{2,1,0:T(8,128)} %bitcast), calls=%async_computation | async-start | bytes 131072 | tf_op jit(solution)/shard_map/all_to_all | solution.py:575
  25.6 18.8 %all-to-all-start.1 = ((f32[32,8,128]{2,1,0:T(8,128)}), f32[32,8,128]{2,1,0:T(8,128)S(1)}, u32[]{:S(2)}, u32[]{:S(2)}) async-start(f32[32,8,128]{2,1,0:T(8,128)} %bitcast.10), calls=%async_computation.1 | async-start | bytes 262144 | tf_op jit(solution)/shard_map/all_to_all | solution.py:590
  35.3 18.4 %collective-permute-start = (f32[72,512]{1,0:T(8,128)S(1)}, f32[72,512]{1,0:T(8,128)S(1)}, u32[]{:S(2)}, u32[]{:S(2)}) collective-permute-start(f32[72,512]{1,0:T(8,128)S(1)} %get-tuple-element.19.off_ref.own_ref), channel_id=1, source_target_pairs={{0,1},{1,0},{2,3},{3,2},{4,5},{5,4},{6,7},{7,6},{8,9},{9,8},{10,11... | collective-permute-start | bytes 442376 | tf_op jit(solution)/shard_map/ppermute | solution.py:583
  37.7 16.0 %collective-permute-start.1 = (f32[72,512]{1,0:T(8,128)S(1)}, f32[72,512]{1,0:T(8,128)S(1)}, u32[]{:S(2)}, u32[]{:S(2)}) collective-permute-start(f32[72,512]{1,0:T(8,128)S(1)} %get-tuple-element.19.off_ref.own_ref), channel_id=1, source_target_pairs={{1,2},{2,1},{3,4},{4,3},{5,6},{6,5},{7,8},{8,7},{9,10},{10,9},{11,... | collective-permute-start | bytes 442376 | tf_op jit(solution)/shard_map/ppermute | solution.py:584
  48.1 22.1 %all-to-all-start.2 = ((f32[16,8,128]{2,1,0:T(8,128)}), f32[16,8,128]{2,1,0:T(8,128)S(1)}, u32[]{:S(2)}, u32[]{:S(2)}) async-start(f32[16,8,128]{2,1,0:T(8,128)} %bitcast.4), calls=%async_computation.2 | async-start | bytes 131072 | tf_op jit(solution)/shard_map/all_to_all | solution.py:600

commit v10 on v9

--- a/solution.py
+++ b/solution.py
@@ -212,10 +212,7 @@
     ]
     for move in moves:
         move.start()
-    moves[4].wait()
-    moves[5].wait()
-    box_tables((1.5, 0.5, -0.5, -1.5), (0.5, -0.5), (0.5, -0.5), 6.0, 0.9, col_ref, row_ref, tab_ref)
-    for move in moves[:4]:
+    for move in moves[:-1]:
         move.wait()
     lane = lax.broadcasted_iota(jnp.int32, (8, POINTS), 1)
     limit = jnp.zeros((8, POINTS), jnp.int32)
@@ -234,6 +231,7 @@
     e_move = pltpu.make_async_copy(e_ref, e_hbm, sems.at[7])
     e_move.start()
     acc = jnp.zeros((RHS, LANE), F32)
+    box_tables((1.5, 0.5, -0.5, -1.5), (0.5, -0.5), (0.5, -0.5), 6.0, 0.9, col_ref, row_ref, tab_ref)
     for (x, y, z), kern in box_pairs(4, 2, 2, tab_ref):
         start = ((x >> 1) * 8 + (x & 1) + 2 * y + 4 * z) * 2 * RHS
         high, low = split(kern)
@@ -435,22 +433,36 @@
     out_ref[...] = flipped[:RHS] + flipped[RHS:]
 
 
+def sides(swap_ref, cross_ref, left_ref, right_ref):
+    odd = lax.rem(lax.axis_index("inner"), 2) == 1
+    left_ref[...] = jnp.where(odd, swap_ref[...], cross_ref[...])
+    right_ref[...] = jnp.where(odd, cross_ref[...], swap_ref[...])
+
+
+def near_kernel(
+    near_ref, own_ref, swap_ref, cross_ref, out_hbm, out_ref, left_ref, right_ref, mask_ref, high_ref, low_ref, sem
+):
+    sides(swap_ref, cross_ref, left_ref, right_ref)
+    near_field(near_ref, left_ref, own_ref, right_ref, out_ref, mask_ref, high_ref, low_ref)
+    move = pltpu.make_async_copy(out_ref, out_hbm, sem)
+    move.start()
+    move.wait()
+
+
 def field_kernel(
-    far_ref, near_ref, own_ref, swap_ref, cross_ref, up_ref, col_ref, row_ref, w_hbm, m_hbm, e_hbm, out_ref, m_ref,
-    pad_ref, e_ref, dl_ref, xtab_ref, tab_ref, w_ref, left_ref, right_ref, mask_ref, high_ref, low_ref, sems,
+    far_ref, swap_ref, cross_ref, up_ref, col_ref, row_ref, w_hbm, m_hbm, e_hbm, near_hbm, out_ref, m_ref,
+    pad_ref, e_ref, dl_ref, xtab_ref, tab_ref, w_ref, left_ref, right_ref, sems,
 ):
     middle = LEAVES * 2 * RHS
     moves = [
         pltpu.make_async_copy(e_hbm, e_ref.at[middle : 2 * middle], sems.at[0]),
         pltpu.make_async_copy(w_hbm, w_ref, sems.at[1]),
         pltpu.make_async_copy(m_hbm, m_ref, sems.at[2]),
+        pltpu.make_async_copy(near_hbm, out_ref, sems.at[3]),
     ]
     for move in moves:
         move.start()
-    odd = lax.rem(lax.axis_index("inner"), 2) == 1
-    left_ref[...] = jnp.where(odd, swap_ref[...], cross_ref[...])
-    right_ref[...] = jnp.where(odd, cross_ref[...], swap_ref[...])
-    near_field(near_ref, left_ref, own_ref, right_ref, out_ref, mask_ref, high_ref, low_ref)
+    sides(swap_ref, cross_ref, left_ref, right_ref)
     inner = lax.axis_index("inner")
     device = lax.axis_index("outer") * INNER + inner
     up = padded(up_ref, pad_ref, 18.0 / TERMS)
@@ -592,7 +604,14 @@
         peers_kernel, "device_to_device", sds((RHS, LANE), F32), [VM, VM, VM],
         [tables(12), pltpu.VMEM((4, 2, 3 * RHS, LANE), BF)], 10, peers_equiv, col, row,
     )
-    groups = tie(groups, peers_part)
+    points = pltpu.VMEM((ROWS, POINTS), F32)
+    spread = pltpu.VMEM((POINTS, 3 * POINTS), BF)
+    near_part = call(
+        near_kernel, "near_field", pltpu.HBM((RHS, POINTS), F32), [VM, VM, VM, VM],
+        [pltpu.VMEM((RHS, POINTS), F32), points, points, pltpu.VMEM((LEAVES, 3 * POINTS), F32), spread, spread, pltpu.SemaphoreType.DMA],
+        14, near, own, swap, cross, out_specs=HB,
+    )
+    groups = tie(groups, peers_part, near_part)
     local = call(
         local_kernel, "group_and_device_local", flow, [VM, VM, VM, VM, VM], [pad, tables(14)], 8,
         groups, peers_part, downward, col, row,
@@ -600,7 +619,7 @@
     dev_local = lax.all_to_all(local, "inner", 0, 0, tiled=True)
     base, evaluate = call(
         field_kernel, "near_and_far_field", (sds((RHS, POINTS), F32), sds((2, SUB, POINTS), BF)),
-        [SM, VM, VM, VM, VM, VM, VM, VM, HB, HB, HB],
+        [SM, VM, VM, VM, VM, VM, HB, HB, HB, HB],
         [
             pad,
             pltpu.VMEM((3 * LEAVES * 2 * RHS, LANE), BF),
@@ -608,14 +627,11 @@
             tables(21),
             tables(30),
             pltpu.VMEM((2, SUB, POINTS), BF),
-            pltpu.VMEM((ROWS, POINTS), F32),
-            pltpu.VMEM((ROWS, POINTS), F32),
-            pltpu.VMEM((LEAVES, 3 * POINTS), F32),
-            pltpu.VMEM((POINTS, 3 * POINTS), BF),
-            pltpu.VMEM((POINTS, 3 * POINTS), BF),
-            pltpu.SemaphoreType.DMA((3,)),
+            points,
+            points,
+            pltpu.SemaphoreType.DMA((4,)),
         ],
-        32, far, near, own, swap, cross, upward, col, row, in_hbm(weights), in_hbm(evaluate), in_hbm(equiv),
+        26, far, swap, cross, upward, col, row, *map(in_hbm, (weights, evaluate, equiv, near_part)),
     )
     return call(tail_kernel, "potential", sds((RHS, POINTS), F32), [VM, VM, VM], [], 4, dev_local, base, evaluate)
 

time: 71.5 us -> 71.6 us (level)
  Pallas kernels: 34.5 us -> 35.7 us
  starting transfers between devices: 31.6 us -> 30.6 us
    all_to_all x1, waiting for transfers between devices: 1.42 us -> 0.01 us  [shards(): groups = lax.all_to_all(group_equiv, 'outer', 0, 0, tiled=True)]
    ppermute x1, waiting for transfers between devices: 0.01 us -> 1.19 us  [shards(): lax.ppermute(own, 'inner', [(i, (i + 1 ^ 1) - 1) for i in range(1, INNER...]
    pallas_call x7 -> x8, Pallas kernels: 34.5 us -> 35.7 us  [call(): pl.pallas_call(kernel, name=name, out_shape=outs, in_specs=specs, out_spe...]
    all_to_all x1, starting transfers between devices: 5.57 us -> 4.47 us  [shards(): dev_local = lax.all_to_all(local, 'inner', 0, 0, tiled=True)]
  transfers between devices with their start and end apart: 5 -> 5, of which waited for: 2 -> 2; matrix products, arithmetic and copies ran while one was open for 0% -> 0% of each run, Pallas kernels for 39% -> 36%
where the time goes in v10:
time: 71.6 us; the launch traced here: 71.1 us
  Pallas kernels  35.7 us (50%)
  starting transfers between devices  30.6 us (43%)
  waiting for transfers between devices  4.74 us (7%)
    pallas_call x8, Pallas kernels, call(): pl.pallas_call(kernel, name=name, out_shape=outs, in_specs=specs, out_spe...  35.7 us
    all_to_all x1, starting transfers between devices, shards(): peers_equiv = lax.all_to_all(dev_equiv, 'inner', 0, 0, tiled=True)  11.8 us
    all_to_all x1, starting transfers between devices, shards(): groups = lax.all_to_all(group_equiv, 'outer', 0, 0, tiled=True)  9.68 us
    all_to_all x1, starting transfers between devices, shards(): dev_local = lax.all_to_all(local, 'inner', 0, 0, tiled=True)  4.47 us
    all_to_all x1, waiting for transfers between devices, shards(): peers_equiv = lax.all_to_all(dev_equiv, 'inner', 0, 0, tiled=True)  3.54 us
    ppermute x1, starting transfers between devices, shards(): swap = lax.ppermute(own, 'inner', [(i, i ^ 1) for i in range(INNER)])  2.35 us
    ppermute x1, starting transfers between devices, shards(): lax.ppermute(own, 'inner', [(i, (i + 1 ^ 1) - 1) for i in range(1, INNER...  2.29 us
  transfers between devices with their start and end apart: 5, of which 2 were waited for; matrix products, arithmetic and copies ran while one was open for 0% of the time, Pallas kernels for 36%

profile of v10, /device:TPU:1, one launch (start us, length us, event | category | flops | bytes accessed | tf_op | source)
XLA Modules:
  0.0 71.1 jit_solution(6475459817904211150)
XLA Ops:
  0.0 0.0 copy-start
  0.0 4.4 %leaf_and_device_equiv.1 = (f32[128,128]{1,0:T(8,128)}, f32[72,512]{1,0:T(8,128)S(1)}, f32[165,165]{1,0:T(8,128)S(1)}, f32[165,165]{1,0:T(8,128)S(1)}, f32[176,1...) custom-call(f32[3,512]{1,0:T(4,128)} %off_hbm.1, f32[64,512]{1,0:T(8,128)} %q_hbm.1, s32[16]{0:T(128)} %counts_hbm.1, ...), custom_call_target="tpu_custom_call" | custom-call | flops 1000 | bytes 1000 | tf_op jit(solution)/shard_map/leaf_and_device_equiv/pallas_call | solution.py:540
  4.4 0.0 copy-start.1
  4.4 11.8 %all-to-all-start = ((f32[16,8,128]{2,1,0:T(8,128)}), f32[16,8,128]{2,1,0:T(8,128)S(1)}, u32[]{:S(2)}, u32[]{:S(2)}) async-start(f32[16,8,128]{2,1,0:T(8,128)} %bitcast), calls=%async_computation | async-start | bytes 131072 | tf_op jit(solution)/shard_map/all_to_all | solution.py:587
  16.2 4.3 %evaluation_and_group_maps.1 = (bf16[16,2,176,256]{3,2,1,0:T(8,128)(2,1)S(1)}, bf16[2,176,512]{2,1,0:T(8,128)(2,1)}, bf16[2,176,512]{2,1,0:T(8,128)(2,1)}) custom-call(f32[128,128]{1,0:T(8,128)} %get-tuple-element.18.flow_ref, f32[72,512]{1,0:T(8,128)S(1)} %get-tuple-element.19.off_ref.own_ref, f32[165,165]{1,0:T(8,128)S(1)} %get-tuple-element.20.down_ref, ...), custom_call_target="tpu_custom_call" | custom-call | flops 1000 | bytes 1000 | tf_op jit(solution)/shard_map/evaluation_and_group_maps/pallas_call | solution.py:540
  20.5 3.5 %all-to-all-done = f32[16,8,128]{2,1,0:T(8,128)S(1)} async-done(((f32[16,8,128]{2,1,0:T(8,128)}), f32[16,8,128]{2,1,0:T(8,128)S(1)}, u32[]{:S(2)}, u32[]{:S(2)}) %all-to-all-start) | async-done | bytes 65568 | tf_op jit(solution)/shard_map/all_to_all | solution.py:587
  24.0 1.4 %group_equiv.1 = f32[256,128]{1,0:T(8,128)} custom-call(f32[128,128]{1,0:T(8,128)S(1)} %bitcast.6, bf16[16,2,176,256]{3,2,1,0:T(8,128)(2,1)S(1)} %get-tuple-element.23.maps_ref, f32[165,165]{1,0:T(8,128)S(1)} %get-tuple-element.24.up_ref), custom_call_target="tpu_custom_call" | custom-call | flops 1000 | bytes 1000 | tf_op jit(solution)/shard_map/group_equiv/pallas_call | solution.py:540
  25.4 9.7 %all-to-all-start.1 = ((f32[32,8,128]{2,1,0:T(8,128)}), f32[32,8,128]{2,1,0:T(8,128)S(1)}, u32[]{:S(2)}, u32[]{:S(2)}) async-start(f32[32,8,128]{2,1,0:T(8,128)} %bitcast.10), calls=%async_computation.1 | async-start | bytes 262144 | tf_op jit(solution)/shard_map/all_to_all | solution.py:602
  35.1 2.4 %collective-permute-start = (f32[72,512]{1,0:T(8,128)S(1)}, f32[72,512]{1,0:T(8,128)S(1)}, u32[]{:S(2)}, u32[]{:S(2)}) collective-permute-start(f32[72,512]{1,0:T(8,128)S(1)} %get-tuple-element.19.off_ref.own_ref), channel_id=1, source_target_pairs={{0,1},{1,0},{2,3},{3,2},{4,5},{5,4},{6,7},{7,6},{8,9},{9,8},{10,11... | collective-permute-start | bytes 442376 | tf_op jit(solution)/shard_map/ppermute | solution.py:595
  37.5 2.3 %collective-permute-start.1 = (f32[72,512]{1,0:T(8,128)S(1)}, f32[72,512]{1,0:T(8,128)S(1)}, u32[]{:S(2)}, u32[]{:S(2)}) collective-permute-start(f32[72,512]{1,0:T(8,128)S(1)} %get-tuple-element.19.off_ref.own_ref), channel_id=1, source_target_pairs={{1,2},{2,1},{3,4},{4,3},{5,6},{6,5},{7,8},{8,7},{9,10},{10,9},{11,... | collective-permute-start | bytes 442376 | tf_op jit(solution)/shard_map/ppermute | solution.py:596
  39.8 3.3 %device_to_device.1.peers_ref = f32[64,256]{1,0:T(8,128)S(1)} custom-call(f32[128,128]{1,0:T(8,128)S(1)} %bitcast.7, f32[176,128]{1,0:T(8,128)S(1)} %get-tuple-element.21.col_ref, f32[8,256]{1,0:T(8,128)S(1)} %get-tuple-element.22.row_ref), custom_call_target="tpu_custom_call" | custom-call | flops 1000 | bytes 1000 | tf_op jit(solution)/shard_map/device_to_device/pallas_call | solution.py:540
  43.0 0.0 collective-permute-done.swap_ref
  43.0 1.2 %collective-permute-done.1.cross_ref = f32[72,512]{1,0:T(8,128)S(1)} collective-permute-done((f32[72,512]{1,0:T(8,128)S(1)}, f32[72,512]{1,0:T(8,128)S(1)}, u32[]{:S(2)}, u32[]{:S(2)}) %collective-permute-start.1) | collective-permute-done | bytes 147488 | tf_op jit(solution)/shard_map/ppermute | solution.py:596
  44.2 0.0 copy-done
  44.2 2.7 %near_field.1.near_hbm = f32[64,512]{1,0:T(8,128)} custom-call(s32[16,12]{1,0:T(8,128)S(1)} %copy-done, f32[72,512]{1,0:T(8,128)S(1)} %get-tuple-element.19.off_ref.own_ref, f32[72,512]{1,0:T(8,128)S(1)} %collective-permute-done.swap_ref, f32[72,512]{1,0:T(8,128)S(1)} %collective-permute-done.1.cross_ref), custom_call_target="tpu_custom_call" | custom-call | flops 1000 | bytes 1000 | tf_op jit(solution)/shard_map/near_field/pallas_call | solution.py:540
  47.0 0.0 all-to-all-done.1
  47.0 3.7 %group_and_device_local.1 = f32[128,128]{1,0:T(8,128)} custom-call(f32[256,128]{1,0:T(8,128)S(1)} %bitcast.8, f32[64,256]{1,0:T(8,128)S(1)} %device_to_device.1.peers_ref, f32[165,165]{1,0:T(8,128)S(1)} %get-tuple-element.20.down_ref, f32[176,128]{1,0:T(8,128)S(1)} %get-tuple-element.21.col_ref, f32[8,256]{1,0:T(8,128)S(1)} %get-tuple-element.22.row_ref), custom_call_target="tpu_custom_call" | custom-call | flops 1000 | bytes 1000 | tf_op jit(solution)/shard_map/group_and_device_local/pallas_call | solution.py:540
  50.6 4.5 %all-to-all-start.2 = ((f32[16,8,128]{2,1,0:T(8,128)}), f32[16,8,128]{2,1,0:T(8,128)S(1)}, u32[]{:S(2)}, u32[]{:S(2)}) async-start(f32[16,8,128]{2,1,0:T(8,128)} %bitcast.4), calls=%async_computation.2 | async-start | bytes 131072 | tf_op jit(solution)/shard_map/all_to_all | solution.py:619
  55.1 0.0 copy-done.1
  55.1 15.1 %near_and_far_field.1 = (f32[64,512]{1,0:T(8,128)S(1)}, bf16[2,176,512]{2,1,0:T(8,128)(2,1)S(1)}) custom-call(s32[16,12]{1,0:T(8,128)S(1)} %copy-done.1, f32[72,512]{1,0:T(8,128)S(1)} %collective-permute-done.swap_ref, f32[72,512]{1,0:T(8,128)S(1)} %collective-permute-done.1.cross_ref, f32[165,165]{1,0:T(8,128)S(1)} %get-tuple-element.24.up_ref, ...), custom_call_target="tpu_custom_call" | custom-call | flops 1000 | bytes 1000 | tf_op jit(solution)/shard_map/near_and_far_field/pallas_call | solution.py:540
  70.3 0.0 all-to-all-done.2
  70.3 0.9 %potential.1 = f32[64,512]{1,0:T(8,128)} custom-call(f32[128,128]{1,0:T(8,128)S(1)} %bitcast.9, f32[64,512]{1,0:T(8,128)S(1)} %get-tuple-element.29.base_ref, bf16[2,176,512]{2,1,0:T(8,128)(2,1)S(1)} %get-tuple-element.30.m_ref), custom_call_target="tpu_custom_call" | custom-call | flops 1000 | bytes 1000 | tf_op jit(solution)/shard_map/potential/pallas_call | solution.py:540
Async XLA Ops:
  0.0 44.2 %copy-start = (s32[16,12]{1,0:T(8,128)S(1)}, s32[16,12]{1,0:T(8,128)}, u32[]{:S(2)}) copy-start(s32[16,12]{1,0:T(8,128)} %near_ref.1) | copy-start | bytes 2308
  4.4 50.7 %copy-start.1 = (s32[16,12]{1,0:T(8,128)S(1)}, s32[16,12]{1,0:T(8,128)}, u32[]{:S(2)}) copy-start(s32[16,12]{1,0:T(8,128)} %far_ref.1) | copy-start | bytes 2308
  4.4 19.7 %all-to-all-start = ((f32[16,8,128]{2,1,0:T(8,128)}), f32[16,8,128]{2,1,0:T(8,128)S(1)}, u32[]{:S(2)}, u32[]{:S(2)}) async-start(f32[16,8,128]{2,1,0:T(8,128)} %bitcast), calls=%async_computation | async-start | bytes 131072 | tf_op jit(solution)/shard_map/all_to_all | solution.py:587
  25.4 21.5 %all-to-all-start.1 = ((f32[32,8,128]{2,1,0:T(8,128)}), f32[32,8,128]{2,1,0:T(8,128)S(1)}, u32[]{:S(2)}, u32[]{:S(2)}) async-start(f32[32,8,128]{2,1,0:T(8,128)} %bitcast.10), calls=%async_computation.1 | async-start | bytes 262144 | tf_op jit(solution)/shard_map/all_to_all | solution.py:602
  35.1 7.9 %collective-permute-start = (f32[72,512]{1,0:T(8,128)S(1)}, f32[72,512]{1,0:T(8,128)S(1)}, u32[]{:S(2)}, u32[]{:S(2)}) collective-permute-start(f32[72,512]{1,0:T(8,128)S(1)} %get-tuple-element.19.off_ref.own_ref), channel_id=1, source_target_pairs={{0,1},{1,0},{2,3},{3,2},{4,5},{5,4},{6,7},{7,6},{8,9},{9,8},{10,11... | collective-permute-start | bytes 442376 | tf_op jit(solution)/shard_map/ppermute | solution.py:595
  37.5 6.8 %collective-permute-start.1 = (f32[72,512]{1,0:T(8,128)S(1)}, f32[72,512]{1,0:T(8,128)S(1)}, u32[]{:S(2)}, u32[]{:S(2)}) collective-permute-start(f32[72,512]{1,0:T(8,128)S(1)} %get-tuple-element.19.off_ref.own_ref), channel_id=1, source_target_pairs={{1,2},{2,1},{3,4},{4,3},{5,6},{6,5},{7,8},{8,7},{9,10},{10,9},{11,... | collective-permute-start | bytes 442376 | tf_op jit(solution)/shard_map/ppermute | solution.py:596
  50.6 19.6 %all-to-all-start.2 = ((f32[16,8,128]{2,1,0:T(8,128)}), f32[16,8,128]{2,1,0:T(8,128)S(1)}, u32[]{:S(2)}, u32[]{:S(2)}) async-start(f32[16,8,128]{2,1,0:T(8,128)} %bitcast.4), calls=%async_computation.2 | async-start | bytes 131072 | tf_op jit(solution)/shard_map/all_to_all | solution.py:619
